TPU v7x, 128 devices: a whole 4x4x4 slice. The times are simulated.
128 devices in a mesh: gx: 8 (over y, core), gy: 16 (over x, z).
Axes of the slice: x: 4, y: 4, z: 4, core: 2. Of those that a mesh axis runs over, the one named last changes fastest.
Arguments:
- tensor: float32 [4, 672, 128, 512], P(None, 'gx', 'gy'), may hold values from -8 to 8, as said below
- start_basis: float32 [672, 96], replicated, may hold values from -6 to 6
Outputs:
- factor: float32 [672, 96], replicated
- core_tensor: float32 [4, 96, 128, 512], P(None, None, 'gy', 'gx')
Inputs may be any that keep to these rules, and one draw needn't show every extreme that they name: `tensor`: row scales and species scales vary; values stay within the bounds.
All inputs are finite; a program needn't handle non-finite values.
Results may differ from a plain program's by a relative error of at most 0.0003.
Values sent between devices are 32-bit elements; how exact they have to be, the bound alone decides.
No kernel may reach another device: no remote copies, remote signals or barrier semaphores. Data moves between devices by JAX's collectives and lax.ppermute only.
A program may use at most 128 MiB of HBM per device.

v0:
```python
import jax
import jax.numpy as jnp
from jax import lax
from jax.sharding import PartitionSpec as P

POWER = 2


def species_grams(pieces):
    flattened = pieces.reshape(pieces.shape[0], pieces.shape[1], -1)
    gram_blocks = jnp.einsum(
        "sxk,syk->sxy",
        flattened,
        flattened,
        precision=lax.Precision.HIGHEST,
        preferred_element_type=jnp.float32,
    )
    return (gram_blocks, pieces)


def orthonormal(mapped):
    inner_gram = jnp.dot(mapped.T, mapped, precision=lax.Precision.HIGHEST)
    lower_factor = jnp.linalg.cholesky(inner_gram)
    return jax.scipy.linalg.solve_triangular(lower_factor, mapped.T, lower=True).T


def per_device(tensor, start_basis):
    gram_blocks, fibers = species_grams(
        lax.all_to_all(tensor, "gx", split_axis=3, concat_axis=1, tiled=True)
    )
    local_gram = jnp.sum(gram_blocks, 0)
    factor = start_basis
    gram_total = lax.psum(local_gram, ("gx", "gy"))
    upper_factor = jnp.linalg.cholesky(gram_total).T
    for iteration in range(POWER):
        inside = jnp.dot(upper_factor, factor, precision=lax.Precision.HIGHEST)
        mapped = jnp.dot(upper_factor.T, inside, precision=lax.Precision.HIGHEST)
        factor = orthonormal(mapped)
    species_total, order_rows, y_cells, z_cells = fibers.shape
    flattened = fibers.reshape(species_total, order_rows, y_cells * z_cells)
    projected = jnp.einsum(
        "xr,sxk->srk",
        factor,
        flattened,
        precision=lax.Precision.HIGHEST,
        preferred_element_type=jnp.float32,
    )
    core_tensor = projected.reshape(species_total, factor.shape[1], y_cells, z_cells)
    return (factor, core_tensor)


def solution(mesh):
    return jax.shard_map(
        per_device,
        mesh=mesh,
        in_specs=(P(None, "gx", "gy", None), P()),
        out_specs=(P(), P(None, None, "gy", "gx")),
        check_vma=False,
    )
```

profile of v0, /device:TPU:1, one launch (start us, length us, event | category | flops | bytes accessed | tf_op | source)
XLA Modules:
  0.0 498.5 jit_solution(14944964828819254309)
XLA Ops:
  7.2 9.3 %copy.20 = f32[4,84,8,512]{1,2,0,3:T(8,128)} copy(f32[4,84,8,512]{3,2,1,0:T(8,128)} %param.5) | data formatting | bytes 11010048 | tf_op args[0]
  16.6 100.9 %all_to_all.15 = f32[4,84,8,512]{1,2,0,3:T(8,128)S(1)} all-to-all(f32[4,84,8,512]{1,2,0,3:T(8,128)} %copy.20), channel_id=1, replica_groups=mesh['gx'=8,'gy'=16] {'gx'}, dimensions={3} | all-to-all | bytes 11010048 | tf_op jit(solution)/shard_map/all_to_all | solution.py:29
  117.4 8.1 %copy.22 = f32[4,8,84,8,64]{2,1,4,3,0:T(8,128)} copy(f32[4,8,84,8,64]{2,3,0,4,1:T(8,128)S(1)} %bitcast.83) | data formatting | bytes 11010048 | tf_op jit(solution)/shard_map/all_to_all | solution.py:29
  125.5 9.5 %reshape.59 = f32[4,672,512]{1,2,0:T(8,128)} reshape(f32[4,8,84,8,64]{2,1,4,3,0:T(8,128)} %copy.22) | data formatting | bytes 11010048 | tf_op jit(solution)/shard_map/reshape | solution.py:10
  135.0 18.5 %convolution_bitcast_fusion = f32[672,672]{0,1:T(8,128)} fusion(f32[4,672,512]{1,2,0:T(8,128)} %reshape.59), kind=kOutput, calls=%fused_computation.4 | convolution fusion | flops 11098128384 | bytes 7311360 | tf_op jit(solution)/shard_map/sxk,syk->sxy/dot_general | solution.py:11
  153.6 151.3 %all-reduce.3.cloned.1.call-done = f32[672,672]{0,1:T(8,128)} async-done(((f32[672,672]{0,1:T(8,128)}), f32[672,672]{0,1:T(8,128)}) %all-reduce.3.cloned.1.call-update) | async-done | bytes 1806352 | tf_op jit(solution)/shard_map/psum | solution.py:33
  304.9 3.5 copy.26
  308.4 1.8 fusion
  310.3 1.3 copy-done.2
  311.6 11.7 %cholesky.180 = f32[128,128]{1,0:T(8,128)S(1)} custom-call(f32[128,128]{1,0:T(8,128)S(1)} %cholesky.494), custom_call_target="Cholesky" | custom-call | tf_op jit(solution)/shard_map/jit(cholesky)/cholesky | solution.py:34
  323.3 9.8 %custom-call.48 = f32[1,128,128]{1,2,0:T(8,128)S(1)} custom-call(f32[1,128,128]{2,1,0:T(8,128)S(1)} %get-tuple-element.19), custom_call_target="InvertDiagBlocksLowerTriangular" | custom-call | tf_op jit(solution)/shard_map/jit(cholesky)/cholesky | solution.py:34
  333.3 1.3 constant_dynamic-update-slice_fusion.4
  334.7 1.3 convolution_subtract_fusion
  336.0 11.7 %cholesky.203 = f32[128,128]{1,0:T(8,128)S(1)} custom-call(f32[128,128]{1,0:T(8,128)S(1)} %cholesky.498), custom_call_target="Cholesky" | custom-call | tf_op jit(solution)/shard_map/jit(cholesky)/cholesky | solution.py:34
  347.8 9.9 %custom-call.49 = f32[1,128,128]{1,2,0:T(8,128)S(1)} custom-call(f32[1,128,128]{2,1,0:T(8,128)S(1)} %get-tuple-element.16), custom_call_target="InvertDiagBlocksLowerTriangular" | custom-call | tf_op jit(solution)/shard_map/jit(cholesky)/cholesky | solution.py:34
  358.1 1.4 convolution_subtract_fusion.1
  359.5 11.7 %cholesky.383 = f32[128,128]{1,0:T(8,128)S(1)} custom-call(f32[128,128]{1,0:T(8,128)S(1)} %cholesky.503), custom_call_target="Cholesky" | custom-call | tf_op jit(solution)/shard_map/jit(cholesky)/cholesky | solution.py:34
  372.0 9.8 %custom-call.50 = f32[1,128,128]{1,2,0:T(8,128)S(1)} custom-call(f32[1,128,128]{2,1,0:T(8,128)S(1)} %get-tuple-element.13), custom_call_target="InvertDiagBlocksLowerTriangular" | custom-call | tf_op jit(solution)/shard_map/jit(cholesky)/cholesky | solution.py:34
  382.1 1.4 convolution_subtract_fusion.2
  383.5 11.9 %cholesky.402 = f32[128,128]{1,0:T(8,128)S(1)} custom-call(f32[128,128]{1,0:T(8,128)S(1)} %cholesky.508), custom_call_target="Cholesky" | custom-call | tf_op jit(solution)/shard_map/jit(cholesky)/cholesky | solution.py:34
  396.1 9.8 %custom-call.51 = f32[1,128,128]{1,2,0:T(8,128)S(1)} custom-call(f32[1,128,128]{2,1,0:T(8,128)S(1)} %get-tuple-element.10), custom_call_target="InvertDiagBlocksLowerTriangular" | custom-call | tf_op jit(solution)/shard_map/jit(cholesky)/cholesky | solution.py:34
  406.1 1.3 convolution_subtract_fusion.3
  407.5 11.7 %cholesky.421 = f32[128,128]{1,0:T(8,128)S(1)} custom-call(f32[128,128]{1,0:T(8,128)S(1)} %cholesky.513), custom_call_target="Cholesky" | custom-call | tf_op jit(solution)/shard_map/jit(cholesky)/cholesky | solution.py:34
  419.9 9.8 %custom-call.52 = f32[1,128,128]{1,2,0:T(8,128)S(1)} custom-call(f32[1,128,128]{2,1,0:T(8,128)S(1)} %get-tuple-element.7), custom_call_target="InvertDiagBlocksLowerTriangular" | custom-call | tf_op jit(solution)/shard_map/jit(cholesky)/cholesky | solution.py:34
  430.8 2.9 cholesky.442
  440.1 2.0 fusion.3
  442.6 8.8 %cholesky.474 = f32[96,96]{1,0:T(8,128)S(1)} custom-call(f32[96,96]{1,0:T(8,128)S(1)} %fusion.33), custom_call_target="Cholesky" | custom-call | tf_op jit(solution)/shard_map/jit(cholesky)/cholesky | solution.py:23
  452.7 7.4 %custom-call.54 = f32[1,96,96]{1,2,0:T(8,128)S(1)} custom-call(f32[1,96,96]{2,1,0:T(8,128)S(1)} %fusion.28), custom_call_target="InvertDiagBlocksLowerTriangular" | custom-call | tf_op jit(solution)/shard_map/jit(_solve_triangular)/triangular_solve | solution.py:24
  461.6 1.6 fusion.1
  463.7 8.8 %cholesky.485 = f32[96,96]{1,0:T(8,128)S(1)} custom-call(f32[96,96]{1,0:T(8,128)S(1)} %fusion.31), custom_call_target="Cholesky" | custom-call | tf_op jit(solution)/shard_map/jit(cholesky)/cholesky | solution.py:23
  473.8 7.4 %custom-call.55 = f32[1,96,96]{1,2,0:T(8,128)S(1)} custom-call(f32[1,96,96]{2,1,0:T(8,128)S(1)} %fusion.29), custom_call_target="InvertDiagBlocksLowerTriangular" | custom-call | tf_op jit(solution)/shard_map/jit(_solve_triangular)/triangular_solve | solution.py:24
  481.7 8.5 %convolution_bitcast_fusion.1 = f32[4,96,512]{2,1,0:T(8,128)S(1)} fusion(f32[4,672,512]{1,2,0:T(8,128)} %reshape.59, f32[96,672]{1,0:T(8,128)S(1)} %fusion.9), kind=kOutput, calls=%fused_computation.5 | convolution fusion | flops 1585446912 | bytes 6549504 | tf_op jit(solution)/shard_map/xr,sxk->srk/dot_general | solution.py:41
  (48 shorter events, 13.7 us)
Async XLA Ops:
  7.2 431.8 %copy-start = (f32[672,96]{0,1:T(8,128)S(1)}, f32[672,96]{0,1:T(8,128)}, u32[]{:S(2)}) copy-start(f32[672,96]{0,1:T(8,128)} %param.6) | copy-start | bytes 774148
  7.2 297.7 %all-reduce.3.cloned.1.call-start = ((), (), s32[]{:S(2)}) async-start(), calls=%async_computation.1 | async-start | bytes 4128768 | tf_op jit(solution)/shard_map/psum | solution.py:33
  304.9 3.6 copy-start.1
  310.3 1.3 copy-start.2
  481.6 8.5 %copy-start.3 = (f32[96,672]{1,0:T(8,128)}, f32[96,672]{1,0:T(8,128)S(1)}, u32[]{:S(2)}) copy-start(f32[96,672]{1,0:T(8,128)S(1)} %fusion.9) | copy-start | bytes 774148
Sparse Core Ops, SparseCore 0:
  153.7 151.1 all-reduce.2
where the time goes:
time: 504 us; the launch traced here: 498 us
  waiting for transfers between devices  151 us (30%)
  other arithmetic  151 us (30%)
  blocking collectives  101 us (20%)
  matrix products  43.3 us (9%)
  local copies, waits for them, and re-layouts  33.4 us (7%)
  between operations  18.4 us (4%)
    psum x1, waiting for transfers between devices, per_device(): gram_total = lax.psum(local_gram, ('gx', 'gy'))  151 us
    another operation x22, other arithmetic, per_device(): upper_factor = jnp.linalg.cholesky(gram_total).T  114 us
    all_to_all x1, blocking collectives, per_device(): lax.all_to_all(tensor, 'gx', split_axis=3, concat_axis=1, tiled=True)  101 us
    another operation x6, other arithmetic, orthonormal(): lower_factor = jnp.linalg.cholesky(inner_gram)  18.9 us
    dot_general x1, matrix products, species_grams(): jnp.einsum('sxk,syk->sxy', flattened, flattened, precision=lax.Precision....  18.5 us
    another operation x4, other arithmetic, orthonormal(): jax.scipy.linalg.solve_triangular(lower_factor, mapped.T, lower=True)  16 us
    unnamed x9, local copies, waits for them, and re-layouts  10.7 us
  transfers between devices with their start and end apart: 1, of which 1 were waited for; matrix products, arithmetic and copies ran while one was open for 0% of the time, Pallas kernels for 0%

commit v1 on v0

v1 whole, which is shorter than its diff:
```python
import jax
import jax.numpy as jnp
from jax import lax
from jax.experimental import pallas as pl
from jax.experimental.pallas import tpu as pltpu
from jax.sharding import PartitionSpec as P

X, R = 672, 96
ROWS = 84
TILES = 6
F32, BF16 = jnp.float32, jnp.bfloat16
NN = (((1,), (0,)), ((), ()))
NT = (((1,), (1,)), ((), ()))
VMEM_LIMIT = 56 * 1024 * 1024


def split(a):
    hi = a.astype(BF16)
    return hi, (a - hi.astype(F32)).astype(BF16)


def dot3(a, b, dims):
    d = lambda p, q: lax.dot_general(p, q, dims, preferred_element_type=F32)
    return d(a[0], b[0]) + (d(a[0], b[1]) + d(a[1], b[0]))


def dot_full(a, b, dims):
    return lax.dot_general(a, b, dims, precision=lax.Precision.HIGHEST, preferred_element_type=F32)


def perm_gx(dy, dc):
    return [(2 * y + c, 2 * ((y + dy) % 4) + (c ^ dc)) for y in range(4) for c in range(2)]


def perm_x(d):
    return [(4 * x + z, 4 * ((x + d) % 4) + z) for x in range(4) for z in range(4)]


def perm_z(d):
    return [(4 * x + z, 4 * x + (z + d) % 4) for x in range(4) for z in range(4)]


def exchange(v, axis, perm):
    got = [lax.ppermute(v, axis, perm(d)) for d in (2, 1, 3)]
    return (v + got[0]) + (got[1] + got[2])


def ring_sum(pieces):
    half = pieces[0] + lax.ppermute(pieces[1], "gx", perm_gx(0, 1))
    got = [lax.ppermute(half[d], "gx", perm_gx(d, 0)) for d in (2, 1, 3)]
    mine = (half[0] + got[0]) + (got[1] + got[2])
    mine = exchange(mine, "gy", perm_x)
    mine = exchange(mine, "gy", perm_z)
    got = {d: lax.ppermute(mine, "gx", perm_gx((4 - d) % 4, 0)) for d in (2, 1, 3)}
    full = jnp.stack([mine, got[1], got[2], got[3]])
    return jnp.stack([full, lax.ppermute(full, "gx", perm_gx(0, 1))])


def put_pieces(acc, place, out):
    y, c = place
    rows = jnp.concatenate(
        [acc[:, 128 * j : 128 * j + 128] for j in range(5)]
        + [jnp.concatenate([acc[:, 640:], jnp.zeros((R, 96), F32)], axis=1)],
        axis=0,
    )
    for cc in range(2):
        for yy in range(4):
            start = 288 * cc + 72 * yy
            out[lax.rem(c + cc, 2), lax.rem(yy - y + 4, 4)] = rows[start : start + 72]


def take_pieces(ref, place):
    y, c = place
    rows = jnp.concatenate(
        [ref[lax.rem(c + cc, 2), lax.rem(yy - y + 4, 4)] for cc in range(2) for yy in range(4)], axis=0
    )
    return jnp.concatenate([rows[96 * j : 96 * j + 96] for j in range(5)] + [rows[480:576, :32]], axis=1)


def first_kernel(pos, basis, *refs):
    blocks, (hi_out, lo_out, out), (cells, sems) = refs[:8], refs[8:11], refs[11:]
    for i in range(8):
        pltpu.make_async_copy(blocks[i], cells.at[pl.ds(pos[2 + i] * 672, 672)], sems.at[i]).start()
    f = split(basis[...])
    for i in range(8):
        pltpu.make_async_copy(blocks[i], cells.at[pl.ds(pos[2 + i] * 672, 672)], sems.at[i]).wait()
    acc = jnp.zeros((R, X), F32)
    for p in range(4):
        a = jnp.concatenate([cells[pl.ds(2 * p + q, X, stride=8), :] for q in range(2)], axis=1)
        a = split(a)
        hi_out[:, 256 * p : 256 * p + 256] = a[0]
        lo_out[:, 256 * p : 256 * p + 256] = a[1]
        z = split(dot3(f, a, NN))
        acc = acc + dot3(z, a, NT)
    put_pieces(acc, (pos[0], pos[1]), out)


def first(pos, basis_t, blocks):
    any_spec = pl.BlockSpec(memory_space=pl.ANY)
    vmem = pl.BlockSpec(memory_space=pltpu.VMEM)
    return pl.pallas_call(
        first_kernel,
        out_shape=(
            jax.ShapeDtypeStruct((X, 1024), BF16),
            jax.ShapeDtypeStruct((X, 1024), BF16),
            jax.ShapeDtypeStruct((2, 4, 72, 128), F32),
        ),
        in_specs=[pl.BlockSpec(memory_space=pltpu.SMEM), vmem] + [any_spec] * 8,
        out_specs=(vmem, vmem, vmem),
        scratch_shapes=[pltpu.VMEM((X * 8, 128), F32), pltpu.SemaphoreType.DMA((8,))],
        compiler_params=pltpu.CompilerParams(vmem_limit_bytes=VMEM_LIMIT),
        cost_estimate=pl.CostEstimate(flops=3 * 4 * X * R * 1024, bytes_accessed=6 * 2**20, transcendentals=0),
    )(pos, basis_t, *blocks)


def second_kernel(pos, m_ref, hi0, lo0, hi1, lo1, out, m_out):
    m = take_pieces(m_ref, (pos[0], pos[1]))
    m_out[...] = m
    f = split(m)
    acc = jnp.zeros((R, X), F32)
    for hi, lo in ((hi0, lo0), (hi1, lo1)):
        for p in range(4):
            a = hi[:, 256 * p : 256 * p + 256], lo[:, 256 * p : 256 * p + 256]
            z = split(dot3(f, a, NN))
            acc = acc + dot3(z, a, NT)
    put_pieces(acc, (pos[0], pos[1]), out)


def second(pos, m, fibers):
    vmem = pl.BlockSpec(memory_space=pltpu.VMEM)
    return pl.pallas_call(
        second_kernel,
        out_shape=(jax.ShapeDtypeStruct((2, 4, 72, 128), F32), jax.ShapeDtypeStruct((R, X), F32)),
        in_specs=[pl.BlockSpec(memory_space=pltpu.SMEM)] + [vmem] * 5,
        out_specs=(vmem, vmem),
        compiler_params=pltpu.CompilerParams(vmem_limit_bytes=VMEM_LIMIT),
        cost_estimate=pl.CostEstimate(flops=3 * 4 * X * R * 2048, bytes_accessed=6 * 2**20, transcendentals=0),
    )(pos, m, *fibers)


def gather_kernel(pos, w_ref, linv, out):
    out[...] = dot_full(linv[...], take_pieces(w_ref, (pos[0], pos[1])), NN)


def gathered(pos, w, linv):
    vmem = pl.BlockSpec(memory_space=pltpu.VMEM)
    return pl.pallas_call(
        gather_kernel,
        out_shape=jax.ShapeDtypeStruct((R, X), F32),
        in_specs=[pl.BlockSpec(memory_space=pltpu.SMEM), vmem, vmem],
        out_specs=vmem,
        compiler_params=pltpu.CompilerParams(vmem_limit_bytes=VMEM_LIMIT),
    )(pos, w, linv)


def core_kernel(linv, m_ref, hi0, lo0, hi1, lo1, factor_t, core):
    f = dot_full(linv[...], m_ref[...], NN)
    factor_t[...] = f
    f = split(f)
    for k, (hi, lo) in enumerate(((hi0, lo0), (hi1, lo1))):
        for y in range(8):
            a = hi[:, 128 * y : 128 * y + 128], lo[:, 128 * y : 128 * y + 128]
            core[k, y] = dot3(f, a, NN).T


def core_of(linv, m, fibers):
    vmem = pl.BlockSpec(memory_space=pltpu.VMEM)
    return pl.pallas_call(
        core_kernel,
        out_shape=(jax.ShapeDtypeStruct((R, X), F32), jax.ShapeDtypeStruct((2, 8, 128, R), F32)),
        in_specs=[vmem] * 6,
        out_specs=(vmem, vmem),
        compiler_params=pltpu.CompilerParams(vmem_limit_bytes=VMEM_LIMIT),
        cost_estimate=pl.CostEstimate(flops=3 * 2 * X * R * 2048, bytes_accessed=7 * 2**20, transcendentals=0),
    )(linv, m, *fibers)


def inverse_factor(m_t):
    inner = lax.dot_general(m_t, m_t, NT, precision=lax.Precision.HIGHEST)
    lower = jnp.linalg.cholesky(inner)
    return jax.scipy.linalg.solve_triangular(lower, jnp.eye(R, dtype=F32), lower=True)


def per_device(tensor, start_basis):
    me = lax.axis_index("gx")
    y, c = me // 2, me % 2
    offsets = [(dy, dc) for dy in (2, 1, 3, 0) for dc in (1, 0)]
    sources = [2 * ((y - dy) % 4) + (c ^ dc) for dy, dc in offsets]
    pos = jnp.stack([y, c] + sources).astype(jnp.int32)
    basis_t = start_basis.T

    fibers, total = [], None
    for k in range(2):
        blocks = []
        for dy, dc in offsets:
            block = lax.dynamic_slice(
                tensor, (2 * (c ^ dc) + k, 0, 0, 128 * ((y + dy) % 4)), (1, ROWS, 8, 128)
            ).reshape(ROWS * 8, 128)
            if dy or dc:
                block = lax.ppermute(block, "gx", perm_gx(dy, dc))
            blocks.append(block)
        hi, lo, part = first(pos, basis_t, blocks)
        fibers += [hi, lo]
        total = part if total is None else total + part

    w_part, m1 = second(pos, ring_sum(total), fibers)
    linv1 = inverse_factor(m1)
    m2 = gathered(pos, ring_sum(w_part), linv1)
    factor_t, core = core_of(inverse_factor(m2), m2, fibers)

    halves = core.reshape(2, 8, 2, 64, R)
    mine = lax.dynamic_index_in_dim(halves, c, 2, keepdims=False)
    theirs = lax.ppermute(lax.dynamic_index_in_dim(halves, 1 - c, 2, keepdims=False), "gx", perm_gx(0, 1))
    out = jnp.where(c == 0, jnp.concatenate([mine, theirs]), jnp.concatenate([theirs, mine]))
    return factor_t.T, out.transpose(0, 3, 1, 2)


def solution(mesh):
    return jax.shard_map(
        per_device,
        mesh=mesh,
        in_specs=(P(None, "gx", "gy", None), P()),
        out_specs=(P(), P(None, None, "gy", "gx")),
        check_vma=False,
    )
```

time: 504 us -> 204 us (0.40)
  waiting for transfers between devices: 151 us -> 38.1 us
  other arithmetic: 151 us -> 39.5 us
  blocking collectives: 101 us -> 0 us
  starting transfers between devices: 0.04 us -> 81.8 us
  matrix products: 43.3 us -> 4.68 us
  Pallas kernels: 0 us -> 30.3 us
  local copies, waits for them, and re-layouts: 33.4 us -> 7.7 us
  between operations: 18.4 us -> 1.08 us
    psum x1 -> x0, waiting for transfers between devices: 151 us -> none  [per_device(): gram_total = lax.psum(local_gram, ('gx', 'gy'))]
    another operation x32 -> x14, other arithmetic: 149 us -> 36.4 us  [the longest x6 18.9 us: inverse_factor(): lower = jnp.linalg.cholesky(inner)]
    all_to_all x1 -> x0, blocking collectives: 101 us -> none  [per_device(): lax.all_to_all(tensor, 'gx', split_axis=3, concat_axis=1, tiled=True)]
    ppermute x0 -> x43, starting transfers between devices: none -> 81.8 us  [the longest x14 36.8 us: per_device(): block = lax.ppermute(block, 'gx', perm_gx(dy, dc))]
    ppermute x0 -> x43, waiting for transfers between devices: none -> 38.1 us  [the longest x14 20.5 us: per_device(): block = lax.ppermute(block, 'gx', perm_gx(dy, dc))]
    dot_general x8 -> x2, matrix products: 33.6 us -> 2.92 us  [inverse_factor(): inner = lax.dot_general(m_t, m_t, NT, precision=lax.Precision.HIGHEST)]
    pallas_call x0 -> x5, Pallas kernels: none -> 30.3 us  [the longest x2 13.2 us: first(): pl.pallas_call(first_kernel, out_shape=(jax.ShapeDtypeStruct((X, 1024), B...]
    unnamed x9 -> x20, local copies, waits for them, and re-layouts: 10.7 us -> 0.75 us
  transfers between devices with their start and end apart: 1 -> 43, of which waited for: 1 -> 20; matrix products, arithmetic and copies ran while one was open for 0% -> 10% of each run, Pallas kernels for 0% -> 3%
where the time goes in v1:
time: 204 us; the launch traced here: 203 us
  starting transfers between devices  81.8 us (40%)
  other arithmetic  39.5 us (19%)
  waiting for transfers between devices  38.1 us (19%)
  Pallas kernels  30.3 us (15%)
  local copies, waits for them, and re-layouts  7.7 us (4%)
  matrix products  4.68 us (2%)
    ppermute x14, starting transfers between devices, per_device(): block = lax.ppermute(block, 'gx', perm_gx(dy, dc))  36.8 us
    ppermute x14, waiting for transfers between devices, per_device(): block = lax.ppermute(block, 'gx', perm_gx(dy, dc))  20.5 us
    ppermute x12, starting transfers between devices, exchange(): got = [lax.ppermute(v, axis, perm(d)) for d in (2, 1, 3)]  19.7 us
    another operation x6, other arithmetic, inverse_factor(): lower = jnp.linalg.cholesky(inner)  18.9 us
    another operation x4, other arithmetic, inverse_factor(): jax.scipy.linalg.solve_triangular(lower, jnp.eye(R, dtype=F32), lower=True)  16 us
    pallas_call x2, Pallas kernels, first(): pl.pallas_call(first_kernel, out_shape=(jax.ShapeDtypeStruct((X, 1024), B...  13.2 us
    ppermute x2, starting transfers between devices, ring_sum(): return jnp.stack([full, lax.ppermute(full, 'gx', perm_gx(0, 1))])  10 us
    ppermute x6, starting transfers between devices, ring_sum(): got = [lax.ppermute(half[d], 'gx', perm_gx(d, 0)) for d in (2, 1, 3)]  9.44 us
  transfers between devices with their start and end apart: 43, of which 20 were waited for; matrix products, arithmetic and copies ran while one was open for 10% of the time, Pallas kernels for 3%

profile of v1, /device:TPU:1, one launch (start us, length us, event | category | flops | bytes accessed | tf_op | source)
XLA Modules:
  0.0 203.1 jit_solution(16825173387947794097)
XLA Ops:
  0.8 3.9 %dynamic-slice_bitcast_fusion.2 = (f32[672,128]{1,0:T(8,128)}, f32[672,128]{1,0:T(8,128)S(1)}, f32[672,128]{1,0:T(8,128)S(1)}, f32[672,128]{1,0:T(8,128)S(1)}, f...) fusion(f32[4,84,8,512]{3,2,1,0:T(8,128)} %param.5, ...), kind=kLoop, calls=%fused_computation.4 | loop fusion | bytes 11010080 | tf_op jit(solution)/shard_map/reshape | solution.py:198
  4.7 2.1 %collective-permute-start.10 = (f32[672,128]{1,0:T(8,128)S(1)}, f32[672,128]{1,0:T(8,128)S(1)}, u32[]{:S(2)}, u32[]{:S(2)}) collective-permute-start(f32[672,128]{1,0:T(8,128)S(1)} %get-tuple-element.27), channel_id=1, source_target_pairs={{0,32},{16,48},{32,64},{48,80},{64,96},{80,112},{96,0},{112,16},{1... | collective-permute-start | bytes 1032200 | tf_op jit(solution)/shard_map/ppermute | solution.py:200
  6.8 2.1 %collective-permute-start.11 = (f32[672,128]{1,0:T(8,128)S(1)}, f32[672,128]{1,0:T(8,128)S(1)}, u32[]{:S(2)}, u32[]{:S(2)}) collective-permute-start(f32[672,128]{1,0:T(8,128)S(1)} %get-tuple-element.26), channel_id=1, source_target_pairs={{0,112},{16,96},{32,16},{48,0},{64,48},{80,32},{96,80},{112,64},{1... | collective-permute-start | bytes 1032200 | tf_op jit(solution)/shard_map/ppermute | solution.py:200
  11.3 4.6 %collective-permute-done.10.refs_3_ = f32[672,128]{1,0:T(8,128)S(1)} collective-permute-done((f32[672,128]{1,0:T(8,128)S(1)}, f32[672,128]{1,0:T(8,128)S(1)}, u32[]{:S(2)}, u32[]{:S(2)}) %collective-permute-start.10) | collective-permute-done | bytes 344096 | tf_op jit(solution)/shard_map/ppermute | solution.py:200
  17.8 2.8 %collective-permute-start.9 = (f32[672,128]{1,0:T(8,128)S(1)}, f32[672,128]{1,0:T(8,128)S(1)}, u32[]{:S(2)}, u32[]{:S(2)}) collective-permute-start(f32[672,128]{1,0:T(8,128)S(1)} %get-tuple-element.28), channel_id=1, source_target_pairs={{0,48},{16,32},{32,80},{48,64},{64,112},{80,96},{96,16},{112,0},{1... | collective-permute-start | bytes 1032200 | tf_op jit(solution)/shard_map/ppermute | solution.py:200
  20.6 4.4 %collective-permute-done.12.refs_5_ = f32[672,128]{1,0:T(8,128)S(1)} collective-permute-done((f32[672,128]{1,0:T(8,128)S(1)}, f32[672,128]{1,0:T(8,128)S(1)}, u32[]{:S(2)}, u32[]{:S(2)}) %collective-permute-start.12) | collective-permute-done | bytes 344096 | tf_op jit(solution)/shard_map/ppermute | solution.py:200
  25.0 5.1 %collective-permute-start = (f32[672,128]{1,0:T(8,128)S(1)}, f32[672,128]{1,0:T(8,128)S(1)}, u32[]{:S(2)}, u32[]{:S(2)}) collective-permute-start(f32[672,128]{1,0:T(8,128)S(1)} %get-tuple-element.38), channel_id=1, source_target_pairs={{0,80},{16,64},{32,112},{48,96},{64,16},{80,0},{96,48},{112,32},{1... | collective-permute-start | bytes 1032200 | tf_op jit(solution)/shard_map/ppermute | solution.py:200
  30.0 3.2 %collective-permute-start.1 = (f32[672,128]{1,0:T(8,128)S(1)}, f32[672,128]{1,0:T(8,128)S(1)}, u32[]{:S(2)}, u32[]{:S(2)}) collective-permute-start(f32[672,128]{1,0:T(8,128)S(1)} %get-tuple-element.37), channel_id=1, source_target_pairs={{0,64},{16,80},{32,96},{48,112},{64,0},{80,16},{96,32},{112,48},{1... | collective-permute-start | bytes 1032200 | tf_op jit(solution)/shard_map/ppermute | solution.py:200
  34.8 6.8 %collective-permute-start.3 = (f32[672,128]{1,0:T(8,128)S(1)}, f32[672,128]{1,0:T(8,128)}, u32[]{:S(2)}, u32[]{:S(2)}) collective-permute-start(f32[672,128]{1,0:T(8,128)S(1)} %get-tuple-element.35), channel_id=1, source_target_pairs={{0,32},{16,48},{32,64},{48,80},{64,96},{80,112},{96,0},{112,16},{1... | collective-permute-start | bytes 1032200 | tf_op jit(solution)/shard_map/ppermute | solution.py:200
  42.8 10.2 %collective-permute-done.refs_0_ = f32[672,128]{1,0:T(8,128)S(1)} collective-permute-done((f32[672,128]{1,0:T(8,128)S(1)}, f32[672,128]{1,0:T(8,128)S(1)}, u32[]{:S(2)}, u32[]{:S(2)}) %collective-permute-start) | collective-permute-done | bytes 344096 | tf_op jit(solution)/shard_map/ppermute | solution.py:200
  55.8 6.0 %collective-permute-start.6 = (f32[672,128]{1,0:T(8,128)S(1)}, f32[672,128]{1,0:T(8,128)}, u32[]{:S(2)}, u32[]{:S(2)}) collective-permute-start(f32[672,128]{1,0:T(8,128)S(1)} %get-tuple-element.32), channel_id=1, source_target_pairs={{0,16},{16,0},{32,48},{48,32},{64,80},{80,64},{96,112},{112,96},{1... | collective-permute-start | bytes 1032200 | tf_op jit(solution)/shard_map/ppermute | solution.py:200
  62.5 6.6 %shard_map.42 = (bf16[672,1024]{1,0:T(8,128)(2,1)}, bf16[672,1024]{1,0:T(8,128)(2,1)}, f32[2,4,72,128]{3,2,1,0:T(8,128)}) custom-call(s32[10]{0:T(128)} %stack.91.pos, f32[96,672]{1,0:T(8,128)} %bitcast.121, f32[672,128]{1,0:T(8,128)} %copy-done.5, f32[672,128]{1,0:T(8,128)} %copy-done.7, f32[672,128]{1,0:T(8,128)} %copy-done.8, f32[672,128]{1,0:T(8,128)} %copy-done, ...), custom_call_target="tpu_custom_call" | custom-call | flops 792723456 | bytes 6291456 | tf_op jit(solution)/shard_map/pallas_call | solution.py:101
  70.1 6.6 %shard_map.41 = (bf16[672,1024]{1,0:T(8,128)(2,1)}, bf16[672,1024]{1,0:T(8,128)(2,1)}, f32[2,4,72,128]{3,2,1,0:T(8,128)}) custom-call(s32[10]{0:T(128)} %stack.91.pos, f32[96,672]{1,0:T(8,128)} %bitcast.122, f32[672,128]{1,0:T(8,128)} %copy-done.3, f32[672,128]{1,0:T(8,128)} %copy-done.6, f32[672,128]{1,0:T(8,128)} %collective-permute-done.2.refs_2_, ...), custom_call_target="tpu_custom_call" | custom-call | flops 792723456 | bytes 6291456 | tf_op jit(solution)/shard_map/pallas_call | solution.py:101
  79.2 2.4 %collective-permute-start.15 = (f32[72,128]{1,0:T(8,128)S(1)}, f32[72,128]{1,0:T(8,128)S(1)}, u32[]{:S(2)}, u32[]{:S(2)}) collective-permute-start(f32[72,128]{1,0:T(8,128)S(1)} %get-tuple-element.51), channel_id=1, source_target_pairs={{0,64},{16,80},{32,96},{48,112},{64,0},{80,16},{96,32},{112,48},{1... | collective-permute-start | bytes 110600 | tf_op jit(solution)/shard_map/ppermute | solution.py:50
  81.7 2.5 %collective-permute-start.17 = (f32[72,128]{1,0:T(8,128)S(1)}, f32[72,128]{1,0:T(8,128)S(1)}, u32[]{:S(2)}, u32[]{:S(2)}) collective-permute-start(f32[72,128]{1,0:T(8,128)S(1)} %get-tuple-element.49), channel_id=1, source_target_pairs={{0,96},{16,112},{32,0},{48,16},{64,32},{80,48},{96,64},{112,80},{1... | collective-permute-start | bytes 110600 | tf_op jit(solution)/shard_map/ppermute | solution.py:50
  85.6 2.8 %collective-permute-start.18 = (f32[72,128]{1,0:T(8,128)S(1)}, f32[72,128]{1,0:T(8,128)S(1)}, u32[]{:S(2)}, u32[]{:S(2)}) collective-permute-start(f32[72,128]{1,0:T(8,128)S(1)} %fusion.17), channel_id=1, source_target_pairs={{0,8},{1,9},{2,10},{3,11},{4,12},{5,13},{6,14},{7,15},{8,0},{9,1},... | collective-permute-start | bytes 110600 | tf_op jit(solution)/shard_map/ppermute | solution.py:44
  88.8 2.4 %collective-permute-start.20 = (f32[72,128]{1,0:T(8,128)S(1)}, f32[72,128]{1,0:T(8,128)S(1)}, u32[]{:S(2)}, u32[]{:S(2)}) collective-permute-start(f32[72,128]{1,0:T(8,128)S(1)} %fusion.17), channel_id=1, source_target_pairs={{0,12},{1,13},{2,14},{3,15},{4,0},{5,1},{6,2},{7,3},{8,4},{9,5},{1... | collective-permute-start | bytes 110600 | tf_op jit(solution)/shard_map/ppermute | solution.py:44
  92.6 3.7 %collective-permute-start.21 = (f32[72,128]{1,0:T(8,128)S(1)}, f32[72,128]{1,0:T(8,128)S(1)}, u32[]{:S(2)}, u32[]{:S(2)}) collective-permute-start(f32[72,128]{1,0:T(8,128)S(1)} %add_add_fusion.3), channel_id=1, source_target_pairs={{0,2},{1,3},{2,0},{3,1},{4,6},{5,7},{6,4},{7,5},{8,10},{9,11},{10,... | collective-permute-start | bytes 110600 | tf_op jit(solution)/shard_map/ppermute | solution.py:44
  100.7 2.6 %collective-permute-start.24 = (f32[72,128]{1,0:T(8,128)S(1)}, f32[72,128]{1,0:T(8,128)S(1)}, u32[]{:S(2)}, u32[]{:S(2)}) collective-permute-start(f32[72,128]{1,0:T(8,128)S(1)} %add_add_fusion.2), channel_id=1, source_target_pairs={{0,96},{16,112},{32,0},{48,16},{64,32},{80,48},{96,64},{112,80},{1... | collective-permute-start | bytes 110600 | tf_op jit(solution)/shard_map/ppermute | solution.py:54
  104.3 3.4 %collective-permute-done.25 = f32[72,128]{1,0:T(8,128)S(1)} collective-permute-done((f32[72,128]{1,0:T(8,128)S(1)}, f32[72,128]{1,0:T(8,128)S(1)}, u32[]{:S(2)}, u32[]{:S(2)}) %collective-permute-start.25) | collective-permute-done | bytes 36896 | tf_op jit(solution)/shard_map/ppermute | solution.py:54
  107.7 6.0 %collective-permute-start.27 = (f32[4,72,128]{2,1,0:T(8,128)S(1)}, f32[4,72,128]{2,1,0:T(8,128)S(1)}, u32[]{:S(2)}, u32[]{:S(2)}) collective-permute-start(f32[4,72,128]{2,1,0:T(8,128)S(1)} %get-tuple-element.48), channel_id=1, source_target_pairs={{0,16},{16,0},{32,48},{48,32},{64,80},{80,64},{96,112},{112,96},{1... | collective-permute-start | bytes 442376 | tf_op jit(solution)/shard_map/ppermute | solution.py:56
  115.4 8.8 %shard_map.43 = (f32[2,4,72,128]{3,2,1,0:T(8,128)}, f32[96,672]{1,0:T(8,128)}) custom-call(s32[10]{0:T(128)} %stack.91.pos, f32[2,4,72,128]{3,2,1,0:T(8,128)} %pad_maximum_fusion.m_ref, bf16[672,1024]{1,0:T(8,128)(2,1)} %get-tuple-element.16.hi0, bf16[672,1024]{1,0:T(8,128)(2,1)} %get-tuple-element.17.lo0, bf16[672,1024]{1,0:T(8,128)(2,1)} %get-tuple-element.18.hi1, ...), custom_call_target="tpu_custom_call" | custom-call | flops 1585446912 | bytes 6291456 | tf_op jit(solution)/shard_map/pallas_call | solution.py:131
  129.7 2.7 %collective-permute-start.31 = (f32[72,128]{1,0:T(8,128)S(1)}, f32[72,128]{1,0:T(8,128)S(1)}, u32[]{:S(2)}, u32[]{:S(2)}) collective-permute-start(f32[72,128]{1,0:T(8,128)S(1)} %get-tuple-element.44), channel_id=1, source_target_pairs={{0,96},{16,112},{32,0},{48,16},{64,32},{80,48},{96,64},{112,80},{1... | collective-permute-start | bytes 110600 | tf_op jit(solution)/shard_map/ppermute | solution.py:50
  132.4 8.8 %cholesky.44 = f32[96,96]{1,0:T(8,128)S(1)} custom-call(f32[96,96]{1,0:T(8,128)S(1)} %fusion.11), custom_call_target="Cholesky" | custom-call | tf_op jit(solution)/shard_map/jit(cholesky)/cholesky | solution.py:180
  142.5 2.4 %collective-permute-start.33 = (f32[72,128]{1,0:T(8,128)S(1)}, f32[72,128]{1,0:T(8,128)S(1)}, u32[]{:S(2)}, u32[]{:S(2)}) collective-permute-start(f32[72,128]{1,0:T(8,128)S(1)} %fusion.15), channel_id=1, source_target_pairs={{0,4},{1,5},{2,6},{3,7},{4,8},{5,9},{6,10},{7,11},{8,12},{9,13},{1... | collective-permute-start | bytes 110600 | tf_op jit(solution)/shard_map/ppermute | solution.py:44
  149.7 2.4 %collective-permute-start.36 = (f32[72,128]{1,0:T(8,128)S(1)}, f32[72,128]{1,0:T(8,128)S(1)}, u32[]{:S(2)}, u32[]{:S(2)}) collective-permute-start(f32[72,128]{1,0:T(8,128)S(1)} %add_add_fusion.1), channel_id=1, source_target_pairs={{0,1},{1,2},{2,3},{3,0},{4,5},{5,6},{6,7},{7,4},{8,9},{9,10},{10,1... | collective-permute-start | bytes 110600 | tf_op jit(solution)/shard_map/ppermute | solution.py:44
  157.3 7.4 %custom-call.6 = f32[1,96,96]{1,2,0:T(8,128)S(1)} custom-call(f32[1,96,96]{2,1,0:T(8,128)S(1)} %fusion.6), custom_call_target="InvertDiagBlocksLowerTriangular" | custom-call | tf_op jit(solution)/shard_map/jit(_solve_triangular)/triangular_solve | solution.py:181
  164.7 4.1 %collective-permute-start.41 = (f32[4,72,128]{2,1,0:T(8,128)S(1)}, f32[4,72,128]{2,1,0:T(8,128)S(1)}, u32[]{:S(2)}, u32[]{:S(2)}) collective-permute-start(f32[4,72,128]{2,1,0:T(8,128)S(1)} %get-tuple-element.43), channel_id=1, source_target_pairs={{0,16},{16,0},{32,48},{48,32},{64,80},{80,64},{96,112},{112,96},{1... | collective-permute-start | bytes 442376 | tf_op jit(solution)/shard_map/ppermute | solution.py:56
  170.6 2.1 %shard_map.44.m_ref = f32[96,672]{1,0:T(8,128)} custom-call(s32[10]{0:T(128)} %stack.91.pos, f32[2,4,72,128]{3,2,1,0:T(8,128)} %pad_maximum_fusion.1.w_ref, f32[96,96]{1,0:T(8,128)} %fusion.4.linv), custom_call_target="tpu_custom_call" | custom-call | tf_op jit(solution)/shard_map/pallas_call | solution.py:147
  174.2 8.8 %cholesky.55 = f32[96,96]{1,0:T(8,128)S(1)} custom-call(f32[96,96]{1,0:T(8,128)S(1)} %fusion.9), custom_call_target="Cholesky" | custom-call | tf_op jit(solution)/shard_map/jit(cholesky)/cholesky | solution.py:180
  184.4 7.4 %custom-call.7 = f32[1,96,96]{1,2,0:T(8,128)S(1)} custom-call(f32[1,96,96]{2,1,0:T(8,128)S(1)} %fusion.7), custom_call_target="InvertDiagBlocksLowerTriangular" | custom-call | tf_op jit(solution)/shard_map/jit(_solve_triangular)/triangular_solve | solution.py:181
  192.6 6.2 %shard_map.45 = (f32[96,672]{1,0:T(8,128)}, f32[2,8,128,96]{3,2,1,0:T(8,128)}) custom-call(f32[96,96]{1,0:T(8,128)} %fusion.2.linv, f32[96,672]{1,0:T(8,128)} %shard_map.44.m_ref, bf16[672,1024]{1,0:T(8,128)(2,1)} %get-tuple-element.16.hi0, bf16[672,1024]{1,0:T(8,128)(2,1)} %get-tuple-element.17.lo0, bf16[672,1024]{1,0:T(8,128)(2,1)} %get-tuple-element.18.hi1, ...), custom_call_target="tpu_custom_call" | custom-call | flops 792723456 | bytes 7340032 | tf_op jit(solution)/shard_map/pallas_call | solution.py:168
  (118 shorter events, 51.3 us)
Async XLA Ops:
  4.7 11.2 %collective-permute-start.10 = (f32[672,128]{1,0:T(8,128)S(1)}, f32[672,128]{1,0:T(8,128)S(1)}, u32[]{:S(2)}, u32[]{:S(2)}) collective-permute-start(f32[672,128]{1,0:T(8,128)S(1)} %get-tuple-element.27), channel_id=1, source_target_pairs={{0,32},{16,48},{32,64},{48,80},{64,96},{80,112},{96,0},{112,16},{1... | collective-permute-start | bytes 1032200 | tf_op jit(solution)/shard_map/ppermute | solution.py:200
  6.8 11.0 %collective-permute-start.11 = (f32[672,128]{1,0:T(8,128)S(1)}, f32[672,128]{1,0:T(8,128)S(1)}, u32[]{:S(2)}, u32[]{:S(2)}) collective-permute-start(f32[672,128]{1,0:T(8,128)S(1)} %get-tuple-element.26), channel_id=1, source_target_pairs={{0,112},{16,96},{32,16},{48,0},{64,48},{80,32},{96,80},{112,64},{1... | collective-permute-start | bytes 1032200 | tf_op jit(solution)/shard_map/ppermute | solution.py:200
  8.9 16.0 %collective-permute-start.12 = (f32[672,128]{1,0:T(8,128)S(1)}, f32[672,128]{1,0:T(8,128)S(1)}, u32[]{:S(2)}, u32[]{:S(2)}) collective-permute-start(f32[672,128]{1,0:T(8,128)S(1)} %get-tuple-element.25), channel_id=1, source_target_pairs={{0,96},{16,112},{32,0},{48,16},{64,32},{80,48},{96,64},{112,80},{1... | collective-permute-start | bytes 1032200 | tf_op jit(solution)/shard_map/ppermute | solution.py:200
  10.5 19.5 %collective-permute-start.13 = (f32[672,128]{1,0:T(8,128)S(1)}, f32[672,128]{1,0:T(8,128)S(1)}, u32[]{:S(2)}, u32[]{:S(2)}) collective-permute-start(f32[672,128]{1,0:T(8,128)S(1)} %get-tuple-element.39), channel_id=1, source_target_pairs={{0,16},{16,0},{32,48},{48,32},{64,80},{80,64},{96,112},{112,96},{1... | collective-permute-start | bytes 1032200 | tf_op jit(solution)/shard_map/ppermute | solution.py:200
  10.5 22.7 %collective-permute-start.7 = (f32[672,128]{1,0:T(8,128)S(1)}, f32[672,128]{1,0:T(8,128)S(1)}, u32[]{:S(2)}, u32[]{:S(2)}) collective-permute-start(f32[672,128]{1,0:T(8,128)S(1)} %get-tuple-element.30), channel_id=1, source_target_pairs={{0,80},{16,64},{32,112},{48,96},{64,16},{80,0},{96,48},{112,32},{1... | collective-permute-start | bytes 1032200 | tf_op jit(solution)/shard_map/ppermute | solution.py:200
  15.9 18.9 %collective-permute-start.8 = (f32[672,128]{1,0:T(8,128)S(1)}, f32[672,128]{1,0:T(8,128)S(1)}, u32[]{:S(2)}, u32[]{:S(2)}) collective-permute-start(f32[672,128]{1,0:T(8,128)S(1)} %get-tuple-element.29), channel_id=1, source_target_pairs={{0,64},{16,80},{32,96},{48,112},{64,0},{80,16},{96,32},{112,48},{1... | collective-permute-start | bytes 1032200 | tf_op jit(solution)/shard_map/ppermute | solution.py:200
  17.8 23.7 %collective-permute-start.9 = (f32[672,128]{1,0:T(8,128)S(1)}, f32[672,128]{1,0:T(8,128)S(1)}, u32[]{:S(2)}, u32[]{:S(2)}) collective-permute-start(f32[672,128]{1,0:T(8,128)S(1)} %get-tuple-element.28), channel_id=1, source_target_pairs={{0,48},{16,32},{32,80},{48,64},{64,112},{80,96},{96,16},{112,0},{1... | collective-permute-start | bytes 1032200 | tf_op jit(solution)/shard_map/ppermute | solution.py:200
  25.0 28.0 %collective-permute-start = (f32[672,128]{1,0:T(8,128)S(1)}, f32[672,128]{1,0:T(8,128)S(1)}, u32[]{:S(2)}, u32[]{:S(2)}) collective-permute-start(f32[672,128]{1,0:T(8,128)S(1)} %get-tuple-element.38), channel_id=1, source_target_pairs={{0,80},{16,64},{32,112},{48,96},{64,16},{80,0},{96,48},{112,32},{1... | collective-permute-start | bytes 1032200 | tf_op jit(solution)/shard_map/ppermute | solution.py:200
  30.0 25.0 %collective-permute-start.1 = (f32[672,128]{1,0:T(8,128)S(1)}, f32[672,128]{1,0:T(8,128)S(1)}, u32[]{:S(2)}, u32[]{:S(2)}) collective-permute-start(f32[672,128]{1,0:T(8,128)S(1)} %get-tuple-element.37), channel_id=1, source_target_pairs={{0,64},{16,80},{32,96},{48,112},{64,0},{80,16},{96,32},{112,48},{1... | collective-permute-start | bytes 1032200 | tf_op jit(solution)/shard_map/ppermute | solution.py:200
  33.2 35.9 %collective-permute-start.2 = (f32[672,128]{1,0:T(8,128)S(1)}, f32[672,128]{1,0:T(8,128)}, u32[]{:S(2)}, u32[]{:S(2)}) collective-permute-start(f32[672,128]{1,0:T(8,128)S(1)} %get-tuple-element.36), channel_id=1, source_target_pairs={{0,48},{16,32},{32,80},{48,64},{64,112},{80,96},{96,16},{112,0},{1... | collective-permute-start | bytes 1032200 | tf_op jit(solution)/shard_map/ppermute | solution.py:200
  34.8 34.7 %collective-permute-start.3 = (f32[672,128]{1,0:T(8,128)S(1)}, f32[672,128]{1,0:T(8,128)}, u32[]{:S(2)}, u32[]{:S(2)}) collective-permute-start(f32[672,128]{1,0:T(8,128)S(1)} %get-tuple-element.35), channel_id=1, source_target_pairs={{0,32},{16,48},{32,64},{48,80},{64,96},{80,112},{96,0},{112,16},{1... | collective-permute-start | bytes 1032200 | tf_op jit(solution)/shard_map/ppermute | solution.py:200
  41.6 27.9 %collective-permute-start.4 = (f32[672,128]{1,0:T(8,128)S(1)}, f32[672,128]{1,0:T(8,128)}, u32[]{:S(2)}, u32[]{:S(2)}) collective-permute-start(f32[672,128]{1,0:T(8,128)S(1)} %get-tuple-element.34), channel_id=1, source_target_pairs={{0,112},{16,96},{32,16},{48,0},{64,48},{80,32},{96,80},{112,64},{1... | collective-permute-start | bytes 1032200 | tf_op jit(solution)/shard_map/ppermute | solution.py:200
  53.0 17.1 %collective-permute-start.5 = (f32[672,128]{1,0:T(8,128)S(1)}, f32[672,128]{1,0:T(8,128)}, u32[]{:S(2)}, u32[]{:S(2)}) collective-permute-start(f32[672,128]{1,0:T(8,128)S(1)} %get-tuple-element.33), channel_id=1, source_target_pairs={{0,96},{16,112},{32,0},{48,16},{64,32},{80,48},{96,64},{112,80},{1... | collective-permute-start | bytes 1032200 | tf_op jit(solution)/shard_map/ppermute | solution.py:200
  55.8 14.3 %collective-permute-start.6 = (f32[672,128]{1,0:T(8,128)S(1)}, f32[672,128]{1,0:T(8,128)}, u32[]{:S(2)}, u32[]{:S(2)}) collective-permute-start(f32[672,128]{1,0:T(8,128)S(1)} %get-tuple-element.32), channel_id=1, source_target_pairs={{0,16},{16,0},{32,48},{48,32},{64,80},{80,64},{96,112},{112,96},{1... | collective-permute-start | bytes 1032200 | tf_op jit(solution)/shard_map/ppermute | solution.py:200
  79.2 5.1 %collective-permute-start.15 = (f32[72,128]{1,0:T(8,128)S(1)}, f32[72,128]{1,0:T(8,128)S(1)}, u32[]{:S(2)}, u32[]{:S(2)}) collective-permute-start(f32[72,128]{1,0:T(8,128)S(1)} %get-tuple-element.51), channel_id=1, source_target_pairs={{0,64},{16,80},{32,96},{48,112},{64,0},{80,16},{96,32},{112,48},{1... | collective-permute-start | bytes 110600 | tf_op jit(solution)/shard_map/ppermute | solution.py:50
  81.6 4.0 %collective-permute-start.16 = (f32[72,128]{1,0:T(8,128)S(1)}, f32[72,128]{1,0:T(8,128)S(1)}, u32[]{:S(2)}, u32[]{:S(2)}) collective-permute-start(f32[72,128]{1,0:T(8,128)S(1)} %get-tuple-element.50), channel_id=1, source_target_pairs={{0,32},{16,48},{32,64},{48,80},{64,96},{80,112},{96,0},{112,16},{1... | collective-permute-start | bytes 110600 | tf_op jit(solution)/shard_map/ppermute | solution.py:50
  85.6 5.5 %collective-permute-start.18 = (f32[72,128]{1,0:T(8,128)S(1)}, f32[72,128]{1,0:T(8,128)S(1)}, u32[]{:S(2)}, u32[]{:S(2)}) collective-permute-start(f32[72,128]{1,0:T(8,128)S(1)} %fusion.17), channel_id=1, source_target_pairs={{0,8},{1,9},{2,10},{3,11},{4,12},{5,13},{6,14},{7,15},{8,0},{9,1},... | collective-permute-start | bytes 110600 | tf_op jit(solution)/shard_map/ppermute | solution.py:44
  88.5 4.2 %collective-permute-start.19 = (f32[72,128]{1,0:T(8,128)S(1)}, f32[72,128]{1,0:T(8,128)S(1)}, u32[]{:S(2)}, u32[]{:S(2)}) collective-permute-start(f32[72,128]{1,0:T(8,128)S(1)} %fusion.17), channel_id=1, source_target_pairs={{0,4},{1,5},{2,6},{3,7},{4,8},{5,9},{6,10},{7,11},{8,12},{9,13},{1... | collective-permute-start | bytes 110600 | tf_op jit(solution)/shard_map/ppermute | solution.py:44
  92.6 6.4 %collective-permute-start.21 = (f32[72,128]{1,0:T(8,128)S(1)}, f32[72,128]{1,0:T(8,128)S(1)}, u32[]{:S(2)}, u32[]{:S(2)}) collective-permute-start(f32[72,128]{1,0:T(8,128)S(1)} %add_add_fusion.3), channel_id=1, source_target_pairs={{0,2},{1,3},{2,0},{3,1},{4,6},{5,7},{6,4},{7,5},{8,10},{9,11},{10,... | collective-permute-start | bytes 110600 | tf_op jit(solution)/shard_map/ppermute | solution.py:44
  96.3 4.3 %collective-permute-start.22 = (f32[72,128]{1,0:T(8,128)S(1)}, f32[72,128]{1,0:T(8,128)S(1)}, u32[]{:S(2)}, u32[]{:S(2)}) collective-permute-start(f32[72,128]{1,0:T(8,128)S(1)} %add_add_fusion.3), channel_id=1, source_target_pairs={{0,1},{1,2},{2,3},{3,0},{4,5},{5,6},{6,7},{7,4},{8,9},{9,10},{10,1... | collective-permute-start | bytes 110600 | tf_op jit(solution)/shard_map/ppermute | solution.py:44
  103.2 4.4 %collective-permute-start.25 = (f32[72,128]{1,0:T(8,128)S(1)}, f32[72,128]{1,0:T(8,128)S(1)}, u32[]{:S(2)}, u32[]{:S(2)}) collective-permute-start(f32[72,128]{1,0:T(8,128)S(1)} %add_add_fusion.2), channel_id=1, source_target_pairs={{0,64},{16,80},{32,96},{48,112},{64,0},{80,16},{96,32},{112,48},{1... | collective-permute-start | bytes 110600 | tf_op jit(solution)/shard_map/ppermute | solution.py:54
  103.2 4.4 %collective-permute-start.26 = (f32[72,128]{1,0:T(8,128)S(1)}, f32[72,128]{1,0:T(8,128)S(1)}, u32[]{:S(2)}, u32[]{:S(2)}) collective-permute-start(f32[72,128]{1,0:T(8,128)S(1)} %add_add_fusion.2), channel_id=1, source_target_pairs={{0,32},{16,48},{32,64},{48,80},{64,96},{80,112},{96,0},{112,16},{1... | collective-permute-start | bytes 110600 | tf_op jit(solution)/shard_map/ppermute | solution.py:54
  107.7 7.0 %collective-permute-start.27 = (f32[4,72,128]{2,1,0:T(8,128)S(1)}, f32[4,72,128]{2,1,0:T(8,128)S(1)}, u32[]{:S(2)}, u32[]{:S(2)}) collective-permute-start(f32[4,72,128]{2,1,0:T(8,128)S(1)} %get-tuple-element.48), channel_id=1, source_target_pairs={{0,16},{16,0},{32,48},{48,32},{64,80},{80,64},{96,112},{112,96},{1... | collective-permute-start | bytes 442376 | tf_op jit(solution)/shard_map/ppermute | solution.py:56
  128.0 13.2 %collective-permute-start.29 = (f32[72,128]{1,0:T(8,128)S(1)}, f32[72,128]{1,0:T(8,128)S(1)}, u32[]{:S(2)}, u32[]{:S(2)}) collective-permute-start(f32[72,128]{1,0:T(8,128)S(1)} %get-tuple-element.46), channel_id=1, source_target_pairs={{0,64},{16,80},{32,96},{48,112},{64,0},{80,16},{96,32},{112,48},{1... | collective-permute-start | bytes 110600 | tf_op jit(solution)/shard_map/ppermute | solution.py:50
  129.7 11.5 %collective-permute-start.30 = (f32[72,128]{1,0:T(8,128)S(1)}, f32[72,128]{1,0:T(8,128)S(1)}, u32[]{:S(2)}, u32[]{:S(2)}) collective-permute-start(f32[72,128]{1,0:T(8,128)S(1)} %get-tuple-element.45), channel_id=1, source_target_pairs={{0,32},{16,48},{32,64},{48,80},{64,96},{80,112},{96,0},{112,16},{1... | collective-permute-start | bytes 110600 | tf_op jit(solution)/shard_map/ppermute | solution.py:50
  129.7 11.5 %collective-permute-start.31 = (f32[72,128]{1,0:T(8,128)S(1)}, f32[72,128]{1,0:T(8,128)S(1)}, u32[]{:S(2)}, u32[]{:S(2)}) collective-permute-start(f32[72,128]{1,0:T(8,128)S(1)} %get-tuple-element.44), channel_id=1, source_target_pairs={{0,96},{16,112},{32,0},{48,16},{64,32},{80,48},{96,64},{112,80},{1... | collective-permute-start | bytes 110600 | tf_op jit(solution)/shard_map/ppermute | solution.py:50
  141.3 4.4 %collective-permute-start.32 = (f32[72,128]{1,0:T(8,128)S(1)}, f32[72,128]{1,0:T(8,128)S(1)}, u32[]{:S(2)}, u32[]{:S(2)}) collective-permute-start(f32[72,128]{1,0:T(8,128)S(1)} %fusion.15), channel_id=1, source_target_pairs={{0,8},{1,9},{2,10},{3,11},{4,12},{5,13},{6,14},{7,15},{8,0},{9,1},... | collective-permute-start | bytes 110600 | tf_op jit(solution)/shard_map/ppermute | solution.py:44
  148.4 4.6 %collective-permute-start.35 = (f32[72,128]{1,0:T(8,128)S(1)}, f32[72,128]{1,0:T(8,128)S(1)}, u32[]{:S(2)}, u32[]{:S(2)}) collective-permute-start(f32[72,128]{1,0:T(8,128)S(1)} %add_add_fusion.1), channel_id=1, source_target_pairs={{0,2},{1,3},{2,0},{3,1},{4,6},{5,7},{6,4},{7,5},{8,10},{9,11},{10,... | collective-permute-start | bytes 110600 | tf_op jit(solution)/shard_map/ppermute | solution.py:44
  155.1 9.6 %collective-permute-start.38 = (f32[72,128]{1,0:T(8,128)S(1)}, f32[72,128]{1,0:T(8,128)S(1)}, u32[]{:S(2)}, u32[]{:S(2)}) collective-permute-start(f32[72,128]{1,0:T(8,128)S(1)} %add_add_fusion), channel_id=1, source_target_pairs={{0,96},{16,112},{32,0},{48,16},{64,32},{80,48},{96,64},{112,80},{1... | collective-permute-start | bytes 110600 | tf_op jit(solution)/shard_map/ppermute | solution.py:54
  155.2 9.5 %collective-permute-start.39 = (f32[72,128]{1,0:T(8,128)S(1)}, f32[72,128]{1,0:T(8,128)S(1)}, u32[]{:S(2)}, u32[]{:S(2)}) collective-permute-start(f32[72,128]{1,0:T(8,128)S(1)} %add_add_fusion), channel_id=1, source_target_pairs={{0,64},{16,80},{32,96},{48,112},{64,0},{80,16},{96,32},{112,48},{1... | collective-permute-start | bytes 110600 | tf_op jit(solution)/shard_map/ppermute | solution.py:54
  155.6 9.1 %collective-permute-start.40 = (f32[72,128]{1,0:T(8,128)S(1)}, f32[72,128]{1,0:T(8,128)S(1)}, u32[]{:S(2)}, u32[]{:S(2)}) collective-permute-start(f32[72,128]{1,0:T(8,128)S(1)} %add_add_fusion), channel_id=1, source_target_pairs={{0,32},{16,48},{32,64},{48,80},{64,96},{80,112},{96,0},{112,16},{1... | collective-permute-start | bytes 110600 | tf_op jit(solution)/shard_map/ppermute | solution.py:54
  164.7 5.1 %collective-permute-start.41 = (f32[4,72,128]{2,1,0:T(8,128)S(1)}, f32[4,72,128]{2,1,0:T(8,128)S(1)}, u32[]{:S(2)}, u32[]{:S(2)}) collective-permute-start(f32[4,72,128]{2,1,0:T(8,128)S(1)} %get-tuple-element.43), channel_id=1, source_target_pairs={{0,16},{16,0},{32,48},{48,32},{64,80},{80,64},{96,112},{112,96},{1... | collective-permute-start | bytes 442376 | tf_op jit(solution)/shard_map/ppermute | solution.py:56
  (21 other events, 275.3 us)

commit v2 on v0

v2 whole, which is shorter than its diff:
```python
import jax
import jax.numpy as jnp
from jax import lax
from jax.experimental import pallas as pl
from jax.experimental.pallas import tpu as pltpu
from jax.sharding import PartitionSpec as P

X, R = 672, 96
ROWS = 84
BLOCK = 8
HALF = 1024
F32, BF16 = jnp.float32, jnp.bfloat16
NN = (((1,), (0,)), ((), ()))
NT = (((1,), (1,)), ((), ()))
VMEM_LIMIT = 56 * 1024 * 1024
STARTS = (0, 672, 1216, 1632, 1920)


def split(a):
    hi = a.astype(BF16)
    return hi, (a - hi.astype(F32)).astype(BF16)


def dot3(a, b, dims):
    d = lambda p, q: lax.dot_general(p, q, dims, preferred_element_type=F32)
    return d(a[0], b[0]) + (d(a[0], b[1]) + d(a[1], b[0]))


def dot_full(a, b, dims):
    return lax.dot_general(a, b, dims, precision=lax.Precision.HIGHEST, preferred_element_type=F32)


def perm_gx(dy, dc):
    return [(2 * y + c, 2 * ((y + dy) % 4) + (c ^ dc)) for y in range(4) for c in range(2)]


SAME_CORE = [[(2 * y + c) * 16 + k for y in range(4) for k in range(16)] for c in range(2)]


def total_over_devices(mine, other):
    half = mine + lax.ppermute(other, "gx", perm_gx(0, 1))
    both = ("gx", "gy")
    parts = lax.all_to_all(half.reshape(64, 16, 128), both, 0, 0, axis_index_groups=SAME_CORE)
    piece = jnp.sum(parts, 0)
    whole = lax.all_to_all(
        jnp.broadcast_to(piece[None], (64, 16, 128)), both, 0, 0, axis_index_groups=SAME_CORE
    ).reshape(HALF, 128)
    return whole, lax.ppermute(whole, "gx", perm_gx(0, 1))


def gram_kernel(pos, *refs):
    n = len(refs) - 8 - 6
    blocks, before = refs[:8], refs[8 : 8 + n]
    hi, lo, mine, other, cells, sems = refs[8 + n : 8 + n + 6]
    packed = cells.at[pl.ds(0, 2 * HALF)]
    for i in range(8):
        pltpu.make_async_copy(blocks[i], cells.at[pl.ds(pos[2 + i] * 672, 672)], sems.at[i]).start()
    for i in range(8):
        pltpu.make_async_copy(blocks[i], cells.at[pl.ds(pos[2 + i] * 672, 672)], sems.at[i]).wait()
    for q in range(8):
        a = split(cells[pl.ds(q, X, stride=8), :])
        hi[:, 128 * q : 128 * q + 128] = a[0]
        lo[:, 128 * q : 128 * q + 128] = a[1]
    for j in range(3):
        low, high = 256 * j, min(256 * j + 256, X)
        g = dot3((hi[low:, :], lo[low:, :]), (hi[low:high, :], lo[low:high, :]), NT)
        for t in (2 * j, 2 * j + 1):
            col = g[128 * (t % 2) : , 128 * (t % 2) : 128 * (t % 2) + 128]
            if t < 4:
                packed[STARTS[t] : STARTS[t] + X - 128 * t, :] = col
            elif t == 4:
                packed[STARTS[4] : STARTS[4] + 128, :] = col[:128]
                packed[STARTS[1] : STARTS[1] + 32, 64:] = col[128:160, :64]
                packed[STARTS[1] + 32 : STARTS[1] + 64, 64:] = col[128:160, 64:]
            else:
                packed[0:32, 96:] = col[:32, :32]
    c = pos[1]
    for out, k, half in ((mine, 0, c), (other, 1, 1 - c)):
        value = packed[pl.ds(pl.multiple_of(half * HALF, HALF), HALF), :]
        if n:
            value = value + before[k][...]
        out[...] = value


def gram(pos, blocks, before):
    any_spec = pl.BlockSpec(memory_space=pl.ANY)
    vmem = pl.BlockSpec(memory_space=pltpu.VMEM)
    return pl.pallas_call(
        gram_kernel,
        out_shape=(
            jax.ShapeDtypeStruct((X, 1024), BF16),
            jax.ShapeDtypeStruct((X, 1024), BF16),
            jax.ShapeDtypeStruct((HALF, 128), F32),
            jax.ShapeDtypeStruct((HALF, 128), F32),
        ),
        in_specs=[pl.BlockSpec(memory_space=pltpu.SMEM)] + [any_spec] * 8 + [vmem] * len(before),
        out_specs=(vmem,) * 4,
        scratch_shapes=[pltpu.VMEM((X * 8, 128), F32), pltpu.SemaphoreType.DMA((8,))],
        compiler_params=pltpu.CompilerParams(vmem_limit_bytes=VMEM_LIMIT),
        cost_estimate=pl.CostEstimate(flops=3 * 2 * X * X * 1024, bytes_accessed=6 * 2**20, transcendentals=0),
    )(pos, *blocks, *before)


def unpack(packed, g):
    row = lax.broadcasted_iota(jnp.int32, (128, 128), 0)
    col = lax.broadcasted_iota(jnp.int32, (128, 128), 1)
    lower = row >= col
    g[640:, 640:] = jnp.zeros((32, 128), F32)
    for j in range(5):
        at = 128 * j
        block = packed[STARTS[j] : STARTS[j] + 128, :]
        g[at : at + 128, at : at + 128] = jnp.where(lower, block, block.T)
        for i in range(j + 1, 5):
            first = STARTS[j] + 128 * (i - j)
            block = packed[first : first + 128, :]
            g[128 * i : 128 * i + 128, at : at + 128] = block
            g[at : at + 128, 128 * i : 128 * i + 128] = block.T
        if j < 4:
            last = packed[STARTS[j] + 640 - at : STARTS[j] + X - at, :]
        else:
            last = jnp.concatenate(
                [packed[STARTS[1] : STARTS[1] + 32, 64:], packed[STARTS[1] + 32 : STARTS[1] + 64, 64:]], axis=1
            )
        g[640:, at : at + 128] = last
        g[at : at + 128, 640:] = jnp.concatenate([last, jnp.zeros((96, 128), F32)], axis=0).T
    block = jnp.concatenate([packed[0:32, :], jnp.zeros((96, 128), F32)], axis=0)
    block = jnp.concatenate([block[:, 96:], jnp.zeros((128, 96), F32)], axis=1)
    g[640:, 640:] = jnp.where(lower, block, block.T)[:32]


def inverse_factor(s, work, out):
    eye = (lax.broadcasted_iota(jnp.int32, (R, 128), 0) == lax.broadcasted_iota(jnp.int32, (R, 128), 1)).astype(F32)
    work[:, 128:] = eye
    work[:, :R] = s
    work[:, R:128] = jnp.zeros((R, 128 - R), F32)
    for b in range(R // BLOCK):
        at = BLOCK * b
        left = [work[at + i : at + i + 1, :128] for i in range(BLOCK)]
        right = [work[at + i : at + i + 1, 128:] for i in range(BLOCK)]
        d = {
            (i, j): jnp.broadcast_to(left[i][:, at + j : at + j + 1], (1, 128))
            for i in range(BLOCK) for j in range(i + 1)
        }
        scaled = []
        for t in range(BLOCK):
            inverse = 1.0 / d[t, t]
            scaled.append(left[t] * inverse)
            for i in range(t + 1, BLOCK):
                m = d[i, t] * inverse
                for j in range(t + 1, i + 1):
                    d[i, j] = d[i, j] - m * d[j, t]
                left[i] = left[i] - m * left[t]
                right[i] = right[i] - m * right[t]
        root = [lax.rsqrt(d[t, t]) for t in range(BLOCK)]
        root = [q * (1.5 - 0.5 * (d[t, t] * q) * q) for t, q in enumerate(root)]
        out[at : at + BLOCK, :] = jnp.concatenate([right[t] * root[t] for t in range(BLOCK)], axis=0)
        if at + BLOCK < R:
            rows = jnp.concatenate(
                [jnp.concatenate(left, axis=0), jnp.concatenate(right, axis=0)], axis=1
            )
            step = dot_full(jnp.concatenate(scaled, axis=0).T, rows, NN)
            work[at + BLOCK :, :] = work[at + BLOCK :, :] - step[at + BLOCK : R]


def finish_kernel(pos, mine, other, basis, hi0, lo0, hi1, lo1, factor_t, core, packed, g, work, linv, a, sems):
    fibers = (hi0, lo0, hi1, lo1)
    for i in range(4):
        pltpu.make_async_copy(fibers[i], a.at[i], sems.at[i]).start()
    c = pos[1]
    packed[pl.ds(pl.multiple_of(c * HALF, HALF), HALF), :] = mine[...]
    packed[pl.ds(pl.multiple_of((1 - c) * HALF, HALF), HALF), :] = other[...]
    unpack(packed, g)
    f = basis[...]
    for _ in range(2):
        m = dot_full(f, g[:, :X], NN)
        inverse_factor(dot_full(m, m, NT), work, linv)
        f = dot_full(linv[:, :R], m, NN)
    factor_t[...] = f
    f = split(f)
    for i in range(4):
        pltpu.make_async_copy(fibers[i], a.at[i], sems.at[i]).wait()
    for k in range(2):
        for y in range(8):
            part = a[2 * k, :, 128 * y : 128 * y + 128], a[2 * k + 1, :, 128 * y : 128 * y + 128]
            core[k, y] = dot3(f, part, NN).T


def finish(pos, mine, other, basis_t, fibers):
    any_spec = pl.BlockSpec(memory_space=pl.ANY)
    vmem = pl.BlockSpec(memory_space=pltpu.VMEM)
    return pl.pallas_call(
        finish_kernel,
        out_shape=(jax.ShapeDtypeStruct((R, X), F32), jax.ShapeDtypeStruct((2, 8, 128, R), F32)),
        in_specs=[pl.BlockSpec(memory_space=pltpu.SMEM)] + [vmem] * 3 + [any_spec] * 4,
        out_specs=(vmem, vmem),
        scratch_shapes=[
            pltpu.VMEM((2 * HALF, 128), F32),
            pltpu.VMEM((X, 768), F32),
            pltpu.VMEM((R, 256), F32),
            pltpu.VMEM((R, 128), F32),
            pltpu.VMEM((4, X, 1024), BF16),
            pltpu.SemaphoreType.DMA((4,)),
        ],
        compiler_params=pltpu.CompilerParams(vmem_limit_bytes=VMEM_LIMIT),
        cost_estimate=pl.CostEstimate(flops=3 * 2 * X * R * 2048, bytes_accessed=7 * 2**20, transcendentals=0),
    )(pos, mine, other, basis_t, *fibers)


def per_device(tensor, start_basis):
    me = lax.axis_index("gx")
    y, c = me // 2, me % 2
    offsets = [(dy, dc) for dy in (2, 1, 3, 0) for dc in (1, 0)]
    sources = [2 * ((y - dy) % 4) + (c ^ dc) for dy, dc in offsets]
    pos = jnp.stack([y, c] + sources).astype(jnp.int32)
    basis_t = start_basis.T

    fibers, halves = [], ()
    for k in range(2):
        blocks = []
        for dy, dc in offsets:
            block = lax.dynamic_slice(
                tensor, (2 * (c ^ dc) + k, 0, 0, 128 * ((y + dy) % 4)), (1, ROWS, 8, 128)
            ).reshape(ROWS * 8, 128)
            if dy or dc:
                block = lax.ppermute(block, "gx", perm_gx(dy, dc))
            blocks.append(block)
        hi, lo, *halves = gram(pos, blocks, halves)
        fibers += [hi, lo]

    factor_t, core = finish(pos, *total_over_devices(*halves), basis_t, fibers)

    halves = core.reshape(2, 8, 2, 64, R)
    mine = lax.dynamic_index_in_dim(halves, c, 2, keepdims=False)
    theirs = lax.ppermute(lax.dynamic_index_in_dim(halves, 1 - c, 2, keepdims=False), "gx", perm_gx(0, 1))
    out = jnp.where(c == 0, jnp.concatenate([mine, theirs]), jnp.concatenate([theirs, mine]))
    return factor_t.T, out.transpose(0, 3, 1, 2)


def solution(mesh):
    return jax.shard_map(
        per_device,
        mesh=mesh,
        in_specs=(P(None, "gx", "gy", None), P()),
        out_specs=(P(), P(None, None, "gy", "gx")),
        check_vma=False,
    )
```

time: 504 us -> 149 us (0.30)
  other arithmetic: 151 us -> 2.25 us
  waiting for transfers between devices: 151 us -> 26.2 us
  blocking collectives: 101 us -> 37.6 us
  matrix products: 43.3 us -> 0 us
  starting transfers between devices: 0.04 us -> 40.6 us
  Pallas kernels: 0 us -> 33.4 us
  local copies, waits for them, and re-layouts: 33.4 us -> 7.48 us
  between operations: 18.4 us -> 0.86 us
    psum x1 -> x0, waiting for transfers between devices: 151 us -> none  [per_device(): gram_total = lax.psum(local_gram, ('gx', 'gy'))]
    another operation x32 -> x0, other arithmetic: 149 us -> none  [the longest x22 114 us: per_device(): upper_factor = jnp.linalg.cholesky(gram_total).T]
    all_to_all x1 -> x2, blocking collectives: 101 us -> 37.6 us  [the longest x1 22.1 us: total_over_devices(): lax.all_to_all(half.reshape(64, 16, 128), both, 0, 0, axis_index_groups=S...]
    ppermute x0 -> x17, starting transfers between devices: none -> 40.6 us  [the longest x14 36.8 us: per_device(): block = lax.ppermute(block, 'gx', perm_gx(dy, dc))]
    dot_general x8 -> x0, matrix products: 33.6 us -> none  [the longest x1 18.5 us: species_grams(): jnp.einsum('sxk,syk->sxy', flattened, flattened, precision=lax.Precision....]
    pallas_call x0 -> x3, Pallas kernels: none -> 33.4 us  [the longest x1 20.7 us: finish(): pl.pallas_call(finish_kernel, out_shape=(jax.ShapeDtypeStruct((R, X), F32...]
    ppermute x0 -> x17, waiting for transfers between devices: none -> 26.2 us  [the longest x14 21 us: per_device(): block = lax.ppermute(block, 'gx', perm_gx(dy, dc))]
    another operation x12 -> x0, matrix products: 9.66 us -> none  [the longest x10 8.78 us: per_device(): upper_factor = jnp.linalg.cholesky(gram_total).T]
  transfers between devices with their start and end apart: 1 -> 17, of which waited for: 1 -> 9; matrix products, arithmetic and copies ran while one was open for 0% -> 0% of each run, Pallas kernels for 0% -> 4%
where the time goes in v2:
time: 149 us; the launch traced here: 148 us
  starting transfers between devices  40.6 us (27%)
  blocking collectives  37.6 us (25%)
  Pallas kernels  33.4 us (22%)
  waiting for transfers between devices  26.2 us (18%)
  local copies, waits for them, and re-layouts  7.48 us (5%)
  other arithmetic  2.25 us (2%)
    ppermute x14, starting transfers between devices, per_device(): block = lax.ppermute(block, 'gx', perm_gx(dy, dc))  36.8 us
    all_to_all x1, blocking collectives, total_over_devices(): lax.all_to_all(half.reshape(64, 16, 128), both, 0, 0, axis_index_groups=S...  22.1 us
    ppermute x14, waiting for transfers between devices, per_device(): block = lax.ppermute(block, 'gx', perm_gx(dy, dc))  21 us
    pallas_call x1, Pallas kernels, finish(): pl.pallas_call(finish_kernel, out_shape=(jax.ShapeDtypeStruct((R, X), F32...  20.7 us
    all_to_all x1, blocking collectives, total_over_devices(): lax.all_to_all(jnp.broadcast_to(piece[None], (64, 16, 128)), both, 0, 0,...  15.5 us
    pallas_call x2, Pallas kernels, gram(): pl.pallas_call(gram_kernel, out_shape=(jax.ShapeDtypeStruct((X, 1024), BF...  12.7 us
    reshape x1, local copies, waits for them, and re-layouts, per_device(): block = lax.dynamic_slice(tensor, (2 * (c ^ dc) + k, 0, 0, 128 * ((y + dy...  3.9 us
    ppermute x1, starting transfers between devices, total_over_devices(): return (whole, lax.ppermute(whole, 'gx', perm_gx(0, 1)))  3.2 us
  transfers between devices with their start and end apart: 17, of which 9 were waited for; matrix products, arithmetic and copies ran while one was open for 0% of the time, Pallas kernels for 4%

profile of v2, /device:TPU:1, one launch (start us, length us, event | category | flops | bytes accessed | tf_op | source)
XLA Modules:
  0.0 148.4 jit_solution(778988415632989693)
XLA Ops:
  0.8 3.9 %dynamic-slice_bitcast_fusion.2 = (f32[672,128]{1,0:T(8,128)}, f32[672,128]{1,0:T(8,128)S(1)}, f32[672,128]{1,0:T(8,128)S(1)}, f32[672,128]{1,0:T(8,128)S(1)}, f...) fusion(f32[4,84,8,512]{3,2,1,0:T(8,128)} %param.2, ...), kind=kLoop, calls=%fused_computation.4 | loop fusion | bytes 11010080 | tf_op jit(solution)/shard_map/reshape | solution.py:223
  4.7 2.1 %collective-permute-start.10 = (f32[672,128]{1,0:T(8,128)S(1)}, f32[672,128]{1,0:T(8,128)S(1)}, u32[]{:S(2)}, u32[]{:S(2)}) collective-permute-start(f32[672,128]{1,0:T(8,128)S(1)} %get-tuple-element.25), channel_id=1, source_target_pairs={{0,32},{16,48},{32,64},{48,80},{64,96},{80,112},{96,0},{112,16},{1... | collective-permute-start | bytes 1032200 | tf_op jit(solution)/shard_map/ppermute | solution.py:225
  6.8 2.1 %collective-permute-start.11 = (f32[672,128]{1,0:T(8,128)S(1)}, f32[672,128]{1,0:T(8,128)S(1)}, u32[]{:S(2)}, u32[]{:S(2)}) collective-permute-start(f32[672,128]{1,0:T(8,128)S(1)} %get-tuple-element.24), channel_id=1, source_target_pairs={{0,112},{16,96},{32,16},{48,0},{64,48},{80,32},{96,80},{112,64},{1... | collective-permute-start | bytes 1032200 | tf_op jit(solution)/shard_map/ppermute | solution.py:225
  8.9 1.6 %collective-permute-start.12 = (f32[672,128]{1,0:T(8,128)S(1)}, f32[672,128]{1,0:T(8,128)S(1)}, u32[]{:S(2)}, u32[]{:S(2)}) collective-permute-start(f32[672,128]{1,0:T(8,128)S(1)} %get-tuple-element.23), channel_id=1, source_target_pairs={{0,96},{16,112},{32,0},{48,16},{64,32},{80,48},{96,64},{112,80},{1... | collective-permute-start | bytes 1032200 | tf_op jit(solution)/shard_map/ppermute | solution.py:225
  10.5 0.7 collective-permute-start.7
  11.3 4.6 %collective-permute-done.10.refs_3_ = f32[672,128]{1,0:T(8,128)S(1)} collective-permute-done((f32[672,128]{1,0:T(8,128)S(1)}, f32[672,128]{1,0:T(8,128)S(1)}, u32[]{:S(2)}, u32[]{:S(2)}) %collective-permute-start.10) | collective-permute-done | bytes 344096 | tf_op jit(solution)/shard_map/ppermute | solution.py:225
  15.9 1.6 %collective-permute-start.8 = (f32[672,128]{1,0:T(8,128)S(1)}, f32[672,128]{1,0:T(8,128)S(1)}, u32[]{:S(2)}, u32[]{:S(2)}) collective-permute-start(f32[672,128]{1,0:T(8,128)S(1)} %get-tuple-element.27), channel_id=1, source_target_pairs={{0,64},{16,80},{32,96},{48,112},{64,0},{80,16},{96,32},{112,48},{1... | collective-permute-start | bytes 1032200 | tf_op jit(solution)/shard_map/ppermute | solution.py:225
  17.8 2.8 %collective-permute-start.9 = (f32[672,128]{1,0:T(8,128)S(1)}, f32[672,128]{1,0:T(8,128)S(1)}, u32[]{:S(2)}, u32[]{:S(2)}) collective-permute-start(f32[672,128]{1,0:T(8,128)S(1)} %get-tuple-element.26), channel_id=1, source_target_pairs={{0,48},{16,32},{32,80},{48,64},{64,112},{80,96},{96,16},{112,0},{1... | collective-permute-start | bytes 1032200 | tf_op jit(solution)/shard_map/ppermute | solution.py:225
  20.6 4.4 %collective-permute-done.12.refs_5_ = f32[672,128]{1,0:T(8,128)S(1)} collective-permute-done((f32[672,128]{1,0:T(8,128)S(1)}, f32[672,128]{1,0:T(8,128)S(1)}, u32[]{:S(2)}, u32[]{:S(2)}) %collective-permute-start.12) | collective-permute-done | bytes 344096 | tf_op jit(solution)/shard_map/ppermute | solution.py:225
  24.9 5.1 %collective-permute-start = (f32[672,128]{1,0:T(8,128)S(1)}, f32[672,128]{1,0:T(8,128)S(1)}, u32[]{:S(2)}, u32[]{:S(2)}) collective-permute-start(f32[672,128]{1,0:T(8,128)S(1)} %get-tuple-element.36), channel_id=1, source_target_pairs={{0,80},{16,64},{32,112},{48,96},{64,16},{80,0},{96,48},{112,32},{1... | collective-permute-start | bytes 1032200 | tf_op jit(solution)/shard_map/ppermute | solution.py:225
  30.0 3.2 %collective-permute-start.1 = (f32[672,128]{1,0:T(8,128)S(1)}, f32[672,128]{1,0:T(8,128)S(1)}, u32[]{:S(2)}, u32[]{:S(2)}) collective-permute-start(f32[672,128]{1,0:T(8,128)S(1)} %get-tuple-element.35), channel_id=1, source_target_pairs={{0,64},{16,80},{32,96},{48,112},{64,0},{80,16},{96,32},{112,48},{1... | collective-permute-start | bytes 1032200 | tf_op jit(solution)/shard_map/ppermute | solution.py:225
  33.2 1.5 %collective-permute-start.2 = (f32[672,128]{1,0:T(8,128)S(1)}, f32[672,128]{1,0:T(8,128)}, u32[]{:S(2)}, u32[]{:S(2)}) collective-permute-start(f32[672,128]{1,0:T(8,128)S(1)} %get-tuple-element.34), channel_id=1, source_target_pairs={{0,48},{16,32},{32,80},{48,64},{64,112},{80,96},{96,16},{112,0},{1... | collective-permute-start | bytes 1032200 | tf_op jit(solution)/shard_map/ppermute | solution.py:225
  34.8 6.8 %collective-permute-start.3 = (f32[672,128]{1,0:T(8,128)S(1)}, f32[672,128]{1,0:T(8,128)}, u32[]{:S(2)}, u32[]{:S(2)}) collective-permute-start(f32[672,128]{1,0:T(8,128)S(1)} %get-tuple-element.33), channel_id=1, source_target_pairs={{0,32},{16,48},{32,64},{48,80},{64,96},{80,112},{96,0},{112,16},{1... | collective-permute-start | bytes 1032200 | tf_op jit(solution)/shard_map/ppermute | solution.py:225
  41.6 1.2 collective-permute-start.4
  42.8 10.2 %collective-permute-done.refs_0_ = f32[672,128]{1,0:T(8,128)S(1)} collective-permute-done((f32[672,128]{1,0:T(8,128)S(1)}, f32[672,128]{1,0:T(8,128)S(1)}, u32[]{:S(2)}, u32[]{:S(2)}) %collective-permute-start) | collective-permute-done | bytes 344096 | tf_op jit(solution)/shard_map/ppermute | solution.py:225
  53.0 2.1 %collective-permute-start.5 = (f32[672,128]{1,0:T(8,128)S(1)}, f32[672,128]{1,0:T(8,128)}, u32[]{:S(2)}, u32[]{:S(2)}) collective-permute-start(f32[672,128]{1,0:T(8,128)S(1)} %get-tuple-element.31), channel_id=1, source_target_pairs={{0,96},{16,112},{32,0},{48,16},{64,32},{80,48},{96,64},{112,80},{1... | collective-permute-start | bytes 1032200 | tf_op jit(solution)/shard_map/ppermute | solution.py:225
  55.1 0.7 copy-done.8
  55.8 6.0 %collective-permute-start.6 = (f32[672,128]{1,0:T(8,128)S(1)}, f32[672,128]{1,0:T(8,128)}, u32[]{:S(2)}, u32[]{:S(2)}) collective-permute-start(f32[672,128]{1,0:T(8,128)S(1)} %get-tuple-element.30), channel_id=1, source_target_pairs={{0,16},{16,0},{32,48},{48,32},{64,80},{80,64},{96,112},{112,96},{1... | collective-permute-start | bytes 1032200 | tf_op jit(solution)/shard_map/ppermute | solution.py:225
  62.5 6.1 %shard_map.41 = (bf16[672,1024]{1,0:T(8,128)(2,1)}, bf16[672,1024]{1,0:T(8,128)(2,1)}, f32[1024,128]{1,0:T(8,128)}, f32[1024,128]{1,0:T(8,128)}) custom-call(s32[10]{0:T(128)} %stack.43.pos, f32[672,128]{1,0:T(8,128)} %copy-done.7, f32[672,128]{1,0:T(8,128)} %copy-done.9, f32[672,128]{1,0:T(8,128)} %copy-done.10, f32[672,128]{1,0:T(8,128)} %copy-done.2, ...), custom_call_target="tpu_custom_call" | custom-call | flops 2774532096 | bytes 6291456 | tf_op jit(solution)/shard_map/pallas_call | solution.py:88
  68.6 0.8 collective-permute-done.3.refs_3_
  70.1 6.7 %shard_map.42 = (bf16[672,1024]{1,0:T(8,128)(2,1)}, bf16[672,1024]{1,0:T(8,128)(2,1)}, f32[1024,128]{1,0:T(8,128)}, f32[1024,128]{1,0:T(8,128)}) custom-call(s32[10]{0:T(128)} %stack.43.pos, f32[672,128]{1,0:T(8,128)} %copy-done.5, f32[672,128]{1,0:T(8,128)} %copy-done.8, f32[672,128]{1,0:T(8,128)} %collective-permute-done.2.refs_2_, ...), custom_call_target="tpu_custom_call" | custom-call | flops 2774532096 | bytes 6291456 | tf_op jit(solution)/shard_map/pallas_call | solution.py:88
  76.8 2.1 %collective-permute-done.14 = f32[1024,128]{1,0:T(8,128)S(1)} collective-permute-done((f32[1024,128]{1,0:T(8,128)}, f32[1024,128]{1,0:T(8,128)S(1)}, u32[]{:S(2)}, u32[]{:S(2)}) %collective-permute-start.14) | collective-permute-done | bytes 524320 | tf_op jit(solution)/shard_map/ppermute | solution.py:41
  78.9 1.1 add.192
  80.0 22.1 %all_to_all.10 = f32[64,16,128]{2,1,0:T(8,128)S(1)} all-to-all(f32[64,16,128]{2,1,0:T(8,128)S(1)} %bitcast.53), channel_id=1, replica_groups={{0,1,2,3,4,5,6,7,8,9,10,11,12,13,14,15,32,33,34,35,36,37,38,39,40,41,42..., dimensions={0} | all-to-all | bytes 1048576 | tf_op jit(solution)/shard_map/all_to_all | solution.py:43
  102.3 15.5 %all_to_all.11 = f32[64,16,128]{2,1,0:T(8,128)S(1)} all-to-all(f32[64,16,128]{2,1,0:T(8,128)S(1)} %broadcast_in_dim.2), channel_id=1, replica_groups={{0,1,2,3,4,5,6,7,8,9,10,11,12,13,14,15,32,33,34,35,36,37,38,39,40,41,42..., dimensions={0} | all-to-all | bytes 1048576 | tf_op jit(solution)/shard_map/all_to_all | solution.py:45
  117.8 3.2 %collective-permute-start.15 = (f32[1024,128]{1,0:T(8,128)S(1)}, f32[1024,128]{1,0:T(8,128)S(1)}, u32[]{:S(2)}, u32[]{:S(2)}) collective-permute-start(f32[1024,128]{1,0:T(8,128)S(1)} %bitcast.54), channel_id=1, source_target_pairs={{0,16},{16,0},{32,48},{48,32},{64,80},{80,64},{96,112},{112,96},{1... | collective-permute-start | bytes 1572872 | tf_op jit(solution)/shard_map/ppermute | solution.py:48
  121.0 1.5 %collective-permute-done.15.other = f32[1024,128]{1,0:T(8,128)S(1)} collective-permute-done((f32[1024,128]{1,0:T(8,128)S(1)}, f32[1024,128]{1,0:T(8,128)S(1)}, u32[]{:S(2)}, u32[]{:S(2)}) %collective-permute-start.15) | collective-permute-done | bytes 524320 | tf_op jit(solution)/shard_map/ppermute | solution.py:48
  122.5 0.8 copy-done.1
  123.3 20.7 %shard_map.43 = (f32[96,672]{1,0:T(8,128)}, f32[2,8,128,96]{3,2,1,0:T(8,128)}) custom-call(s32[10]{0:T(128)} %stack.43.pos, f32[1024,128]{1,0:T(8,128)} %bitcast.55, f32[1024,128]{1,0:T(8,128)} %copy-done.1, f32[96,672]{1,0:T(8,128)} %bitcast.57, bf16[672,1024]{1,0:T(8,128)(2,1)} %get-tuple-element.16.hi0, bf16[672,1024]{1,0:T(8,128)(2,1)} %get-tuple-element.17.lo0, ...), custom_call_target="tpu_custom_call" | custom-call | flops 792723456 | bytes 7340032 | tf_op jit(solution)/shard_map/pallas_call | solution.py:191
  144.0 1.3 dynamic-slice_bitcast_fusion.1
  145.8 1.5 %collective-permute-done.16 = f32[2,8,64,96]{3,2,1,0:T(8,128)S(1)} collective-permute-done((f32[2,8,64,96]{3,2,1,0:T(8,128)S(1)}, f32[2,8,64,96]{3,2,1,0:T(8,128)S(1)}, u32[]{:S(2)}, u32[]{:S(2)}) %collective-permute-start.16) | collective-permute-done | bytes 393248 | tf_op jit(solution)/shard_map/ppermute | solution.py:234
  147.3 1.1 fusion
  (36 shorter events, 2.4 us)
Async XLA Ops:
  4.7 11.2 %collective-permute-start.10 = (f32[672,128]{1,0:T(8,128)S(1)}, f32[672,128]{1,0:T(8,128)S(1)}, u32[]{:S(2)}, u32[]{:S(2)}) collective-permute-start(f32[672,128]{1,0:T(8,128)S(1)} %get-tuple-element.25), channel_id=1, source_target_pairs={{0,32},{16,48},{32,64},{48,80},{64,96},{80,112},{96,0},{112,16},{1... | collective-permute-start | bytes 1032200 | tf_op jit(solution)/shard_map/ppermute | solution.py:225
  6.8 11.0 %collective-permute-start.11 = (f32[672,128]{1,0:T(8,128)S(1)}, f32[672,128]{1,0:T(8,128)S(1)}, u32[]{:S(2)}, u32[]{:S(2)}) collective-permute-start(f32[672,128]{1,0:T(8,128)S(1)} %get-tuple-element.24), channel_id=1, source_target_pairs={{0,112},{16,96},{32,16},{48,0},{64,48},{80,32},{96,80},{112,64},{1... | collective-permute-start | bytes 1032200 | tf_op jit(solution)/shard_map/ppermute | solution.py:225
  8.9 16.0 %collective-permute-start.12 = (f32[672,128]{1,0:T(8,128)S(1)}, f32[672,128]{1,0:T(8,128)S(1)}, u32[]{:S(2)}, u32[]{:S(2)}) collective-permute-start(f32[672,128]{1,0:T(8,128)S(1)} %get-tuple-element.23), channel_id=1, source_target_pairs={{0,96},{16,112},{32,0},{48,16},{64,32},{80,48},{96,64},{112,80},{1... | collective-permute-start | bytes 1032200 | tf_op jit(solution)/shard_map/ppermute | solution.py:225
  10.5 19.5 %collective-permute-start.13 = (f32[672,128]{1,0:T(8,128)S(1)}, f32[672,128]{1,0:T(8,128)S(1)}, u32[]{:S(2)}, u32[]{:S(2)}) collective-permute-start(f32[672,128]{1,0:T(8,128)S(1)} %get-tuple-element.37), channel_id=1, source_target_pairs={{0,16},{16,0},{32,48},{48,32},{64,80},{80,64},{96,112},{112,96},{1... | collective-permute-start | bytes 1032200 | tf_op jit(solution)/shard_map/ppermute | solution.py:225
  10.5 22.7 %collective-permute-start.7 = (f32[672,128]{1,0:T(8,128)S(1)}, f32[672,128]{1,0:T(8,128)S(1)}, u32[]{:S(2)}, u32[]{:S(2)}) collective-permute-start(f32[672,128]{1,0:T(8,128)S(1)} %get-tuple-element.28), channel_id=1, source_target_pairs={{0,80},{16,64},{32,112},{48,96},{64,16},{80,0},{96,48},{112,32},{1... | collective-permute-start | bytes 1032200 | tf_op jit(solution)/shard_map/ppermute | solution.py:225
  15.9 46.7 %copy-start.2 = (f32[672,128]{1,0:T(8,128)}, f32[672,128]{1,0:T(8,128)S(1)}, u32[]{:S(2)}) copy-start(f32[672,128]{1,0:T(8,128)S(1)} %collective-permute-done.10.refs_3_) | copy-start | bytes 1032196
  15.9 18.9 %collective-permute-start.8 = (f32[672,128]{1,0:T(8,128)S(1)}, f32[672,128]{1,0:T(8,128)S(1)}, u32[]{:S(2)}, u32[]{:S(2)}) collective-permute-start(f32[672,128]{1,0:T(8,128)S(1)} %get-tuple-element.27), channel_id=1, source_target_pairs={{0,64},{16,80},{32,96},{48,112},{64,0},{80,16},{96,32},{112,48},{1... | collective-permute-start | bytes 1032200 | tf_op jit(solution)/shard_map/ppermute | solution.py:225
  17.8 44.7 %copy-start.3 = (f32[672,128]{1,0:T(8,128)}, f32[672,128]{1,0:T(8,128)S(1)}, u32[]{:S(2)}) copy-start(f32[672,128]{1,0:T(8,128)S(1)} %collective-permute-done.11.refs_4_) | copy-start | bytes 1032196
  17.8 23.7 %collective-permute-start.9 = (f32[672,128]{1,0:T(8,128)S(1)}, f32[672,128]{1,0:T(8,128)S(1)}, u32[]{:S(2)}, u32[]{:S(2)}) collective-permute-start(f32[672,128]{1,0:T(8,128)S(1)} %get-tuple-element.26), channel_id=1, source_target_pairs={{0,48},{16,32},{32,80},{48,64},{64,112},{80,96},{96,16},{112,0},{1... | collective-permute-start | bytes 1032200 | tf_op jit(solution)/shard_map/ppermute | solution.py:225
  24.9 37.6 %copy-start.4 = (f32[672,128]{1,0:T(8,128)}, f32[672,128]{1,0:T(8,128)S(1)}, u32[]{:S(2)}) copy-start(f32[672,128]{1,0:T(8,128)S(1)} %collective-permute-done.12.refs_5_) | copy-start | bytes 1032196
  24.9 28.0 %collective-permute-start = (f32[672,128]{1,0:T(8,128)S(1)}, f32[672,128]{1,0:T(8,128)S(1)}, u32[]{:S(2)}, u32[]{:S(2)}) collective-permute-start(f32[672,128]{1,0:T(8,128)S(1)} %get-tuple-element.36), channel_id=1, source_target_pairs={{0,80},{16,64},{32,112},{48,96},{64,16},{80,0},{96,48},{112,32},{1... | collective-permute-start | bytes 1032200 | tf_op jit(solution)/shard_map/ppermute | solution.py:225
  30.0 32.5 %copy-start.6 = (f32[672,128]{1,0:T(8,128)}, f32[672,128]{1,0:T(8,128)S(1)}, u32[]{:S(2)}) copy-start(f32[672,128]{1,0:T(8,128)S(1)} %collective-permute-done.13.refs_6_) | copy-start | bytes 1032196
  30.0 25.0 %collective-permute-start.1 = (f32[672,128]{1,0:T(8,128)S(1)}, f32[672,128]{1,0:T(8,128)S(1)}, u32[]{:S(2)}, u32[]{:S(2)}) collective-permute-start(f32[672,128]{1,0:T(8,128)S(1)} %get-tuple-element.35), channel_id=1, source_target_pairs={{0,64},{16,80},{32,96},{48,112},{64,0},{80,16},{96,32},{112,48},{1... | collective-permute-start | bytes 1032200 | tf_op jit(solution)/shard_map/ppermute | solution.py:225
  33.2 21.9 %copy-start.7 = (f32[672,128]{1,0:T(8,128)}, f32[672,128]{1,0:T(8,128)S(1)}, u32[]{:S(2)}) copy-start(f32[672,128]{1,0:T(8,128)S(1)} %collective-permute-done.7.refs_0_) | copy-start | bytes 1032196
  33.2 35.4 %collective-permute-start.2 = (f32[672,128]{1,0:T(8,128)S(1)}, f32[672,128]{1,0:T(8,128)}, u32[]{:S(2)}, u32[]{:S(2)}) collective-permute-start(f32[672,128]{1,0:T(8,128)S(1)} %get-tuple-element.34), channel_id=1, source_target_pairs={{0,48},{16,32},{32,80},{48,64},{64,112},{80,96},{96,16},{112,0},{1... | collective-permute-start | bytes 1032200 | tf_op jit(solution)/shard_map/ppermute | solution.py:225
  34.8 20.3 %copy-start.9 = (f32[672,128]{1,0:T(8,128)}, f32[672,128]{1,0:T(8,128)S(1)}, u32[]{:S(2)}) copy-start(f32[672,128]{1,0:T(8,128)S(1)} %collective-permute-done.8.refs_1_) | copy-start | bytes 1032196
  34.8 34.7 %collective-permute-start.3 = (f32[672,128]{1,0:T(8,128)S(1)}, f32[672,128]{1,0:T(8,128)}, u32[]{:S(2)}, u32[]{:S(2)}) collective-permute-start(f32[672,128]{1,0:T(8,128)S(1)} %get-tuple-element.33), channel_id=1, source_target_pairs={{0,32},{16,48},{32,64},{48,80},{64,96},{80,112},{96,0},{112,16},{1... | collective-permute-start | bytes 1032200 | tf_op jit(solution)/shard_map/ppermute | solution.py:225
  41.5 13.5 %copy-start.10 = (f32[672,128]{1,0:T(8,128)}, f32[672,128]{1,0:T(8,128)S(1)}, u32[]{:S(2)}) copy-start(f32[672,128]{1,0:T(8,128)S(1)} %collective-permute-done.9.refs_2_) | copy-start | bytes 1032196
  41.6 27.9 %collective-permute-start.4 = (f32[672,128]{1,0:T(8,128)S(1)}, f32[672,128]{1,0:T(8,128)}, u32[]{:S(2)}, u32[]{:S(2)}) collective-permute-start(f32[672,128]{1,0:T(8,128)S(1)} %get-tuple-element.32), channel_id=1, source_target_pairs={{0,112},{16,96},{32,16},{48,0},{64,48},{80,32},{96,80},{112,64},{1... | collective-permute-start | bytes 1032200 | tf_op jit(solution)/shard_map/ppermute | solution.py:225
  53.0 15.6 %copy-start.5 = (f32[672,128]{1,0:T(8,128)}, f32[672,128]{1,0:T(8,128)S(1)}, u32[]{:S(2)}) copy-start(f32[672,128]{1,0:T(8,128)S(1)} %collective-permute-done.refs_0_) | copy-start | bytes 1032196
  53.0 17.1 %collective-permute-start.5 = (f32[672,128]{1,0:T(8,128)S(1)}, f32[672,128]{1,0:T(8,128)}, u32[]{:S(2)}, u32[]{:S(2)}) collective-permute-start(f32[672,128]{1,0:T(8,128)S(1)} %get-tuple-element.31), channel_id=1, source_target_pairs={{0,96},{16,112},{32,0},{48,16},{64,32},{80,48},{96,64},{112,80},{1... | collective-permute-start | bytes 1032200 | tf_op jit(solution)/shard_map/ppermute | solution.py:225
  55.1 0.8 copy-start.8
  55.8 14.2 %collective-permute-start.6 = (f32[672,128]{1,0:T(8,128)S(1)}, f32[672,128]{1,0:T(8,128)}, u32[]{:S(2)}, u32[]{:S(2)}) collective-permute-start(f32[672,128]{1,0:T(8,128)S(1)} %get-tuple-element.30), channel_id=1, source_target_pairs={{0,16},{16,0},{32,48},{48,32},{64,80},{80,64},{96,112},{112,96},{1... | collective-permute-start | bytes 1032200 | tf_op jit(solution)/shard_map/ppermute | solution.py:225
  76.7 2.2 %collective-permute-start.14 = (f32[1024,128]{1,0:T(8,128)}, f32[1024,128]{1,0:T(8,128)S(1)}, u32[]{:S(2)}, u32[]{:S(2)}) collective-permute-start(f32[1024,128]{1,0:T(8,128)} %get-tuple-element.15), channel_id=1, source_target_pairs={{0,16},{16,0},{32,48},{48,32},{64,80},{80,64},{96,112},{112,96},{1... | collective-permute-start | bytes 1572872 | tf_op jit(solution)/shard_map/ppermute | solution.py:41
  117.8 4.7 %copy-start = (f32[64,16,128]{2,1,0:T(8,128)}, f32[64,16,128]{2,1,0:T(8,128)S(1)}, u32[]{:S(2)}) copy-start(f32[64,16,128]{2,1,0:T(8,128)S(1)} %all_to_all.11) | copy-start | bytes 1572868
  117.8 4.7 %collective-permute-start.15 = (f32[1024,128]{1,0:T(8,128)S(1)}, f32[1024,128]{1,0:T(8,128)S(1)}, u32[]{:S(2)}, u32[]{:S(2)}) collective-permute-start(f32[1024,128]{1,0:T(8,128)S(1)} %bitcast.54), channel_id=1, source_target_pairs={{0,16},{16,0},{32,48},{48,32},{64,80},{80,64},{96,112},{112,96},{1... | collective-permute-start | bytes 1572872 | tf_op jit(solution)/shard_map/ppermute | solution.py:48
  122.5 0.8 copy-start.1
  145.3 2.0 %collective-permute-start.16 = (f32[2,8,64,96]{3,2,1,0:T(8,128)S(1)}, f32[2,8,64,96]{3,2,1,0:T(8,128)S(1)}, u32[]{:S(2)}, u32[]{:S(2)}) collective-permute-start(f32[2,8,64,96]{3,2,1,0:T(8,128)S(1)} %get-tuple-element.39), channel_id=1, source_target_pairs={{0,16},{16,0},{32,48},{48,32},{64,80},{80,64},{96,112},{112,96},{1... | collective-permute-start | bytes 1179656 | tf_op jit(solution)/shard_map/ppermute | solution.py:234

commit v3 on v2

--- a/solution.py
+++ b/solution.py
@@ -7,7 +7,7 @@
 
 X, R = 672, 96
 ROWS = 84
-BLOCK = 8
+BLOCK = 16
 HALF = 1024
 F32, BF16 = jnp.float32, jnp.bfloat16
 NN = (((1,), (0,)), ((), ()))
@@ -24,6 +24,19 @@
 def dot3(a, b, dims):
     d = lambda p, q: lax.dot_general(p, q, dims, preferred_element_type=F32)
     return d(a[0], b[0]) + (d(a[0], b[1]) + d(a[1], b[0]))
+
+
+def dot_thin(a, b):
+    def parts(v):
+        first = v.astype(BF16)
+        v = v - first.astype(F32)
+        second = v.astype(BF16)
+        return first, second, (v - second.astype(F32)).astype(BF16)
+
+    p, q = parts(a), parts(b)
+    left = jnp.concatenate([p[0], p[0], p[1], p[0], p[1], p[2]], axis=0)
+    right = jnp.concatenate([q[0], q[1], q[0], q[2], q[1], q[0]], axis=0)
+    return lax.dot_general(left, right, (((0,), (0,)), ((), ())), preferred_element_type=F32)
 
 
 def dot_full(a, b, dims):
@@ -49,9 +62,9 @@
 
 
 def gram_kernel(pos, *refs):
-    n = len(refs) - 8 - 6
+    n = len(refs) - 8 - 8
     blocks, before = refs[:8], refs[8 : 8 + n]
-    hi, lo, mine, other, cells, sems = refs[8 + n : 8 + n + 6]
+    hi_out, lo_out, mine, other, cells, hi, lo, sems = refs[8 + n :]
     packed = cells.at[pl.ds(0, 2 * HALF)]
     for i in range(8):
         pltpu.make_async_copy(blocks[i], cells.at[pl.ds(pos[2 + i] * 672, 672)], sems.at[i]).start()
@@ -61,6 +74,9 @@
         a = split(cells[pl.ds(q, X, stride=8), :])
         hi[:, 128 * q : 128 * q + 128] = a[0]
         lo[:, 128 * q : 128 * q + 128] = a[1]
+    outward = [pltpu.make_async_copy(hi, hi_out, sems.at[8]), pltpu.make_async_copy(lo, lo_out, sems.at[9])]
+    for copy in outward:
+        copy.start()
     for j in range(3):
         low, high = 256 * j, min(256 * j + 256, X)
         g = dot3((hi[low:, :], lo[low:, :]), (hi[low:high, :], lo[low:high, :]), NT)
@@ -80,10 +96,12 @@
         if n:
             value = value + before[k][...]
         out[...] = value
+    for copy in outward:
+        copy.wait()
 
 
 def gram(pos, blocks, before):
-    any_spec = pl.BlockSpec(memory_space=pl.ANY)
+    hbm = pl.BlockSpec(memory_space=pltpu.HBM)
     vmem = pl.BlockSpec(memory_space=pltpu.VMEM)
     return pl.pallas_call(
         gram_kernel,
@@ -93,9 +111,14 @@
             jax.ShapeDtypeStruct((HALF, 128), F32),
             jax.ShapeDtypeStruct((HALF, 128), F32),
         ),
-        in_specs=[pl.BlockSpec(memory_space=pltpu.SMEM)] + [any_spec] * 8 + [vmem] * len(before),
-        out_specs=(vmem,) * 4,
-        scratch_shapes=[pltpu.VMEM((X * 8, 128), F32), pltpu.SemaphoreType.DMA((8,))],
+        in_specs=[pl.BlockSpec(memory_space=pltpu.SMEM)] + [hbm] * 8 + [vmem] * len(before),
+        out_specs=(hbm, hbm, vmem, vmem),
+        scratch_shapes=[
+            pltpu.VMEM((X * 8, 128), F32),
+            pltpu.VMEM((X, 1024), BF16),
+            pltpu.VMEM((X, 1024), BF16),
+            pltpu.SemaphoreType.DMA((10,)),
+        ],
         compiler_params=pltpu.CompilerParams(vmem_limit_bytes=VMEM_LIMIT),
         cost_estimate=pl.CostEstimate(flops=3 * 2 * X * X * 1024, bytes_accessed=6 * 2**20, transcendentals=0),
     )(pos, *blocks, *before)
@@ -158,7 +181,7 @@
             rows = jnp.concatenate(
                 [jnp.concatenate(left, axis=0), jnp.concatenate(right, axis=0)], axis=1
             )
-            step = dot_full(jnp.concatenate(scaled, axis=0).T, rows, NN)
+            step = dot_thin(jnp.concatenate(scaled, axis=0), rows)
             work[at + BLOCK :, :] = work[at + BLOCK :, :] - step[at + BLOCK : R]
 
 
@@ -182,16 +205,18 @@
     for k in range(2):
         for y in range(8):
             part = a[2 * k, :, 128 * y : 128 * y + 128], a[2 * k + 1, :, 128 * y : 128 * y + 128]
-            core[k, y] = dot3(f, part, NN).T
+            value = dot3(f, part, NN).T
+            core[2 * k, y] = value[:64]
+            core[2 * k + 1, y] = value[64:]
 
 
 def finish(pos, mine, other, basis_t, fibers):
-    any_spec = pl.BlockSpec(memory_space=pl.ANY)
+    hbm = pl.BlockSpec(memory_space=pltpu.HBM)
     vmem = pl.BlockSpec(memory_space=pltpu.VMEM)
     return pl.pallas_call(
         finish_kernel,
-        out_shape=(jax.ShapeDtypeStruct((R, X), F32), jax.ShapeDtypeStruct((2, 8, 128, R), F32)),
-        in_specs=[pl.BlockSpec(memory_space=pltpu.SMEM)] + [vmem] * 3 + [any_spec] * 4,
+        out_shape=(jax.ShapeDtypeStruct((R, X), F32), jax.ShapeDtypeStruct((4, 8, 64, R), F32)),
+        in_specs=[pl.BlockSpec(memory_space=pltpu.SMEM)] + [vmem] * 3 + [hbm] * 4,
         out_specs=(vmem, vmem),
         scratch_shapes=[
             pltpu.VMEM((2 * HALF, 128), F32),
@@ -206,10 +231,37 @@
     )(pos, mine, other, basis_t, *fibers)
 
 
+def pack_kernel(pos, species, same, across):
+    rows = same.shape[0]
+    a, b = species[0].reshape(rows, 128), species[1].reshape(rows, 128)
+    first = lax.broadcasted_iota(jnp.int32, (rows, 128), 1) < 64
+    low = jnp.where(first, a, pltpu.roll(b, 64, 1))
+    high = jnp.where(first, pltpu.roll(a, 64, 1), b)
+    even = pos[0] == 0
+    same[...] = jnp.where(even, low, high)
+    across[...] = jnp.where(even, high, low)
+
+
+def pack(core_and_tile, tensor, k):
+    rows = ROWS // 2
+    out = pl.BlockSpec((rows * 8, 128), lambda i, pos: (i, 0))
+    return pl.pallas_call(
+        pack_kernel,
+        grid_spec=pltpu.PrefetchScalarGridSpec(
+            num_scalar_prefetch=1,
+            grid=(2,),
+            in_specs=[pl.BlockSpec((2, rows, 8, 128), lambda i, pos: (k, i, 0, pos[1]))],
+            out_specs=(out, out),
+        ),
+        out_shape=(jax.ShapeDtypeStruct((ROWS * 8, 128), F32),) * 2,
+        cost_estimate=pl.CostEstimate(flops=2**20, bytes_accessed=2**20, transcendentals=0),
+    )(core_and_tile, tensor)
+
+
 def per_device(tensor, start_basis):
     me = lax.axis_index("gx")
     y, c = me // 2, me % 2
-    offsets = [(dy, dc) for dy in (2, 1, 3, 0) for dc in (1, 0)]
+    offsets = [(dy, dc) for dy in (1, 3, 2, 0) for dc in (1, 0)]
     sources = [2 * ((y - dy) % 4) + (c ^ dc) for dy, dc in offsets]
     pos = jnp.stack([y, c] + sources).astype(jnp.int32)
     basis_t = start_basis.T
@@ -217,23 +269,19 @@
     fibers, halves = [], ()
     for k in range(2):
         blocks = []
-        for dy, dc in offsets:
-            block = lax.dynamic_slice(
-                tensor, (2 * (c ^ dc) + k, 0, 0, 128 * ((y + dy) % 4)), (1, ROWS, 8, 128)
-            ).reshape(ROWS * 8, 128)
-            if dy or dc:
-                block = lax.ppermute(block, "gx", perm_gx(dy, dc))
-            blocks.append(block)
+        for dy in (1, 3, 2, 0):
+            where = jnp.stack([c, (y + dy) % 4]).astype(jnp.int32)
+            if k:
+                where, _ = lax.optimization_barrier((where, earlier))
+            same, across = pack(where, tensor, k)
+            blocks.append(lax.ppermute(across, "gx", perm_gx(dy, 1)))
+            blocks.append(lax.ppermute(same, "gx", perm_gx(dy, 0)) if dy else same)
+        earlier = blocks[6]
         hi, lo, *halves = gram(pos, blocks, halves)
         fibers += [hi, lo]
 
     factor_t, core = finish(pos, *total_over_devices(*halves), basis_t, fibers)
-
-    halves = core.reshape(2, 8, 2, 64, R)
-    mine = lax.dynamic_index_in_dim(halves, c, 2, keepdims=False)
-    theirs = lax.ppermute(lax.dynamic_index_in_dim(halves, 1 - c, 2, keepdims=False), "gx", perm_gx(0, 1))
-    out = jnp.where(c == 0, jnp.concatenate([mine, theirs]), jnp.concatenate([theirs, mine]))
-    return factor_t.T, out.transpose(0, 3, 1, 2)
+    return factor_t.T, core.transpose(0, 3, 1, 2)
 
 
 def solution(mesh):

time: 149 us -> 153 us (1.027)
  Pallas kernels: 33.4 us -> 50.3 us
  waiting for transfers between devices: 26.2 us -> 14.5 us
  blocking collectives: 37.6 us -> 47.7 us
  starting transfers between devices: 40.6 us -> 34 us
  local copies, waits for them, and re-layouts: 7.48 us -> 1.6 us
    pallas_call x0 -> x8, Pallas kernels: none -> 22.1 us  [pack(): pl.pallas_call(pack_kernel, grid_spec=pltpu.PrefetchScalarGridSpec(num_sc...]
    ppermute x15 -> x14, waiting for transfers between devices: 22.5 us -> 11.2 us  [the longest x6 11.1 us: per_device(): blocks.append(lax.ppermute(same, 'gx', perm_gx(dy, 0)) if dy else same)]
    all_to_all x1, blocking collectives: 22.1 us -> 32.2 us  [total_over_devices(): lax.all_to_all(half.reshape(64, 16, 128), both, 0, 0, axis_index_groups=S...]
    ppermute x15 -> x14, starting transfers between devices: 37.3 us -> 29.6 us  [the longest x6 18.5 us: per_device(): blocks.append(lax.ppermute(same, 'gx', perm_gx(dy, 0)) if dy else same)]
    pallas_call x1, Pallas kernels: 20.7 us -> 15.1 us  [finish(): pl.pallas_call(finish_kernel, out_shape=(jax.ShapeDtypeStruct((R, X), F32...]
    reshape x1 -> x0, local copies, waits for them, and re-layouts: 3.9 us -> none  [per_device(): block = lax.dynamic_slice(tensor, (2 * (c ^ dc) + k, 0, 0, 128 * ((y + dy...]
    another operation x0 -> x3, other arithmetic: none -> 1.85 us  [per_device(): where = jnp.stack([c, (y + dy) % 4]).astype(jnp.int32)]
  transfers between devices with their start and end apart: 17 -> 16, of which waited for: 9 -> 6; matrix products, arithmetic and copies ran while one was open for 0% -> 1% of each run, Pallas kernels for 4% -> 17%
where the time goes in v3:
time: 153 us; the launch traced here: 152 us
  Pallas kernels  50.3 us (33%)
  blocking collectives  47.7 us (31%)
  starting transfers between devices  34 us (22%)
  waiting for transfers between devices  14.5 us (9%)
  other arithmetic  3.04 us (2%)
  local copies, waits for them, and re-layouts  1.6 us (1%)
    all_to_all x1, blocking collectives, total_over_devices(): lax.all_to_all(half.reshape(64, 16, 128), both, 0, 0, axis_index_groups=S...  32.2 us
    pallas_call x8, Pallas kernels, pack(): pl.pallas_call(pack_kernel, grid_spec=pltpu.PrefetchScalarGridSpec(num_sc...  22.1 us
    ppermute x6, starting transfers between devices, per_device(): blocks.append(lax.ppermute(same, 'gx', perm_gx(dy, 0)) if dy else same)  18.5 us
    all_to_all x1, blocking collectives, total_over_devices(): lax.all_to_all(jnp.broadcast_to(piece[None], (64, 16, 128)), both, 0, 0,...  15.5 us
    pallas_call x1, Pallas kernels, finish(): pl.pallas_call(finish_kernel, out_shape=(jax.ShapeDtypeStruct((R, X), F32...  15.1 us
    pallas_call x2, Pallas kernels, gram(): pl.pallas_call(gram_kernel, out_shape=(jax.ShapeDtypeStruct((X, 1024), BF...  13.1 us
    ppermute x6, waiting for transfers between devices, per_device(): blocks.append(lax.ppermute(same, 'gx', perm_gx(dy, 0)) if dy else same)  11.1 us
    ppermute x8, starting transfers between devices, per_device(): blocks.append(lax.ppermute(across, 'gx', perm_gx(dy, 1)))  11 us
  transfers between devices with their start and end apart: 16, of which 6 were waited for; matrix products, arithmetic and copies ran while one was open for 1% of the time, Pallas kernels for 17%

profile of v3, /device:TPU:1, one launch (start us, length us, event | category | flops | bytes accessed | tf_op | source)
XLA Modules:
  0.0 152.1 jit_solution(2228760250556352579)
XLA Ops:
  1.3 2.7 %shard_map.41 = (f32[672,128]{1,0:T(8,128)}, f32[672,128]{1,0:T(8,128)}) custom-call(s32[2]{0:T(128)} %pad_add_fusion.1.pos, f32[4,84,8,512]{3,2,1,0:T(8,128)} %species.15), custom_call_target="tpu_custom_call" | custom-call | flops 1048576 | bytes 1048576 | tf_op jit(solution)/shard_map/pallas_call | solution.py:248
  4.0 1.4 collective-permute-start
  6.1 2.8 %shard_map.46 = (f32[672,128]{1,0:T(8,128)}, f32[672,128]{1,0:T(8,128)}) custom-call(s32[2]{0:T(128)} %get-tuple-element.33.pos, f32[4,84,8,512]{3,2,1,0:T(8,128)} %species.15), custom_call_target="tpu_custom_call" | custom-call | flops 1048576 | bytes 1048576 | tf_op jit(solution)/shard_map/pallas_call | solution.py:248
  8.8 1.3 collective-permute-start.8
  10.1 1.3 collective-permute-start.9
  11.4 2.8 %shard_map.47 = (f32[672,128]{1,0:T(8,128)}, f32[672,128]{1,0:T(8,128)}) custom-call(s32[2]{0:T(128)} %get-tuple-element.36.pos, f32[4,84,8,512]{3,2,1,0:T(8,128)} %species.15), custom_call_target="tpu_custom_call" | custom-call | flops 1048576 | bytes 1048576 | tf_op jit(solution)/shard_map/pallas_call | solution.py:248
  14.2 2.1 %collective-permute-start.10 = (f32[672,128]{1,0:T(8,128)}, f32[672,128]{1,0:T(8,128)S(1)}, u32[]{:S(2)}, u32[]{:S(2)}) collective-permute-start(f32[672,128]{1,0:T(8,128)} %get-tuple-element.47), channel_id=1, source_target_pairs={{0,112},{16,96},{32,16},{48,0},{64,48},{80,32},{96,80},{112,64},{1... | collective-permute-start | bytes 1032200 | tf_op jit(solution)/shard_map/ppermute | solution.py:277
  16.9 2.7 %shard_map.48 = (f32[672,128]{1,0:T(8,128)}, f32[672,128]{1,0:T(8,128)}) custom-call(s32[2]{0:T(128)} %pad_add_fusion.3.pos, f32[4,84,8,512]{3,2,1,0:T(8,128)} %species.15), custom_call_target="tpu_custom_call" | custom-call | flops 1048576 | bytes 1048576 | tf_op jit(solution)/shard_map/pallas_call | solution.py:248
  19.6 1.8 %collective-permute-start.12 = (f32[672,128]{1,0:T(8,128)}, f32[672,128]{1,0:T(8,128)S(1)}, u32[]{:S(2)}, u32[]{:S(2)}) collective-permute-start(f32[672,128]{1,0:T(8,128)} %get-tuple-element.49), channel_id=1, source_target_pairs={{0,80},{16,64},{32,112},{48,96},{64,16},{80,0},{96,48},{112,32},{1... | collective-permute-start | bytes 1032200 | tf_op jit(solution)/shard_map/ppermute | solution.py:277
  21.4 2.7 %shard_map.42 = (f32[672,128]{1,0:T(8,128)}, f32[672,128]{1,0:T(8,128)}) custom-call(s32[2]{0:T(128)} %get-tuple-element.33.pos, f32[4,84,8,512]{3,2,1,0:T(8,128)} %species.15), custom_call_target="tpu_custom_call" | custom-call | flops 1048576 | bytes 1048576 | tf_op jit(solution)/shard_map/pallas_call | solution.py:248
  24.1 1.6 %collective-permute-start.13 = (f32[672,128]{1,0:T(8,128)}, f32[672,128]{1,0:T(8,128)S(1)}, u32[]{:S(2)}, u32[]{:S(2)}) collective-permute-start(f32[672,128]{1,0:T(8,128)} %get-tuple-element.50), channel_id=1, source_target_pairs={{0,64},{16,80},{32,96},{48,112},{64,0},{80,16},{96,32},{112,48},{1... | collective-permute-start | bytes 1032200 | tf_op jit(solution)/shard_map/ppermute | solution.py:278
  25.7 1.8 %collective-permute-done.9.refs_1_ = f32[672,128]{1,0:T(8,128)S(1)} collective-permute-done((f32[672,128]{1,0:T(8,128)}, f32[672,128]{1,0:T(8,128)S(1)}, u32[]{:S(2)}, u32[]{:S(2)}) %collective-permute-start.9) | collective-permute-done | bytes 344096 | tf_op jit(solution)/shard_map/ppermute | solution.py:278
  27.5 1.2 collective-permute-start.1
  28.7 14.8 %collective-permute-start.2 = (f32[672,128]{1,0:T(8,128)}, f32[672,128]{1,0:T(8,128)S(1)}, u32[]{:S(2)}, u32[]{:S(2)}) collective-permute-start(f32[672,128]{1,0:T(8,128)} %get-tuple-element.35), channel_id=1, source_target_pairs={{0,32},{16,48},{32,64},{48,80},{64,96},{80,112},{96,0},{112,16},{1... | collective-permute-start | bytes 1032200 | tf_op jit(solution)/shard_map/ppermute | solution.py:278
  43.5 2.7 %shard_map.43 = (f32[672,128]{1,0:T(8,128)}, f32[672,128]{1,0:T(8,128)}) custom-call(s32[2]{0:T(128)} %get-tuple-element.36.pos, f32[4,84,8,512]{3,2,1,0:T(8,128)} %species.15), custom_call_target="tpu_custom_call" | custom-call | flops 1048576 | bytes 1048576 | tf_op jit(solution)/shard_map/pallas_call | solution.py:248
  46.2 2.7 %shard_map.45 = (f32[672,128]{1,0:T(8,128)}, f32[672,128]{1,0:T(8,128)}) custom-call(s32[2]{0:T(128)} %pad_add_fusion.1.pos, f32[4,84,8,512]{3,2,1,0:T(8,128)} %species.15), custom_call_target="tpu_custom_call" | custom-call | flops 1048576 | bytes 1048576 | tf_op jit(solution)/shard_map/pallas_call | solution.py:248
  49.0 2.9 %shard_map.44 = (f32[672,128]{1,0:T(8,128)}, f32[672,128]{1,0:T(8,128)}) custom-call(s32[2]{0:T(128)} %pad_add_fusion.3.pos, f32[4,84,8,512]{3,2,1,0:T(8,128)} %species.15), custom_call_target="tpu_custom_call" | custom-call | flops 1048576 | bytes 1048576 | tf_op jit(solution)/shard_map/pallas_call | solution.py:248
  52.0 0.7 collective-permute-start.4
  52.9 3.2 %collective-permute-start.5 = (f32[672,128]{1,0:T(8,128)}, f32[672,128]{1,0:T(8,128)}, u32[]{:S(2)}, u32[]{:S(2)}) collective-permute-start(f32[672,128]{1,0:T(8,128)} %get-tuple-element.40), channel_id=1, source_target_pairs={{0,80},{16,64},{32,112},{48,96},{64,16},{80,0},{96,48},{112,32},{1... | collective-permute-start | bytes 1032200 | tf_op jit(solution)/shard_map/ppermute | solution.py:277
  56.1 3.2 %collective-permute-done.2.refs_1_ = f32[672,128]{1,0:T(8,128)S(1)} collective-permute-done((f32[672,128]{1,0:T(8,128)}, f32[672,128]{1,0:T(8,128)S(1)}, u32[]{:S(2)}, u32[]{:S(2)}) %collective-permute-start.2) | collective-permute-done | bytes 344096 | tf_op jit(solution)/shard_map/ppermute | solution.py:278
  59.9 6.3 %shard_map.49 = (bf16[672,1024]{1,0:T(8,128)(2,1)}, bf16[672,1024]{1,0:T(8,128)(2,1)}, f32[1024,128]{1,0:T(8,128)}, f32[1024,128]{1,0:T(8,128)}) custom-call(s32[10]{0:T(128)} %stack.83.pos, f32[672,128]{1,0:T(8,128)} %copy-done.3, f32[672,128]{1,0:T(8,128)} %copy-done.4, f32[672,128]{1,0:T(8,128)} %copy-done.5, f32[672,128]{1,0:T(8,128)} %copy-done.6, ...), custom_call_target="tpu_custom_call" | custom-call | flops 2774532096 | bytes 6291456 | tf_op jit(solution)/shard_map/pallas_call | solution.py:106
  66.4 6.2 %collective-permute-done.6.refs_5_ = f32[672,128]{1,0:T(8,128)} collective-permute-done((f32[672,128]{1,0:T(8,128)}, f32[672,128]{1,0:T(8,128)}, u32[]{:S(2)}, u32[]{:S(2)}) %collective-permute-start.6) | collective-permute-done | bytes 344096 | tf_op jit(solution)/shard_map/ppermute | solution.py:278
  72.6 6.8 %shard_map.50 = (bf16[672,1024]{1,0:T(8,128)(2,1)}, bf16[672,1024]{1,0:T(8,128)(2,1)}, f32[1024,128]{1,0:T(8,128)}, f32[1024,128]{1,0:T(8,128)}) custom-call(s32[10]{0:T(128)} %stack.83.pos, f32[672,128]{1,0:T(8,128)} %copy-done.7, f32[672,128]{1,0:T(8,128)} %copy-done.9, f32[672,128]{1,0:T(8,128)} %copy-done.11, f32[672,128]{1,0:T(8,128)} %copy-done.14, ...), custom_call_target="tpu_custom_call" | custom-call | flops 2774532096 | bytes 6291456 | tf_op jit(solution)/shard_map/pallas_call | solution.py:106
  79.4 1.2 collective-permute-start.14
  80.6 1.7 %collective-permute-done.14 = f32[1024,128]{1,0:T(8,128)S(1)} collective-permute-done((f32[1024,128]{1,0:T(8,128)}, f32[1024,128]{1,0:T(8,128)S(1)}, u32[]{:S(2)}, u32[]{:S(2)}) %collective-permute-start.14) | collective-permute-done | bytes 524320 | tf_op jit(solution)/shard_map/ppermute | solution.py:54
  82.4 1.1 add.96
  83.5 32.2 %all_to_all.10 = f32[64,16,128]{2,1,0:T(8,128)S(1)} all-to-all(f32[64,16,128]{2,1,0:T(8,128)S(1)} %bitcast.19), channel_id=1, replica_groups={{0,1,2,3,4,5,6,7,8,9,10,11,12,13,14,15,32,33,34,35,36,37,38,39,40,41,42..., dimensions={0} | all-to-all | bytes 1048576 | tf_op jit(solution)/shard_map/all_to_all | solution.py:56
  115.8 15.5 %all_to_all.11 = f32[64,16,128]{2,1,0:T(8,128)S(1)} all-to-all(f32[64,16,128]{2,1,0:T(8,128)S(1)} %broadcast_in_dim.2), channel_id=1, replica_groups={{0,1,2,3,4,5,6,7,8,9,10,11,12,13,14,15,32,33,34,35,36,37,38,39,40,41,42..., dimensions={0} | all-to-all | bytes 1048576 | tf_op jit(solution)/shard_map/all_to_all | solution.py:58
  131.3 3.2 %collective-permute-start.15 = (f32[1024,128]{1,0:T(8,128)S(1)}, f32[1024,128]{1,0:T(8,128)S(1)}, u32[]{:S(2)}, u32[]{:S(2)}) collective-permute-start(f32[1024,128]{1,0:T(8,128)S(1)} %bitcast.20), channel_id=1, source_target_pairs={{0,16},{16,0},{32,48},{48,32},{64,80},{80,64},{96,112},{112,96},{1... | collective-permute-start | bytes 1572872 | tf_op jit(solution)/shard_map/ppermute | solution.py:61
  134.5 1.5 %collective-permute-done.15.other = f32[1024,128]{1,0:T(8,128)S(1)} collective-permute-done((f32[1024,128]{1,0:T(8,128)S(1)}, f32[1024,128]{1,0:T(8,128)S(1)}, u32[]{:S(2)}, u32[]{:S(2)}) %collective-permute-start.15) | collective-permute-done | bytes 524320 | tf_op jit(solution)/shard_map/ppermute | solution.py:61
  136.1 0.8 copy-done.1
  136.9 15.1 %shard_map.51 = (f32[96,672]{1,0:T(8,128)}, f32[4,8,64,96]{3,2,1,0:T(8,128)}) custom-call(s32[10]{0:T(128)} %stack.83.pos, f32[1024,128]{1,0:T(8,128)} %bitcast.21, f32[1024,128]{1,0:T(8,128)} %copy-done.1, f32[96,672]{1,0:T(8,128)} %bitcast.22, bf16[672,1024]{1,0:T(8,128)(2,1)} %get-tuple-element.56.hi0, bf16[672,1024]{1,0:T(8,128)(2,1)} %get-tuple-element.57.lo0, ...), custom_call_target="tpu_custom_call" | custom-call | flops 792723456 | bytes 7340032 | tf_op jit(solution)/shard_map/pallas_call | solution.py:216
  (52 shorter events, 3.1 us)
Async XLA Ops:
  4.0 15.6 %collective-permute-start = (f32[672,128]{1,0:T(8,128)}, f32[672,128]{1,0:T(8,128)S(1)}, u32[]{:S(2)}, u32[]{:S(2)}) collective-permute-start(f32[672,128]{1,0:T(8,128)} %get-tuple-element.32), channel_id=1, source_target_pairs={{0,16},{16,0},{32,48},{48,32},{64,80},{80,64},{96,112},{112,96},{1... | collective-permute-start | bytes 1032200 | tf_op jit(solution)/shard_map/ppermute | solution.py:277
  8.8 15.3 %collective-permute-start.8 = (f32[672,128]{1,0:T(8,128)}, f32[672,128]{1,0:T(8,128)S(1)}, u32[]{:S(2)}, u32[]{:S(2)}) collective-permute-start(f32[672,128]{1,0:T(8,128)} %get-tuple-element.45), channel_id=1, source_target_pairs={{0,48},{16,32},{32,80},{48,64},{64,112},{80,96},{96,16},{112,0},{1... | collective-permute-start | bytes 1032200 | tf_op jit(solution)/shard_map/ppermute | solution.py:277
  10.1 17.4 %collective-permute-start.9 = (f32[672,128]{1,0:T(8,128)}, f32[672,128]{1,0:T(8,128)S(1)}, u32[]{:S(2)}, u32[]{:S(2)}) collective-permute-start(f32[672,128]{1,0:T(8,128)} %get-tuple-element.46), channel_id=1, source_target_pairs={{0,32},{16,48},{32,64},{48,80},{64,96},{80,112},{96,0},{112,16},{1... | collective-permute-start | bytes 1032200 | tf_op jit(solution)/shard_map/ppermute | solution.py:278
  14.2 14.5 %collective-permute-start.10 = (f32[672,128]{1,0:T(8,128)}, f32[672,128]{1,0:T(8,128)S(1)}, u32[]{:S(2)}, u32[]{:S(2)}) collective-permute-start(f32[672,128]{1,0:T(8,128)} %get-tuple-element.47), channel_id=1, source_target_pairs={{0,112},{16,96},{32,16},{48,0},{64,48},{80,32},{96,80},{112,64},{1... | collective-permute-start | bytes 1032200 | tf_op jit(solution)/shard_map/ppermute | solution.py:277
  16.2 35.7 %collective-permute-start.11 = (f32[672,128]{1,0:T(8,128)}, f32[672,128]{1,0:T(8,128)S(1)}, u32[]{:S(2)}, u32[]{:S(2)}) collective-permute-start(f32[672,128]{1,0:T(8,128)} %get-tuple-element.48), channel_id=1, source_target_pairs={{0,96},{16,112},{32,0},{48,16},{64,32},{80,48},{96,64},{112,80},{1... | collective-permute-start | bytes 1032200 | tf_op jit(solution)/shard_map/ppermute | solution.py:278
  19.6 4.5 %copy-start.2 = (f32[672,128]{1,0:T(8,128)}, f32[672,128]{1,0:T(8,128)S(1)}, u32[]{:S(2)}) copy-start(f32[672,128]{1,0:T(8,128)S(1)} %collective-permute-done.refs_6_) | copy-start | bytes 1032196
  19.6 32.4 %collective-permute-start.12 = (f32[672,128]{1,0:T(8,128)}, f32[672,128]{1,0:T(8,128)S(1)}, u32[]{:S(2)}, u32[]{:S(2)}) collective-permute-start(f32[672,128]{1,0:T(8,128)} %get-tuple-element.49), channel_id=1, source_target_pairs={{0,80},{16,64},{32,112},{48,96},{64,16},{80,0},{96,48},{112,32},{1... | collective-permute-start | bytes 1032200 | tf_op jit(solution)/shard_map/ppermute | solution.py:277
  24.1 22.1 %copy-start.3 = (f32[672,128]{1,0:T(8,128)}, f32[672,128]{1,0:T(8,128)S(1)}, u32[]{:S(2)}) copy-start(f32[672,128]{1,0:T(8,128)S(1)} %collective-permute-done.8.refs_0_) | copy-start | bytes 1032196
  24.1 28.6 %collective-permute-start.13 = (f32[672,128]{1,0:T(8,128)}, f32[672,128]{1,0:T(8,128)S(1)}, u32[]{:S(2)}, u32[]{:S(2)}) collective-permute-start(f32[672,128]{1,0:T(8,128)} %get-tuple-element.50), channel_id=1, source_target_pairs={{0,64},{16,80},{32,96},{48,112},{64,0},{80,16},{96,32},{112,48},{1... | collective-permute-start | bytes 1032200 | tf_op jit(solution)/shard_map/ppermute | solution.py:278
  27.5 18.7 %copy-start.4 = (f32[672,128]{1,0:T(8,128)}, f32[672,128]{1,0:T(8,128)S(1)}, u32[]{:S(2)}) copy-start(f32[672,128]{1,0:T(8,128)S(1)} %collective-permute-done.9.refs_1_) | copy-start | bytes 1032196
  27.5 25.3 %collective-permute-start.1 = (f32[672,128]{1,0:T(8,128)}, f32[672,128]{1,0:T(8,128)S(1)}, u32[]{:S(2)}, u32[]{:S(2)}) collective-permute-start(f32[672,128]{1,0:T(8,128)} %get-tuple-element.34), channel_id=1, source_target_pairs={{0,48},{16,32},{32,80},{48,64},{64,112},{80,96},{96,16},{112,0},{1... | collective-permute-start | bytes 1032200 | tf_op jit(solution)/shard_map/ppermute | solution.py:277
  28.7 17.5 %copy-start.5 = (f32[672,128]{1,0:T(8,128)}, f32[672,128]{1,0:T(8,128)S(1)}, u32[]{:S(2)}) copy-start(f32[672,128]{1,0:T(8,128)S(1)} %collective-permute-done.10.refs_2_) | copy-start | bytes 1032196
  28.7 30.5 %collective-permute-start.2 = (f32[672,128]{1,0:T(8,128)}, f32[672,128]{1,0:T(8,128)S(1)}, u32[]{:S(2)}, u32[]{:S(2)}) collective-permute-start(f32[672,128]{1,0:T(8,128)} %get-tuple-element.35), channel_id=1, source_target_pairs={{0,32},{16,48},{32,64},{48,80},{64,96},{80,112},{96,0},{112,16},{1... | collective-permute-start | bytes 1032200 | tf_op jit(solution)/shard_map/ppermute | solution.py:278
  49.0 2.9 %copy-start.15 = (f32[672,128]{1,0:T(8,128)S(1)}, f32[672,128]{1,0:T(8,128)}, u32[]{:S(2)}) copy-start(f32[672,128]{1,0:T(8,128)} %get-tuple-element.37) | copy-start | bytes 1032196
  49.0 3.0 %copy-start.13 = (f32[672,128]{1,0:T(8,128)S(1)}, f32[672,128]{1,0:T(8,128)}, u32[]{:S(2)}) copy-start(f32[672,128]{1,0:T(8,128)} %get-tuple-element.38) | copy-start | bytes 1032196
  49.0 3.8 %copy-start.12 = (f32[672,128]{1,0:T(8,128)S(1)}, f32[672,128]{1,0:T(8,128)}, u32[]{:S(2)}) copy-start(f32[672,128]{1,0:T(8,128)} %get-tuple-element.43) | copy-start | bytes 1032196
  51.9 8.0 %copy-start.6 = (f32[672,128]{1,0:T(8,128)}, f32[672,128]{1,0:T(8,128)S(1)}, u32[]{:S(2)}) copy-start(f32[672,128]{1,0:T(8,128)S(1)} %collective-permute-done.11.refs_3_) | copy-start | bytes 1032196
  51.9 14.3 %collective-permute-start.3 = (f32[672,128]{1,0:T(8,128)S(1)}, f32[672,128]{1,0:T(8,128)S(1)}, u32[]{:S(2)}, u32[]{:S(2)}) collective-permute-start(f32[672,128]{1,0:T(8,128)S(1)} %copy-done.15), channel_id=1, source_target_pairs={{0,112},{16,96},{32,16},{48,0},{64,48},{80,32},{96,80},{112,64},{1... | collective-permute-start | bytes 1032200 | tf_op jit(solution)/shard_map/ppermute | solution.py:277
  52.0 7.9 %copy-start.8 = (f32[672,128]{1,0:T(8,128)}, f32[672,128]{1,0:T(8,128)S(1)}, u32[]{:S(2)}) copy-start(f32[672,128]{1,0:T(8,128)S(1)} %collective-permute-done.12.refs_4_) | copy-start | bytes 1032196
  52.0 14.3 %collective-permute-start.4 = (f32[672,128]{1,0:T(8,128)S(1)}, f32[672,128]{1,0:T(8,128)S(1)}, u32[]{:S(2)}, u32[]{:S(2)}) collective-permute-start(f32[672,128]{1,0:T(8,128)S(1)} %copy-done.13), channel_id=1, source_target_pairs={{0,96},{16,112},{32,0},{48,16},{64,32},{80,48},{96,64},{112,80},{1... | collective-permute-start | bytes 1032200 | tf_op jit(solution)/shard_map/ppermute | solution.py:278
  52.7 7.2 %copy-start.10 = (f32[672,128]{1,0:T(8,128)}, f32[672,128]{1,0:T(8,128)S(1)}, u32[]{:S(2)}) copy-start(f32[672,128]{1,0:T(8,128)S(1)} %collective-permute-done.13.refs_5_) | copy-start | bytes 1032196
  52.8 13.5 %collective-permute-start.7 = (f32[672,128]{1,0:T(8,128)S(1)}, f32[672,128]{1,0:T(8,128)}, u32[]{:S(2)}, u32[]{:S(2)}) collective-permute-start(f32[672,128]{1,0:T(8,128)S(1)} %copy-done.12), channel_id=1, source_target_pairs={{0,16},{16,0},{32,48},{48,32},{64,80},{80,64},{96,112},{112,96},{1... | collective-permute-start | bytes 1032200 | tf_op jit(solution)/shard_map/ppermute | solution.py:277
  52.9 13.4 %copy-start.7 = (f32[672,128]{1,0:T(8,128)}, f32[672,128]{1,0:T(8,128)S(1)}, u32[]{:S(2)}) copy-start(f32[672,128]{1,0:T(8,128)S(1)} %collective-permute-done.1.refs_0_) | copy-start | bytes 1032196
  52.9 13.5 %collective-permute-start.5 = (f32[672,128]{1,0:T(8,128)}, f32[672,128]{1,0:T(8,128)}, u32[]{:S(2)}, u32[]{:S(2)}) collective-permute-start(f32[672,128]{1,0:T(8,128)} %get-tuple-element.40), channel_id=1, source_target_pairs={{0,80},{16,64},{32,112},{48,96},{64,16},{80,0},{96,48},{112,32},{1... | collective-permute-start | bytes 1032200 | tf_op jit(solution)/shard_map/ppermute | solution.py:277
  59.2 7.0 %copy-start.9 = (f32[672,128]{1,0:T(8,128)}, f32[672,128]{1,0:T(8,128)S(1)}, u32[]{:S(2)}) copy-start(f32[672,128]{1,0:T(8,128)S(1)} %collective-permute-done.2.refs_1_) | copy-start | bytes 1032196
  59.2 13.3 %collective-permute-start.6 = (f32[672,128]{1,0:T(8,128)}, f32[672,128]{1,0:T(8,128)}, u32[]{:S(2)}, u32[]{:S(2)}) collective-permute-start(f32[672,128]{1,0:T(8,128)} %get-tuple-element.41), channel_id=1, source_target_pairs={{0,64},{16,80},{32,96},{48,112},{64,0},{80,16},{96,32},{112,48},{1... | collective-permute-start | bytes 1032200 | tf_op jit(solution)/shard_map/ppermute | solution.py:278
  66.3 6.3 %copy-start.11 = (f32[672,128]{1,0:T(8,128)}, f32[672,128]{1,0:T(8,128)S(1)}, u32[]{:S(2)}) copy-start(f32[672,128]{1,0:T(8,128)S(1)} %collective-permute-done.3.refs_2_) | copy-start | bytes 1032196
  66.3 6.3 %copy-start.14 = (f32[672,128]{1,0:T(8,128)}, f32[672,128]{1,0:T(8,128)S(1)}, u32[]{:S(2)}) copy-start(f32[672,128]{1,0:T(8,128)S(1)} %collective-permute-done.4.refs_3_) | copy-start | bytes 1032196
  79.4 3.0 %collective-permute-start.14 = (f32[1024,128]{1,0:T(8,128)}, f32[1024,128]{1,0:T(8,128)S(1)}, u32[]{:S(2)}, u32[]{:S(2)}) collective-permute-start(f32[1024,128]{1,0:T(8,128)} %get-tuple-element.55), channel_id=1, source_target_pairs={{0,16},{16,0},{32,48},{48,32},{64,80},{80,64},{96,112},{112,96},{1... | collective-permute-start | bytes 1572872 | tf_op jit(solution)/shard_map/ppermute | solution.py:54
  131.3 4.7 %copy-start = (f32[64,16,128]{2,1,0:T(8,128)}, f32[64,16,128]{2,1,0:T(8,128)S(1)}, u32[]{:S(2)}) copy-start(f32[64,16,128]{2,1,0:T(8,128)S(1)} %all_to_all.11) | copy-start | bytes 1572868
  131.3 4.7 %collective-permute-start.15 = (f32[1024,128]{1,0:T(8,128)S(1)}, f32[1024,128]{1,0:T(8,128)S(1)}, u32[]{:S(2)}, u32[]{:S(2)}) collective-permute-start(f32[1024,128]{1,0:T(8,128)S(1)} %bitcast.20), channel_id=1, source_target_pairs={{0,16},{16,0},{32,48},{48,32},{64,80},{80,64},{96,112},{112,96},{1... | collective-permute-start | bytes 1572872 | tf_op jit(solution)/shard_map/ppermute | solution.py:61
  136.1 0.8 copy-start.1

commit v4 on v3

--- a/solution.py
+++ b/solution.py
@@ -8,6 +8,7 @@
 X, R = 672, 96
 ROWS = 84
 BLOCK = 16
+STEPS = (0, 1, 3, 2)
 HALF = 1024
 F32, BF16 = jnp.float32, jnp.bfloat16
 NN = (((1,), (0,)), ((), ()))
@@ -231,52 +232,50 @@
     )(pos, mine, other, basis_t, *fibers)
 
 
-def pack_kernel(pos, species, same, across):
-    rows = same.shape[0]
-    a, b = species[0].reshape(rows, 128), species[1].reshape(rows, 128)
+def pack_kernel(pos, species, *outs):
+    rows = outs[0].shape[0]
     first = lax.broadcasted_iota(jnp.int32, (rows, 128), 1) < 64
-    low = jnp.where(first, a, pltpu.roll(b, 64, 1))
-    high = jnp.where(first, pltpu.roll(a, 64, 1), b)
-    even = pos[0] == 0
-    same[...] = jnp.where(even, low, high)
-    across[...] = jnp.where(even, high, low)
-
-
-def pack(core_and_tile, tensor, k):
-    rows = ROWS // 2
+    even = pos[1] == 0
+    for i, dy in enumerate(STEPS):
+        at = pl.ds(pl.multiple_of(lax.rem(pos[0] + dy, 4) * 128, 128), 128)
+        a, b = (species[q, :, :, at].reshape(rows, 128) for q in range(2))
+        low = jnp.where(first, a, pltpu.roll(b, 64, 1))
+        high = jnp.where(first, pltpu.roll(a, 64, 1), b)
+        outs[2 * i][...] = jnp.where(even, low, high)
+        outs[2 * i + 1][...] = jnp.where(even, high, low)
+
+
+def pack(pos, tensor, k):
+    rows = 12
     out = pl.BlockSpec((rows * 8, 128), lambda i, pos: (i, 0))
     return pl.pallas_call(
         pack_kernel,
         grid_spec=pltpu.PrefetchScalarGridSpec(
             num_scalar_prefetch=1,
-            grid=(2,),
-            in_specs=[pl.BlockSpec((2, rows, 8, 128), lambda i, pos: (k, i, 0, pos[1]))],
-            out_specs=(out, out),
+            grid=(ROWS // rows,),
+            in_specs=[pl.BlockSpec((2, rows, 8, 512), lambda i, pos: (k, i, 0, 0))],
+            out_specs=(out,) * 8,
         ),
-        out_shape=(jax.ShapeDtypeStruct((ROWS * 8, 128), F32),) * 2,
-        cost_estimate=pl.CostEstimate(flops=2**20, bytes_accessed=2**20, transcendentals=0),
-    )(core_and_tile, tensor)
+        out_shape=(jax.ShapeDtypeStruct((ROWS * 8, 128), F32),) * 8,
+        cost_estimate=pl.CostEstimate(flops=2**20, bytes_accessed=11 * 2**19, transcendentals=0),
+    )(pos, tensor)
 
 
 def per_device(tensor, start_basis):
     me = lax.axis_index("gx")
     y, c = me // 2, me % 2
-    offsets = [(dy, dc) for dy in (1, 3, 2, 0) for dc in (1, 0)]
-    sources = [2 * ((y - dy) % 4) + (c ^ dc) for dy, dc in offsets]
+    sources = [2 * ((y - dy) % 4) + (c ^ dc) for dy in STEPS for dc in range(2)]
     pos = jnp.stack([y, c] + sources).astype(jnp.int32)
     basis_t = start_basis.T
 
     fibers, halves = [], ()
     for k in range(2):
-        blocks = []
-        for dy in (1, 3, 2, 0):
-            where = jnp.stack([c, (y + dy) % 4]).astype(jnp.int32)
-            if k:
-                where, _ = lax.optimization_barrier((where, earlier))
-            same, across = pack(where, tensor, k)
-            blocks.append(lax.ppermute(across, "gx", perm_gx(dy, 1)))
-            blocks.append(lax.ppermute(same, "gx", perm_gx(dy, 0)) if dy else same)
-        earlier = blocks[6]
+        blocks = list(pack(pos, tensor, k))
+        if k:
+            for i in (3, 5):
+                blocks[i], _ = lax.optimization_barrier((blocks[i], halves[0]))
+        for i in range(1, 8):
+            blocks[i] = lax.ppermute(blocks[i], "gx", perm_gx(STEPS[i // 2], i % 2))
         hi, lo, *halves = gram(pos, blocks, halves)
         fibers += [hi, lo]
 

time: 153 us -> 147 us (0.961)
  starting transfers between devices: 34 us -> 45.2 us
  Pallas kernels: 50.3 us -> 41.2 us
  blocking collectives: 47.7 us -> 39.1 us
  other arithmetic: 3.04 us -> 1.19 us
  waiting for transfers between devices: 14.5 us -> 16.1 us
    ppermute x14, starting transfers between devices: 29.6 us -> 40.7 us  [per_device(): blocks[i] = lax.ppermute(blocks[i], 'gx', perm_gx(STEPS[i // 2], i % 2))]
    pallas_call x8 -> x2, Pallas kernels: 22.1 us -> 12.9 us  [pack(): pl.pallas_call(pack_kernel, grid_spec=pltpu.PrefetchScalarGridSpec(num_sc...]
    all_to_all x1, blocking collectives: 32.2 us -> 23.4 us  [total_over_devices(): lax.all_to_all(half.reshape(64, 16, 128), both, 0, 0, axis_index_groups=S...]
    another operation x3 -> x0, other arithmetic: 1.85 us -> none  [per_device(): where = jnp.stack([c, (y + dy) % 4]).astype(jnp.int32)]
    ppermute x14, waiting for transfers between devices: 11.2 us -> 12.8 us  [per_device(): blocks[i] = lax.ppermute(blocks[i], 'gx', perm_gx(STEPS[i // 2], i % 2))]
  transfers between devices with their start and end apart: 16 -> 16, of which waited for: 6 -> 6; matrix products, arithmetic and copies ran while one was open for 1% -> 0% of each run, Pallas kernels for 17% -> 9%
where the time goes in v4:
time: 147 us
  starting transfers between devices  45.2 us (31%)
  Pallas kernels  41.2 us (28%)
  blocking collectives  39.1 us (27%)
  waiting for transfers between devices  16.1 us (11%)
  local copies, waits for them, and re-layouts  2.93 us (2%)
    ppermute x14, starting transfers between devices, per_device(): blocks[i] = lax.ppermute(blocks[i], 'gx', perm_gx(STEPS[i // 2], i % 2))  40.7 us
    all_to_all x1, blocking collectives, total_over_devices(): lax.all_to_all(half.reshape(64, 16, 128), both, 0, 0, axis_index_groups=S...  23.4 us
    all_to_all x1, blocking collectives, total_over_devices(): lax.all_to_all(jnp.broadcast_to(piece[None], (64, 16, 128)), both, 0, 0,...  15.7 us
    pallas_call x1, Pallas kernels, finish(): pl.pallas_call(finish_kernel, out_shape=(jax.ShapeDtypeStruct((R, X), F32...  15.1 us
    pallas_call x2, Pallas kernels, gram(): pl.pallas_call(gram_kernel, out_shape=(jax.ShapeDtypeStruct((X, 1024), BF...  13.3 us
    pallas_call x2, Pallas kernels, pack(): pl.pallas_call(pack_kernel, grid_spec=pltpu.PrefetchScalarGridSpec(num_sc...  12.9 us
    ppermute x14, waiting for transfers between devices, per_device(): blocks[i] = lax.ppermute(blocks[i], 'gx', perm_gx(STEPS[i // 2], i % 2))  12.8 us
    ppermute x1, starting transfers between devices, total_over_devices(): return (whole, lax.ppermute(whole, 'gx', perm_gx(0, 1)))  3.2 us
  transfers between devices with their start and end apart: 16, of which 6 were waited for; matrix products, arithmetic and copies ran while one was open for 0% of the time, Pallas kernels for 9%

profile of v4, /device:TPU:1, one launch (start us, length us, event | category | flops | bytes accessed | tf_op | source)
XLA Modules:
  0.0 146.8 jit_solution(10232637430869488853)
XLA Ops:
  0.7 0.6 stack.43.pos
  1.3 6.4 %shard_map.42 = (f32[672,128]{1,0:T(8,128)}, f32[672,128]{1,0:T(8,128)}, f32[672,128]{1,0:T(8,128)}, f32[672,128]{1,0:T(8,128)}, f32[672,128]{1,0:T(8,128)}, /*i...) custom-call(s32[10]{0:T(128)} %stack.43.pos, f32[4,84,8,512]{3,2,1,0:T(8,128)} %species.3), custom_call_target="tpu_custom_call" | custom-call | flops 1048576 | bytes 5767168 | tf_op jit(solution)/shard_map/pallas_call | solution.py:251
  7.7 1.5 %collective-permute-start.2 = (f32[672,128]{1,0:T(8,128)}, f32[672,128]{1,0:T(8,128)S(1)}, u32[]{:S(2)}, u32[]{:S(2)}) collective-permute-start(f32[672,128]{1,0:T(8,128)} %get-tuple-element.35), channel_id=1, source_target_pairs={{0,16},{16,0},{32,48},{48,32},{64,80},{80,64},{96,112},{112,96},{1... | collective-permute-start | bytes 1032200 | tf_op jit(solution)/shard_map/ppermute | solution.py:278
  9.2 1.4 collective-permute-start.3
  10.6 1.5 %collective-permute-start.4 = (f32[672,128]{1,0:T(8,128)}, f32[672,128]{1,0:T(8,128)S(1)}, u32[]{:S(2)}, u32[]{:S(2)}) collective-permute-start(f32[672,128]{1,0:T(8,128)} %get-tuple-element.37), channel_id=1, source_target_pairs={{0,48},{16,32},{32,80},{48,64},{64,112},{80,96},{96,16},{112,0},{1... | collective-permute-start | bytes 1032200 | tf_op jit(solution)/shard_map/ppermute | solution.py:278
  12.1 1.4 collective-permute-start.5
  13.5 0.6 collective-permute-start.6
  14.1 1.6 %collective-permute-start.7 = (f32[672,128]{1,0:T(8,128)}, f32[672,128]{1,0:T(8,128)S(1)}, u32[]{:S(2)}, u32[]{:S(2)}) collective-permute-start(f32[672,128]{1,0:T(8,128)} %get-tuple-element.40), channel_id=1, source_target_pairs={{0,64},{16,80},{32,96},{48,112},{64,0},{80,16},{96,32},{112,48},{1... | collective-permute-start | bytes 1032200 | tf_op jit(solution)/shard_map/ppermute | solution.py:278
  15.7 4.8 %collective-permute-done.3.refs_2_ = f32[672,128]{1,0:T(8,128)S(1)} collective-permute-done((f32[672,128]{1,0:T(8,128)}, f32[672,128]{1,0:T(8,128)S(1)}, u32[]{:S(2)}, u32[]{:S(2)}) %collective-permute-start.3) | collective-permute-done | bytes 344096 | tf_op jit(solution)/shard_map/ppermute | solution.py:278
  20.6 2.7 %collective-permute-start.8 = (f32[672,128]{1,0:T(8,128)}, f32[672,128]{1,0:T(8,128)S(1)}, u32[]{:S(2)}, u32[]{:S(2)}) collective-permute-start(f32[672,128]{1,0:T(8,128)} %get-tuple-element.41), channel_id=1, source_target_pairs={{0,80},{16,64},{32,112},{48,96},{64,16},{80,0},{96,48},{112,32},{1... | collective-permute-start | bytes 1032200 | tf_op jit(solution)/shard_map/ppermute | solution.py:278
  23.3 6.5 %shard_map.41 = (f32[672,128]{1,0:T(8,128)}, f32[672,128]{1,0:T(8,128)}, f32[672,128]{1,0:T(8,128)}, f32[672,128]{1,0:T(8,128)}, f32[672,128]{1,0:T(8,128)}, /*i...) custom-call(s32[10]{0:T(128)} %stack.43.pos, f32[4,84,8,512]{3,2,1,0:T(8,128)} %species.3), custom_call_target="tpu_custom_call" | custom-call | flops 1048576 | bytes 5767168 | tf_op jit(solution)/shard_map/pallas_call | solution.py:251
  29.9 0.5 collective-permute-start.1
  30.4 16.5 %collective-permute-start.10 = (f32[672,128]{1,0:T(8,128)}, f32[672,128]{1,0:T(8,128)S(1)}, u32[]{:S(2)}, u32[]{:S(2)}) collective-permute-start(f32[672,128]{1,0:T(8,128)} %get-tuple-element.44), channel_id=1, source_target_pairs={{0,96},{16,112},{32,0},{48,16},{64,32},{80,48},{96,64},{112,80},{1... | collective-permute-start | bytes 1032200 | tf_op jit(solution)/shard_map/ppermute | solution.py:278
  46.9 0.5 collective-permute-start.12
  47.4 0.2 copy-done.12
  47.6 0.5 copy-done.14
  48.1 6.4 %shard_map.43 = (bf16[672,1024]{1,0:T(8,128)(2,1)}, bf16[672,1024]{1,0:T(8,128)(2,1)}, f32[1024,128]{1,0:T(8,128)}, f32[1024,128]{1,0:T(8,128)}) custom-call(s32[10]{0:T(128)} %stack.43.pos, f32[672,128]{1,0:T(8,128)} %get-tuple-element.34.refs_0_, f32[672,128]{1,0:T(8,128)} %copy-done.3, f32[672,128]{1,0:T(8,128)} %copy-done.5, f32[672,128]{1,0:T(8,128)} %copy-done.7, ...), custom_call_target="tpu_custom_call" | custom-call | flops 2774532096 | bytes 6291456 | tf_op jit(solution)/shard_map/pallas_call | solution.py:107
  54.6 2.2 %collective-permute-start.11 = (f32[672,128]{1,0:T(8,128)S(1)}, f32[672,128]{1,0:T(8,128)S(1)}, u32[]{:S(2)}, u32[]{:S(2)}) collective-permute-start(f32[672,128]{1,0:T(8,128)S(1)} %copy-done.6), channel_id=1, source_target_pairs={{0,112},{16,96},{32,16},{48,0},{64,48},{80,32},{96,80},{112,64},{1... | collective-permute-start | bytes 1032200 | tf_op jit(solution)/shard_map/ppermute | solution.py:278
  56.8 10.3 %collective-permute-start.9 = (f32[672,128]{1,0:T(8,128)S(1)}, f32[672,128]{1,0:T(8,128)S(1)}, u32[]{:S(2)}, u32[]{:S(2)}) collective-permute-start(f32[672,128]{1,0:T(8,128)S(1)} %copy-done.4), channel_id=1, source_target_pairs={{0,48},{16,32},{32,80},{48,64},{64,112},{80,96},{96,16},{112,0},{1... | collective-permute-start | bytes 1032200 | tf_op jit(solution)/shard_map/ppermute | solution.py:278
  67.1 0.5 collective-permute-done.13.refs_7_
  67.6 7.4 %collective-permute-done.11.refs_5_ = f32[672,128]{1,0:T(8,128)S(1)} collective-permute-done((f32[672,128]{1,0:T(8,128)S(1)}, f32[672,128]{1,0:T(8,128)S(1)}, u32[]{:S(2)}, u32[]{:S(2)}) %collective-permute-start.11) | collective-permute-done | bytes 344096 | tf_op jit(solution)/shard_map/ppermute | solution.py:278
  75.1 0.6 copy-done.16
  75.9 6.8 %shard_map.44 = (bf16[672,1024]{1,0:T(8,128)(2,1)}, bf16[672,1024]{1,0:T(8,128)(2,1)}, f32[1024,128]{1,0:T(8,128)}, f32[1024,128]{1,0:T(8,128)}) custom-call(s32[10]{0:T(128)} %stack.43.pos, f32[672,128]{1,0:T(8,128)} %get-tuple-element.30.refs_0_, f32[672,128]{1,0:T(8,128)} %copy-done.2, f32[672,128]{1,0:T(8,128)} %copy-done.8, f32[672,128]{1,0:T(8,128)} %copy-done.17, ...), custom_call_target="tpu_custom_call" | custom-call | flops 2774532096 | bytes 6291456 | tf_op jit(solution)/shard_map/pallas_call | solution.py:107
  82.7 1.2 collective-permute-start.14
  83.9 1.7 %collective-permute-done.14 = f32[1024,128]{1,0:T(8,128)S(1)} collective-permute-done((f32[1024,128]{1,0:T(8,128)}, f32[1024,128]{1,0:T(8,128)S(1)}, u32[]{:S(2)}, u32[]{:S(2)}) %collective-permute-start.14) | collective-permute-done | bytes 524320 | tf_op jit(solution)/shard_map/ppermute | solution.py:55
  85.7 1.1 add.64
  86.8 23.4 %all_to_all.10 = f32[64,16,128]{2,1,0:T(8,128)S(1)} all-to-all(f32[64,16,128]{2,1,0:T(8,128)S(1)} %bitcast.15), channel_id=1, replica_groups={{0,1,2,3,4,5,6,7,8,9,10,11,12,13,14,15,32,33,34,35,36,37,38,39,40,41,42..., dimensions={0} | all-to-all | bytes 1048576 | tf_op jit(solution)/shard_map/all_to_all | solution.py:57
  110.3 15.7 %all_to_all.11 = f32[64,16,128]{2,1,0:T(8,128)S(1)} all-to-all(f32[64,16,128]{2,1,0:T(8,128)S(1)} %broadcast_in_dim.2), channel_id=1, replica_groups={{0,1,2,3,4,5,6,7,8,9,10,11,12,13,14,15,32,33,34,35,36,37,38,39,40,41,42..., dimensions={0} | all-to-all | bytes 1048576 | tf_op jit(solution)/shard_map/all_to_all | solution.py:59
  126.0 3.2 %collective-permute-start.15 = (f32[1024,128]{1,0:T(8,128)S(1)}, f32[1024,128]{1,0:T(8,128)S(1)}, u32[]{:S(2)}, u32[]{:S(2)}) collective-permute-start(f32[1024,128]{1,0:T(8,128)S(1)} %bitcast.16), channel_id=1, source_target_pairs={{0,16},{16,0},{32,48},{48,32},{64,80},{80,64},{96,112},{112,96},{1... | collective-permute-start | bytes 1572872 | tf_op jit(solution)/shard_map/ppermute | solution.py:62
  129.2 1.5 %collective-permute-done.15.other = f32[1024,128]{1,0:T(8,128)S(1)} collective-permute-done((f32[1024,128]{1,0:T(8,128)S(1)}, f32[1024,128]{1,0:T(8,128)S(1)}, u32[]{:S(2)}, u32[]{:S(2)}) %collective-permute-start.15) | collective-permute-done | bytes 524320 | tf_op jit(solution)/shard_map/ppermute | solution.py:62
  130.8 0.8 copy-done.1
  131.6 15.1 %shard_map.45 = (f32[96,672]{1,0:T(8,128)}, f32[4,8,64,96]{3,2,1,0:T(8,128)}) custom-call(s32[10]{0:T(128)} %stack.43.pos, f32[1024,128]{1,0:T(8,128)} %bitcast.17, f32[1024,128]{1,0:T(8,128)} %copy-done.1, f32[96,672]{1,0:T(8,128)} %bitcast.18, bf16[672,1024]{1,0:T(8,128)(2,1)} %get-tuple-element.52.hi0, bf16[672,1024]{1,0:T(8,128)(2,1)} %get-tuple-element.53.lo0, ...), custom_call_target="tpu_custom_call" | custom-call | flops 792723456 | bytes 7340032 | tf_op jit(solution)/shard_map/pallas_call | solution.py:217
  (47 shorter events, 0.5 us)
Async XLA Ops:
  7.7 6.4 %collective-permute-start.2 = (f32[672,128]{1,0:T(8,128)}, f32[672,128]{1,0:T(8,128)S(1)}, u32[]{:S(2)}, u32[]{:S(2)}) collective-permute-start(f32[672,128]{1,0:T(8,128)} %get-tuple-element.35), channel_id=1, source_target_pairs={{0,16},{16,0},{32,48},{48,32},{64,80},{80,64},{96,112},{112,96},{1... | collective-permute-start | bytes 1032200 | tf_op jit(solution)/shard_map/ppermute | solution.py:278
  9.2 11.3 %collective-permute-start.3 = (f32[672,128]{1,0:T(8,128)}, f32[672,128]{1,0:T(8,128)S(1)}, u32[]{:S(2)}, u32[]{:S(2)}) collective-permute-start(f32[672,128]{1,0:T(8,128)} %get-tuple-element.36), channel_id=1, source_target_pairs={{0,32},{16,48},{32,64},{48,80},{64,96},{80,112},{96,0},{112,16},{1... | collective-permute-start | bytes 1032200 | tf_op jit(solution)/shard_map/ppermute | solution.py:278
  10.6 19.1 %collective-permute-start.4 = (f32[672,128]{1,0:T(8,128)}, f32[672,128]{1,0:T(8,128)S(1)}, u32[]{:S(2)}, u32[]{:S(2)}) collective-permute-start(f32[672,128]{1,0:T(8,128)} %get-tuple-element.37), channel_id=1, source_target_pairs={{0,48},{16,32},{32,80},{48,64},{64,112},{80,96},{96,16},{112,0},{1... | collective-permute-start | bytes 1032200 | tf_op jit(solution)/shard_map/ppermute | solution.py:278
  12.1 17.7 %collective-permute-start.5 = (f32[672,128]{1,0:T(8,128)}, f32[672,128]{1,0:T(8,128)S(1)}, u32[]{:S(2)}, u32[]{:S(2)}) collective-permute-start(f32[672,128]{1,0:T(8,128)} %get-tuple-element.38), channel_id=1, source_target_pairs={{0,96},{16,112},{32,0},{48,16},{64,32},{80,48},{96,64},{112,80},{1... | collective-permute-start | bytes 1032200 | tf_op jit(solution)/shard_map/ppermute | solution.py:278
  13.5 16.9 %collective-permute-start.6 = (f32[672,128]{1,0:T(8,128)}, f32[672,128]{1,0:T(8,128)S(1)}, u32[]{:S(2)}, u32[]{:S(2)}) collective-permute-start(f32[672,128]{1,0:T(8,128)} %get-tuple-element.39), channel_id=1, source_target_pairs={{0,112},{16,96},{32,16},{48,0},{64,48},{80,32},{96,80},{112,64},{1... | collective-permute-start | bytes 1032200 | tf_op jit(solution)/shard_map/ppermute | solution.py:278
  14.1 15.6 %copy-start.3 = (f32[672,128]{1,0:T(8,128)}, f32[672,128]{1,0:T(8,128)S(1)}, u32[]{:S(2)}) copy-start(f32[672,128]{1,0:T(8,128)S(1)} %collective-permute-done.2.refs_1_) | copy-start | bytes 1032196
  14.1 32.8 %collective-permute-start.7 = (f32[672,128]{1,0:T(8,128)}, f32[672,128]{1,0:T(8,128)S(1)}, u32[]{:S(2)}, u32[]{:S(2)}) collective-permute-start(f32[672,128]{1,0:T(8,128)} %get-tuple-element.40), channel_id=1, source_target_pairs={{0,64},{16,80},{32,96},{48,112},{64,0},{80,16},{96,32},{112,48},{1... | collective-permute-start | bytes 1032200 | tf_op jit(solution)/shard_map/ppermute | solution.py:278
  20.6 9.2 %copy-start.5 = (f32[672,128]{1,0:T(8,128)}, f32[672,128]{1,0:T(8,128)S(1)}, u32[]{:S(2)}) copy-start(f32[672,128]{1,0:T(8,128)S(1)} %collective-permute-done.3.refs_2_) | copy-start | bytes 1032196
  20.6 26.8 %collective-permute-start.8 = (f32[672,128]{1,0:T(8,128)}, f32[672,128]{1,0:T(8,128)S(1)}, u32[]{:S(2)}, u32[]{:S(2)}) collective-permute-start(f32[672,128]{1,0:T(8,128)} %get-tuple-element.41), channel_id=1, source_target_pairs={{0,80},{16,64},{32,112},{48,96},{64,16},{80,0},{96,48},{112,32},{1... | collective-permute-start | bytes 1032200 | tf_op jit(solution)/shard_map/ppermute | solution.py:278
  29.8 17.6 %copy-start.7 = (f32[672,128]{1,0:T(8,128)}, f32[672,128]{1,0:T(8,128)S(1)}, u32[]{:S(2)}) copy-start(f32[672,128]{1,0:T(8,128)S(1)} %collective-permute-done.4.refs_3_) | copy-start | bytes 1032196
  29.8 24.8 %collective-permute-start = (f32[672,128]{1,0:T(8,128)}, f32[672,128]{1,0:T(8,128)S(1)}, u32[]{:S(2)}, u32[]{:S(2)}) collective-permute-start(f32[672,128]{1,0:T(8,128)} %get-tuple-element.31), channel_id=1, source_target_pairs={{0,16},{16,0},{32,48},{48,32},{64,80},{80,64},{96,112},{112,96},{1... | collective-permute-start | bytes 1032200 | tf_op jit(solution)/shard_map/ppermute | solution.py:278
  29.9 17.5 %copy-start.9 = (f32[672,128]{1,0:T(8,128)}, f32[672,128]{1,0:T(8,128)S(1)}, u32[]{:S(2)}) copy-start(f32[672,128]{1,0:T(8,128)S(1)} %collective-permute-done.5.refs_4_) | copy-start | bytes 1032196
  29.9 26.9 %collective-permute-start.1 = (f32[672,128]{1,0:T(8,128)}, f32[672,128]{1,0:T(8,128)S(1)}, u32[]{:S(2)}, u32[]{:S(2)}) collective-permute-start(f32[672,128]{1,0:T(8,128)} %get-tuple-element.32), channel_id=1, source_target_pairs={{0,32},{16,48},{32,64},{48,80},{64,96},{80,112},{96,0},{112,16},{1... | collective-permute-start | bytes 1032200 | tf_op jit(solution)/shard_map/ppermute | solution.py:278
  30.4 17.0 %copy-start.10 = (f32[672,128]{1,0:T(8,128)}, f32[672,128]{1,0:T(8,128)S(1)}, u32[]{:S(2)}) copy-start(f32[672,128]{1,0:T(8,128)S(1)} %collective-permute-done.6.refs_5_) | copy-start | bytes 1032196
  30.4 36.7 %collective-permute-start.10 = (f32[672,128]{1,0:T(8,128)}, f32[672,128]{1,0:T(8,128)S(1)}, u32[]{:S(2)}, u32[]{:S(2)}) collective-permute-start(f32[672,128]{1,0:T(8,128)} %get-tuple-element.44), channel_id=1, source_target_pairs={{0,96},{16,112},{32,0},{48,16},{64,32},{80,48},{96,64},{112,80},{1... | collective-permute-start | bytes 1032200 | tf_op jit(solution)/shard_map/ppermute | solution.py:278
  46.9 0.8 copy-start.12
  46.9 20.3 %collective-permute-start.12 = (f32[672,128]{1,0:T(8,128)}, f32[672,128]{1,0:T(8,128)S(1)}, u32[]{:S(2)}, u32[]{:S(2)}) collective-permute-start(f32[672,128]{1,0:T(8,128)} %get-tuple-element.47), channel_id=1, source_target_pairs={{0,64},{16,80},{32,96},{48,112},{64,0},{80,16},{96,32},{112,48},{1... | collective-permute-start | bytes 1032200 | tf_op jit(solution)/shard_map/ppermute | solution.py:278
  47.4 20.2 %collective-permute-start.13 = (f32[672,128]{1,0:T(8,128)}, f32[672,128]{1,0:T(8,128)S(1)}, u32[]{:S(2)}, u32[]{:S(2)}) collective-permute-start(f32[672,128]{1,0:T(8,128)} %get-tuple-element.48), channel_id=1, source_target_pairs={{0,80},{16,64},{32,112},{48,96},{64,16},{80,0},{96,48},{112,32},{1... | collective-permute-start | bytes 1032200 | tf_op jit(solution)/shard_map/ppermute | solution.py:278
  48.1 6.5 %copy-start.6 = (f32[672,128]{1,0:T(8,128)S(1)}, f32[672,128]{1,0:T(8,128)}, u32[]{:S(2)}) copy-start(f32[672,128]{1,0:T(8,128)} %get-tuple-element.46) | copy-start | bytes 1032196
  48.1 8.7 %copy-start.4 = (f32[672,128]{1,0:T(8,128)S(1)}, f32[672,128]{1,0:T(8,128)}, u32[]{:S(2)}) copy-start(f32[672,128]{1,0:T(8,128)} %get-tuple-element.43) | copy-start | bytes 1032196
  54.6 20.5 %copy-start.2 = (f32[672,128]{1,0:T(8,128)}, f32[672,128]{1,0:T(8,128)S(1)}, u32[]{:S(2)}) copy-start(f32[672,128]{1,0:T(8,128)S(1)} %collective-permute-done.refs_1_) | copy-start | bytes 1032196
  54.6 20.4 %collective-permute-start.11 = (f32[672,128]{1,0:T(8,128)S(1)}, f32[672,128]{1,0:T(8,128)S(1)}, u32[]{:S(2)}, u32[]{:S(2)}) collective-permute-start(f32[672,128]{1,0:T(8,128)S(1)} %copy-done.6), channel_id=1, source_target_pairs={{0,112},{16,96},{32,16},{48,0},{64,48},{80,32},{96,80},{112,64},{1... | collective-permute-start | bytes 1032200 | tf_op jit(solution)/shard_map/ppermute | solution.py:278
  56.8 18.3 %copy-start.8 = (f32[672,128]{1,0:T(8,128)}, f32[672,128]{1,0:T(8,128)S(1)}, u32[]{:S(2)}) copy-start(f32[672,128]{1,0:T(8,128)S(1)} %collective-permute-done.1.refs_2_) | copy-start | bytes 1032196
  56.8 18.3 %collective-permute-start.9 = (f32[672,128]{1,0:T(8,128)S(1)}, f32[672,128]{1,0:T(8,128)S(1)}, u32[]{:S(2)}, u32[]{:S(2)}) collective-permute-start(f32[672,128]{1,0:T(8,128)S(1)} %copy-done.4), channel_id=1, source_target_pairs={{0,48},{16,32},{32,80},{48,64},{64,112},{80,96},{96,16},{112,0},{1... | collective-permute-start | bytes 1032200 | tf_op jit(solution)/shard_map/ppermute | solution.py:278
  67.1 8.0 %copy-start.11 = (f32[672,128]{1,0:T(8,128)}, f32[672,128]{1,0:T(8,128)S(1)}, u32[]{:S(2)}) copy-start(f32[672,128]{1,0:T(8,128)S(1)} %collective-permute-done.10.refs_4_) | copy-start | bytes 1032196
  67.1 8.0 %copy-start.13 = (f32[672,128]{1,0:T(8,128)}, f32[672,128]{1,0:T(8,128)S(1)}, u32[]{:S(2)}) copy-start(f32[672,128]{1,0:T(8,128)S(1)} %collective-permute-done.12.refs_6_) | copy-start | bytes 1032196
  67.6 7.5 %copy-start.15 = (f32[672,128]{1,0:T(8,128)}, f32[672,128]{1,0:T(8,128)S(1)}, u32[]{:S(2)}) copy-start(f32[672,128]{1,0:T(8,128)S(1)} %collective-permute-done.13.refs_7_) | copy-start | bytes 1032196
  75.1 0.8 copy-start.17
  82.7 3.0 %collective-permute-start.14 = (f32[1024,128]{1,0:T(8,128)}, f32[1024,128]{1,0:T(8,128)S(1)}, u32[]{:S(2)}, u32[]{:S(2)}) collective-permute-start(f32[1024,128]{1,0:T(8,128)} %get-tuple-element.51), channel_id=1, source_target_pairs={{0,16},{16,0},{32,48},{48,32},{64,80},{80,64},{96,112},{112,96},{1... | collective-permute-start | bytes 1572872 | tf_op jit(solution)/shard_map/ppermute | solution.py:55
  126.0 4.7 %copy-start = (f32[64,16,128]{2,1,0:T(8,128)}, f32[64,16,128]{2,1,0:T(8,128)S(1)}, u32[]{:S(2)}) copy-start(f32[64,16,128]{2,1,0:T(8,128)S(1)} %all_to_all.11) | copy-start | bytes 1572868
  126.0 4.7 %collective-permute-start.15 = (f32[1024,128]{1,0:T(8,128)S(1)}, f32[1024,128]{1,0:T(8,128)S(1)}, u32[]{:S(2)}, u32[]{:S(2)}) collective-permute-start(f32[1024,128]{1,0:T(8,128)S(1)} %bitcast.16), channel_id=1, source_target_pairs={{0,16},{16,0},{32,48},{48,32},{64,80},{80,64},{96,112},{112,96},{1... | collective-permute-start | bytes 1572872 | tf_op jit(solution)/shard_map/ppermute | solution.py:62
  130.8 0.8 copy-start.1
  (2 other events, 1.5 us)

commit v5 on v4

v5 whole, which is shorter than its diff:
```python
import jax
import jax.numpy as jnp
from jax import lax
from jax.experimental import pallas as pl
from jax.experimental.pallas import tpu as pltpu
from jax.sharding import PartitionSpec as P

X, R = 672, 96
ROWS = 84
BLOCK = 16
OFFSETS = ((1, 0), (3, 1), (3, 0), (0, 1), (2, 1), (2, 0), (1, 1), (0, 0))
HALF = 1024
F32, BF16 = jnp.float32, jnp.bfloat16
NN = (((1,), (0,)), ((), ()))
NT = (((1,), (1,)), ((), ()))
VMEM_LIMIT = 56 * 1024 * 1024
STARTS = (0, 672, 1216, 1632, 1920)


def split(a):
    hi = a.astype(BF16)
    return hi, (a - hi.astype(F32)).astype(BF16)


def dot3(a, b, dims):
    d = lambda p, q: lax.dot_general(p, q, dims, preferred_element_type=F32)
    return d(a[0], b[0]) + (d(a[0], b[1]) + d(a[1], b[0]))


def dot_thin(a, b):
    def parts(v):
        first = v.astype(BF16)
        v = v - first.astype(F32)
        second = v.astype(BF16)
        return first, second, (v - second.astype(F32)).astype(BF16)

    p, q = parts(a), parts(b)
    left = jnp.concatenate([p[0], p[0], p[1], p[0], p[1], p[2]], axis=0)
    right = jnp.concatenate([q[0], q[1], q[0], q[2], q[1], q[0]], axis=0)
    return lax.dot_general(left, right, (((0,), (0,)), ((), ())), preferred_element_type=F32)


def dot_full(a, b, dims):
    return lax.dot_general(a, b, dims, precision=lax.Precision.HIGHEST, preferred_element_type=F32)


def perm_gx(dy, dc):
    return [(2 * y + c, 2 * ((y + dy) % 4) + (c ^ dc)) for y in range(4) for c in range(2)]


SAME_CORE = [[(2 * y + c) * 16 + k for y in range(4) for k in range(16)] for c in range(2)]


def total_over_devices(mine, other):
    half = mine + lax.ppermute(other, "gx", perm_gx(0, 1))
    both = ("gx", "gy")
    parts = lax.all_to_all(half.reshape(64, 16, 128), both, 0, 0, axis_index_groups=SAME_CORE)
    piece = jnp.sum(parts, 0)
    whole = lax.all_to_all(
        jnp.broadcast_to(piece[None], (64, 16, 128)), both, 0, 0, axis_index_groups=SAME_CORE
    ).reshape(HALF, 128)
    return whole, lax.ppermute(whole, "gx", perm_gx(0, 1))


def place():
    me = lax.axis_index("gx")
    return lax.div(me, 2), lax.rem(me, 2)


def gathers(blocks, cells, sems):
    y, c = place()
    copies = []
    for i, (dy, dc) in enumerate(OFFSETS):
        source = 2 * lax.rem(y + 4 - dy, 4) + lax.bitwise_xor(c, dc)
        at = pl.ds(pl.multiple_of(source * 672, 672), 672)
        copies += [pltpu.make_async_copy(blocks[8 * k + i], cells.at[k, at], sems.at[k, i]) for k in range(2)]
    return copies[::2], copies[1::2]


def gram_kernel(*refs):
    blocks, (mine, other, cells, hi, lo, packed, sems) = refs[:16], refs[16:]
    copies = gathers(blocks, cells, sems)
    for k in range(2):
        for copy in copies[k]:
            copy.start()

    def put(k, start, value):
        rows = slice(start, start + value.shape[0])
        packed[rows, :] = packed[rows, :] + value if k else value

    for k in range(2):
        for copy in copies[k]:
            copy.wait()
        for q in range(8):
            at = slice(128 * q, 128 * q + 128)
            hi[k, :, at], lo[k, :, at] = split(cells[k, pl.ds(q, X, stride=8), :])
        for j in range(3):
            low, high = 256 * j, min(256 * j + 256, X)
            g = dot3((hi[k, low:, :], lo[k, low:, :]), (hi[k, low:high, :], lo[k, low:high, :]), NT)
            for t in (2 * j, 2 * j + 1):
                col = g[128 * (t % 2) :, 128 * (t % 2) : 128 * (t % 2) + 128]
                if t < 4:
                    put(k, STARTS[t], col)
                elif t == 4:
                    put(k, STARTS[4], col[:128])
                    put(k, 2 * HALF, col[128:160])
                else:
                    put(k, 2 * HALF + 32, jnp.concatenate([col, jnp.zeros((32, 96), F32)], axis=1))
    packed[STARTS[1] : STARTS[1] + 32, 64:] = packed[2 * HALF : 2 * HALF + 32, :64]
    packed[STARTS[1] + 32 : STARTS[1] + 64, 64:] = packed[2 * HALF : 2 * HALF + 32, 64:]
    packed[0:32, 96:] = packed[2 * HALF + 32 : 2 * HALF + 64, :32]
    c = place()[1]
    for out, half in ((mine, c), (other, 1 - c)):
        out[...] = packed[pl.ds(pl.multiple_of(half * HALF, HALF), HALF), :]


def gram(blocks):
    hbm = pl.BlockSpec(memory_space=pl.ANY)
    vmem = pl.BlockSpec(memory_space=pltpu.VMEM)
    return pl.pallas_call(
        gram_kernel,
        out_shape=(jax.ShapeDtypeStruct((HALF, 128), F32),) * 2,
        in_specs=[hbm] * 16,
        out_specs=(vmem, vmem),
        scratch_shapes=[
            pltpu.VMEM((2, X * 8, 128), F32),
            pltpu.VMEM((2, X, 1024), BF16),
            pltpu.VMEM((2, X, 1024), BF16),
            pltpu.VMEM((2 * HALF + 64, 128), F32),
            pltpu.SemaphoreType.DMA((2, 8)),
        ],
        compiler_params=pltpu.CompilerParams(vmem_limit_bytes=VMEM_LIMIT),
        cost_estimate=pl.CostEstimate(flops=3 * 2 * X * X * 2048, bytes_accessed=7 * 2**20, transcendentals=0),
    )(*blocks)


def unpack(packed, g):
    row = lax.broadcasted_iota(jnp.int32, (128, 128), 0)
    col = lax.broadcasted_iota(jnp.int32, (128, 128), 1)
    lower = row >= col
    g[640:, 640:] = jnp.zeros((32, 128), F32)
    for j in range(5):
        at = 128 * j
        block = packed[STARTS[j] : STARTS[j] + 128, :]
        g[at : at + 128, at : at + 128] = jnp.where(lower, block, block.T)
        for i in range(j + 1, 5):
            first = STARTS[j] + 128 * (i - j)
            block = packed[first : first + 128, :]
            g[128 * i : 128 * i + 128, at : at + 128] = block
            g[at : at + 128, 128 * i : 128 * i + 128] = block.T
        if j < 4:
            last = packed[STARTS[j] + 640 - at : STARTS[j] + X - at, :]
        else:
            last = jnp.concatenate(
                [packed[STARTS[1] : STARTS[1] + 32, 64:], packed[STARTS[1] + 32 : STARTS[1] + 64, 64:]], axis=1
            )
        g[640:, at : at + 128] = last
        g[at : at + 128, 640:] = jnp.concatenate([last, jnp.zeros((96, 128), F32)], axis=0).T
    block = jnp.concatenate([packed[0:32, :], jnp.zeros((96, 128), F32)], axis=0)
    block = jnp.concatenate([block[:, 96:], jnp.zeros((128, 96), F32)], axis=1)
    g[640:, 640:] = jnp.where(lower, block, block.T)[:32]


def inverse_factor(s, work, out):
    eye = (lax.broadcasted_iota(jnp.int32, (R, 128), 0) == lax.broadcasted_iota(jnp.int32, (R, 128), 1)).astype(F32)
    work[:, 128:] = eye
    work[:, :R] = s
    work[:, R:128] = jnp.zeros((R, 128 - R), F32)
    for b in range(R // BLOCK):
        at = BLOCK * b
        left = [work[at + i : at + i + 1, :128] for i in range(BLOCK)]
        right = [work[at + i : at + i + 1, 128:] for i in range(BLOCK)]
        d = {
            (i, j): jnp.broadcast_to(left[i][:, at + j : at + j + 1], (1, 128))
            for i in range(BLOCK) for j in range(i + 1)
        }
        scaled = []
        for t in range(BLOCK):
            inverse = 1.0 / d[t, t]
            scaled.append(left[t] * inverse)
            for i in range(t + 1, BLOCK):
                m = d[i, t] * inverse
                for j in range(t + 1, i + 1):
                    d[i, j] = d[i, j] - m * d[j, t]
                left[i] = left[i] - m * left[t]
                right[i] = right[i] - m * right[t]
        root = [lax.rsqrt(d[t, t]) for t in range(BLOCK)]
        root = [q * (1.5 - 0.5 * (d[t, t] * q) * q) for t, q in enumerate(root)]
        out[at : at + BLOCK, :] = jnp.concatenate([right[t] * root[t] for t in range(BLOCK)], axis=0)
        if at + BLOCK < R:
            rows = jnp.concatenate(
                [jnp.concatenate(left, axis=0), jnp.concatenate(right, axis=0)], axis=1
            )
            step = dot_thin(jnp.concatenate(scaled, axis=0), rows)
            work[at + BLOCK :, :] = work[at + BLOCK :, :] - step[at + BLOCK : R]


def finish_kernel(*refs):
    blocks, (mine, other, basis, factor_t, core, packed, g, work, linv, cells, sems) = refs[:16], refs[16:]
    copies = sum(gathers(blocks, cells, sems), [])
    for copy in copies:
        copy.start()
    c = place()[1]
    packed[pl.ds(pl.multiple_of(c * HALF, HALF), HALF), :] = mine[...]
    packed[pl.ds(pl.multiple_of((1 - c) * HALF, HALF), HALF), :] = other[...]
    unpack(packed, g)
    f = basis[...]
    for _ in range(2):
        m = dot_full(f, g[:, :X], NN)
        inverse_factor(dot_full(m, m, NT), work, linv)
        f = dot_full(linv[:, :R], m, NN)
    factor_t[...] = f
    f = split(f)
    for copy in copies:
        copy.wait()
    for k in range(2):
        for y in range(8):
            value = dot3(f, split(cells[k, pl.ds(y, X, stride=8), :]), NN).T
            core[2 * k, y] = value[:64]
            core[2 * k + 1, y] = value[64:]


def finish(blocks, mine, other, basis_t):
    hbm = pl.BlockSpec(memory_space=pl.ANY)
    vmem = pl.BlockSpec(memory_space=pltpu.VMEM)
    return pl.pallas_call(
        finish_kernel,
        out_shape=(jax.ShapeDtypeStruct((R, X), F32), jax.ShapeDtypeStruct((4, 8, 64, R), F32)),
        in_specs=[hbm] * 16 + [vmem] * 3,
        out_specs=(vmem, vmem),
        scratch_shapes=[
            pltpu.VMEM((2 * HALF, 128), F32),
            pltpu.VMEM((X, 768), F32),
            pltpu.VMEM((R, 256), F32),
            pltpu.VMEM((R, 128), F32),
            pltpu.VMEM((2, X * 8, 128), F32),
            pltpu.SemaphoreType.DMA((2, 8)),
        ],
        compiler_params=pltpu.CompilerParams(vmem_limit_bytes=VMEM_LIMIT),
        cost_estimate=pl.CostEstimate(flops=3 * 2 * X * R * 2048, bytes_accessed=7 * 2**20, transcendentals=0),
    )(*blocks, mine, other, basis_t)


def pack_kernel(species, *outs):
    rows = outs[0].shape[0]
    first = lax.broadcasted_iota(jnp.int32, (rows, 128), 1) < 64
    y, c = place()
    even = c == 0
    for dy in range(4):
        at = pl.ds(pl.multiple_of(lax.rem(y + dy, 4) * 128, 128), 128)
        a, b = (species[q, :, :, at].reshape(rows, 128) for q in range(2))
        low = jnp.where(first, a, pltpu.roll(b, 64, 1))
        high = jnp.where(first, pltpu.roll(a, 64, 1), b)
        outs[OFFSETS.index((dy, 0))][...] = jnp.where(even, low, high)
        outs[OFFSETS.index((dy, 1))][...] = jnp.where(even, high, low)


def pack(tensor, k):
    rows = ROWS // 2
    out = pl.BlockSpec((rows * 8, 128), lambda i: (i, 0))
    return pl.pallas_call(
        pack_kernel,
        grid=(2,),
        in_specs=[pl.BlockSpec((2, rows, 8, 512), lambda i: (k, i, 0, 0))],
        out_specs=(out,) * 8,
        out_shape=(jax.ShapeDtypeStruct((ROWS * 8, 128), F32),) * 8,
        compiler_params=pltpu.CompilerParams(vmem_limit_bytes=VMEM_LIMIT),
        cost_estimate=pl.CostEstimate(flops=2**20, bytes_accessed=11 * 2**19, transcendentals=0),
    )(tensor)


def per_device(tensor, start_basis):
    basis_t = start_basis.T
    blocks = []
    for k in range(2):
        packs = pack(tensor, k)
        blocks += [lax.ppermute(b, "gx", perm_gx(*o)) for b, o in zip(packs[:7], OFFSETS)] + [packs[7]]
    factor_t, core = finish(blocks, *total_over_devices(*gram(blocks)), basis_t)
    return factor_t.T, core.transpose(0, 3, 1, 2)


def solution(mesh):
    return jax.shard_map(
        per_device,
        mesh=mesh,
        in_specs=(P(None, "gx", "gy", None), P()),
        out_specs=(P(), P(None, None, "gy", "gx")),
        check_vma=False,
    )
```

time: 147 us -> 142 us (0.966)
  waiting for transfers between devices: 16.1 us -> 32.9 us
  Pallas kernels: 41.2 us -> 30.7 us
  starting transfers between devices: 45.2 us -> 35.9 us
    ppermute x14, waiting for transfers between devices: 12.8 us -> 29.7 us  [per_device(): lax.ppermute(b, 'gx', perm_gx(*o))]
    pallas_call x4 -> x3, Pallas kernels: 26.2 us -> 14.7 us  [the longest x1 8.15 us: gram(): pl.pallas_call(gram_kernel, out_shape=(jax.ShapeDtypeStruct((HALF, 128),...]
    ppermute x14, starting transfers between devices: 40.7 us -> 32.3 us  [per_device(): lax.ppermute(b, 'gx', perm_gx(*o))]
  transfers between devices with their start and end apart: 16 -> 16, of which waited for: 6 -> 9; matrix products, arithmetic and copies ran while one was open for 0% -> 0% of each run, Pallas kernels for 9% -> 2%
where the time goes in v5:
time: 142 us; the launch traced here: 141 us
  blocking collectives  38.2 us (27%)
  starting transfers between devices  35.9 us (25%)
  waiting for transfers between devices  32.9 us (23%)
  Pallas kernels  30.7 us (22%)
  local copies, waits for them, and re-layouts  1.53 us (1%)
    ppermute x14, starting transfers between devices, per_device(): lax.ppermute(b, 'gx', perm_gx(*o))  32.3 us
    ppermute x14, waiting for transfers between devices, per_device(): lax.ppermute(b, 'gx', perm_gx(*o))  29.7 us
    all_to_all x1, blocking collectives, total_over_devices(): lax.all_to_all(half.reshape(64, 16, 128), both, 0, 0, axis_index_groups=S...  22.5 us
    pallas_call x1, Pallas kernels, finish(): pl.pallas_call(finish_kernel, out_shape=(jax.ShapeDtypeStruct((R, X), F32...  16 us
    all_to_all x1, blocking collectives, total_over_devices(): lax.all_to_all(jnp.broadcast_to(piece[None], (64, 16, 128)), both, 0, 0,...  15.7 us
    pallas_call x1, Pallas kernels, gram(): pl.pallas_call(gram_kernel, out_shape=(jax.ShapeDtypeStruct((HALF, 128),...  8.15 us
    pallas_call x2, Pallas kernels, pack(): pl.pallas_call(pack_kernel, grid=(2,), in_specs=[pl.BlockSpec((2, rows, 8...  6.58 us
    ppermute x1, starting transfers between devices, total_over_devices(): return (whole, lax.ppermute(whole, 'gx', perm_gx(0, 1)))  3.2 us
  transfers between devices with their start and end apart: 16, of which 9 were waited for; matrix products, arithmetic and copies ran while one was open for 0% of the time, Pallas kernels for 2%

profile of v5, /device:TPU:1, one launch (start us, length us, event | category | flops | bytes accessed | tf_op | source)
XLA Modules:
  0.0 141.5 jit_solution(9032102955362488519)
XLA Ops:
  0.6 3.3 %shard_map.42 = (f32[672,128]{1,0:T(8,128)}, f32[672,128]{1,0:T(8,128)}, f32[672,128]{1,0:T(8,128)}, f32[672,128]{1,0:T(8,128)}, f32[672,128]{1,0:T(8,128)}, /*i...) custom-call(f32[4,84,8,512]{3,2,1,0:T(8,128)} %species.3), custom_call_target="tpu_custom_call" | custom-call | flops 1048576 | bytes 5767168 | tf_op jit(solution)/shard_map/pallas_call | solution.py:261
  4.0 2.2 %collective-permute-start.7 = (f32[672,128]{1,0:T(8,128)}, f32[672,128]{1,0:T(8,128)S(1)}, u32[]{:S(2)}, u32[]{:S(2)}) collective-permute-start(f32[672,128]{1,0:T(8,128)} %get-tuple-element.30), channel_id=1, source_target_pairs={{0,32},{16,48},{32,64},{48,80},{64,96},{80,112},{96,0},{112,16},{1... | collective-permute-start | bytes 1032200 | tf_op jit(solution)/shard_map/ppermute | solution.py:277
  6.2 2.1 %collective-permute-start.8 = (f32[672,128]{1,0:T(8,128)}, f32[672,128]{1,0:T(8,128)S(1)}, u32[]{:S(2)}, u32[]{:S(2)}) collective-permute-start(f32[672,128]{1,0:T(8,128)} %get-tuple-element.31), channel_id=1, source_target_pairs={{0,112},{16,96},{32,16},{48,0},{64,48},{80,32},{96,80},{112,64},{1... | collective-permute-start | bytes 1032200 | tf_op jit(solution)/shard_map/ppermute | solution.py:277
  8.3 1.6 %collective-permute-start.9 = (f32[672,128]{1,0:T(8,128)}, f32[672,128]{1,0:T(8,128)S(1)}, u32[]{:S(2)}, u32[]{:S(2)}) collective-permute-start(f32[672,128]{1,0:T(8,128)} %get-tuple-element.32), channel_id=1, source_target_pairs={{0,96},{16,112},{32,0},{48,16},{64,32},{80,48},{96,64},{112,80},{1... | collective-permute-start | bytes 1032200 | tf_op jit(solution)/shard_map/ppermute | solution.py:277
  9.9 0.7 collective-permute-start.11
  10.7 3.3 %shard_map.41 = (f32[672,128]{1,0:T(8,128)}, f32[672,128]{1,0:T(8,128)}, f32[672,128]{1,0:T(8,128)}, f32[672,128]{1,0:T(8,128)}, f32[672,128]{1,0:T(8,128)}, /*i...) custom-call(f32[4,84,8,512]{3,2,1,0:T(8,128)} %species.3), custom_call_target="tpu_custom_call" | custom-call | flops 1048576 | bytes 5767168 | tf_op jit(solution)/shard_map/pallas_call | solution.py:261
  13.9 1.5 %collective-permute-done.7.refs_8_ = f32[672,128]{1,0:T(8,128)S(1)} collective-permute-done((f32[672,128]{1,0:T(8,128)}, f32[672,128]{1,0:T(8,128)S(1)}, u32[]{:S(2)}, u32[]{:S(2)}) %collective-permute-start.7) | collective-permute-done | bytes 344096 | tf_op jit(solution)/shard_map/ppermute | solution.py:277
  15.4 1.6 %collective-permute-start.12 = (f32[672,128]{1,0:T(8,128)S(1)}, f32[672,128]{1,0:T(8,128)S(1)}, u32[]{:S(2)}, u32[]{:S(2)}) collective-permute-start(f32[672,128]{1,0:T(8,128)S(1)} %copy-done.17), channel_id=1, source_target_pairs={{0,64},{16,80},{32,96},{48,112},{64,0},{80,16},{96,32},{112,48},{1... | collective-permute-start | bytes 1032200 | tf_op jit(solution)/shard_map/ppermute | solution.py:277
  17.4 2.8 %collective-permute-start.13 = (f32[672,128]{1,0:T(8,128)S(1)}, f32[672,128]{1,0:T(8,128)S(1)}, u32[]{:S(2)}, u32[]{:S(2)}) collective-permute-start(f32[672,128]{1,0:T(8,128)S(1)} %copy-done.16), channel_id=1, source_target_pairs={{0,48},{16,32},{32,80},{48,64},{64,112},{80,96},{96,16},{112,0},{1... | collective-permute-start | bytes 1032200 | tf_op jit(solution)/shard_map/ppermute | solution.py:277
  20.3 4.3 %collective-permute-done.9.refs_10_ = f32[672,128]{1,0:T(8,128)S(1)} collective-permute-done((f32[672,128]{1,0:T(8,128)}, f32[672,128]{1,0:T(8,128)S(1)}, u32[]{:S(2)}, u32[]{:S(2)}) %collective-permute-start.9) | collective-permute-done | bytes 344096 | tf_op jit(solution)/shard_map/ppermute | solution.py:277
  24.5 4.7 %collective-permute-start = (f32[672,128]{1,0:T(8,128)}, f32[672,128]{1,0:T(8,128)S(1)}, u32[]{:S(2)}, u32[]{:S(2)}) collective-permute-start(f32[672,128]{1,0:T(8,128)} %get-tuple-element.22), channel_id=1, source_target_pairs={{0,32},{16,48},{32,64},{48,80},{64,96},{80,112},{96,0},{112,16},{1... | collective-permute-start | bytes 1032200 | tf_op jit(solution)/shard_map/ppermute | solution.py:277
  29.2 3.6 %collective-permute-start.1 = (f32[672,128]{1,0:T(8,128)}, f32[672,128]{1,0:T(8,128)S(1)}, u32[]{:S(2)}, u32[]{:S(2)}) collective-permute-start(f32[672,128]{1,0:T(8,128)} %get-tuple-element.23), channel_id=1, source_target_pairs={{0,112},{16,96},{32,16},{48,0},{64,48},{80,32},{96,80},{112,64},{1... | collective-permute-start | bytes 1032200 | tf_op jit(solution)/shard_map/ppermute | solution.py:277
  32.8 1.5 %collective-permute-start.2 = (f32[672,128]{1,0:T(8,128)}, f32[672,128]{1,0:T(8,128)S(1)}, u32[]{:S(2)}, u32[]{:S(2)}) collective-permute-start(f32[672,128]{1,0:T(8,128)} %get-tuple-element.24), channel_id=1, source_target_pairs={{0,96},{16,112},{32,0},{48,16},{64,32},{80,48},{96,64},{112,80},{1... | collective-permute-start | bytes 1032200 | tf_op jit(solution)/shard_map/ppermute | solution.py:277
  34.3 3.4 %collective-permute-start.3 = (f32[672,128]{1,0:T(8,128)}, f32[672,128]{1,0:T(8,128)S(1)}, u32[]{:S(2)}, u32[]{:S(2)}) collective-permute-start(f32[672,128]{1,0:T(8,128)} %get-tuple-element.25), channel_id=1, source_target_pairs={{0,16},{16,0},{32,48},{48,32},{64,80},{80,64},{96,112},{112,96},{1... | collective-permute-start | bytes 1032200 | tf_op jit(solution)/shard_map/ppermute | solution.py:277
  37.7 5.9 %collective-permute-start.4 = (f32[672,128]{1,0:T(8,128)}, f32[672,128]{1,0:T(8,128)S(1)}, u32[]{:S(2)}, u32[]{:S(2)}) collective-permute-start(f32[672,128]{1,0:T(8,128)} %get-tuple-element.26), channel_id=1, source_target_pairs={{0,80},{16,64},{32,112},{48,96},{64,16},{80,0},{96,48},{112,32},{1... | collective-permute-start | bytes 1032200 | tf_op jit(solution)/shard_map/ppermute | solution.py:277
  43.6 3.2 %collective-permute-done.refs_0_ = f32[672,128]{1,0:T(8,128)S(1)} collective-permute-done((f32[672,128]{1,0:T(8,128)}, f32[672,128]{1,0:T(8,128)S(1)}, u32[]{:S(2)}, u32[]{:S(2)}) %collective-permute-start) | collective-permute-done | bytes 344096 | tf_op jit(solution)/shard_map/ppermute | solution.py:277
  46.8 0.8 collective-permute-start.5
  47.6 1.3 collective-permute-start.6
  48.9 5.2 %collective-permute-done.2.refs_2_ = f32[672,128]{1,0:T(8,128)S(1)} collective-permute-done((f32[672,128]{1,0:T(8,128)}, f32[672,128]{1,0:T(8,128)S(1)}, u32[]{:S(2)}, u32[]{:S(2)}) %collective-permute-start.2) | collective-permute-done | bytes 344096 | tf_op jit(solution)/shard_map/ppermute | solution.py:277
  54.1 8.4 %collective-permute-done.5.refs_5_ = f32[672,128]{1,0:T(8,128)S(1)} collective-permute-done((f32[672,128]{1,0:T(8,128)}, f32[672,128]{1,0:T(8,128)S(1)}, u32[]{:S(2)}, u32[]{:S(2)}) %collective-permute-start.5) | collective-permute-done | bytes 344096 | tf_op jit(solution)/shard_map/ppermute | solution.py:277
  62.5 6.7 %collective-permute-done.6.refs_6_ = f32[672,128]{1,0:T(8,128)S(1)} collective-permute-done((f32[672,128]{1,0:T(8,128)}, f32[672,128]{1,0:T(8,128)S(1)}, u32[]{:S(2)}, u32[]{:S(2)}) %collective-permute-start.6) | collective-permute-done | bytes 344096 | tf_op jit(solution)/shard_map/ppermute | solution.py:277
  69.3 0.6 copy-done.15
  70.0 8.2 %shard_map.43 = (f32[1024,128]{1,0:T(8,128)}, f32[1024,128]{1,0:T(8,128)}) custom-call(f32[672,128]{1,0:T(8,128)} %copy-done.9, f32[672,128]{1,0:T(8,128)} %copy-done.10, f32[672,128]{1,0:T(8,128)} %copy-done.11, f32[672,128]{1,0:T(8,128)} %copy-done.12, f32[672,128]{1,0:T(8,128)} %copy-done.13, f32[672,128]{1,0:T(8,128)} %copy-done.14, ...), custom_call_target="tpu_custom_call" | custom-call | flops 5549064192 | bytes 7340032 | tf_op jit(solution)/shard_map/pallas_call | solution.py:120
  78.1 0.5 collective-permute-start.14
  78.6 1.7 %collective-permute-done.14 = f32[1024,128]{1,0:T(8,128)S(1)} collective-permute-done((f32[1024,128]{1,0:T(8,128)}, f32[1024,128]{1,0:T(8,128)S(1)}, u32[]{:S(2)}, u32[]{:S(2)}) %collective-permute-start.14) | collective-permute-done | bytes 524320 | tf_op jit(solution)/shard_map/ppermute | solution.py:55
  80.4 1.1 add.3
  81.5 22.5 %all_to_all.10 = f32[64,16,128]{2,1,0:T(8,128)S(1)} all-to-all(f32[64,16,128]{2,1,0:T(8,128)S(1)} %bitcast.5), channel_id=1, replica_groups={{0,1,2,3,4,5,6,7,8,9,10,11,12,13,14,15,32,33,34,35,36,37,38,39,40,41,42..., dimensions={0} | all-to-all | bytes 1048576 | tf_op jit(solution)/shard_map/all_to_all | solution.py:57
  104.1 15.7 %all_to_all.11 = f32[64,16,128]{2,1,0:T(8,128)S(1)} all-to-all(f32[64,16,128]{2,1,0:T(8,128)S(1)} %broadcast_in_dim.2), channel_id=1, replica_groups={{0,1,2,3,4,5,6,7,8,9,10,11,12,13,14,15,32,33,34,35,36,37,38,39,40,41,42..., dimensions={0} | all-to-all | bytes 1048576 | tf_op jit(solution)/shard_map/all_to_all | solution.py:59
  119.8 3.2 %collective-permute-start.15 = (f32[1024,128]{1,0:T(8,128)S(1)}, f32[1024,128]{1,0:T(8,128)S(1)}, u32[]{:S(2)}, u32[]{:S(2)}) collective-permute-start(f32[1024,128]{1,0:T(8,128)S(1)} %bitcast.6), channel_id=1, source_target_pairs={{0,16},{16,0},{32,48},{48,32},{64,80},{80,64},{96,112},{112,96},{1... | collective-permute-start | bytes 1572872 | tf_op jit(solution)/shard_map/ppermute | solution.py:62
  123.0 1.5 %collective-permute-done.15.refs_17_ = f32[1024,128]{1,0:T(8,128)S(1)} collective-permute-done((f32[1024,128]{1,0:T(8,128)S(1)}, f32[1024,128]{1,0:T(8,128)S(1)}, u32[]{:S(2)}, u32[]{:S(2)}) %collective-permute-start.15) | collective-permute-done | bytes 524320 | tf_op jit(solution)/shard_map/ppermute | solution.py:62
  124.5 0.8 copy-done.1
  125.3 16.0 %shard_map.44 = (f32[96,672]{1,0:T(8,128)}, f32[4,8,64,96]{3,2,1,0:T(8,128)}) custom-call(f32[672,128]{1,0:T(8,128)} %copy-done.9, f32[672,128]{1,0:T(8,128)} %copy-done.10, f32[672,128]{1,0:T(8,128)} %copy-done.11, f32[672,128]{1,0:T(8,128)} %copy-done.12, f32[672,128]{1,0:T(8,128)} %copy-done.13, f32[672,128]{1,0:T(8,128)} %copy-done.14, ...), custom_call_target="tpu_custom_call" | custom-call | flops 792723456 | bytes 7340032 | tf_op jit(solution)/shard_map/pallas_call | solution.py:226
  (45 shorter events, 0.6 us)
Async XLA Ops:
  4.0 11.5 %copy-start.17 = (f32[672,128]{1,0:T(8,128)S(1)}, f32[672,128]{1,0:T(8,128)}, u32[]{:S(2)}) copy-start(f32[672,128]{1,0:T(8,128)} %get-tuple-element.35) | copy-start | bytes 1032196
  4.0 13.5 %copy-start.16 = (f32[672,128]{1,0:T(8,128)S(1)}, f32[672,128]{1,0:T(8,128)}, u32[]{:S(2)}) copy-start(f32[672,128]{1,0:T(8,128)} %get-tuple-element.36) | copy-start | bytes 1032196
  4.0 11.5 %collective-permute-start.7 = (f32[672,128]{1,0:T(8,128)}, f32[672,128]{1,0:T(8,128)S(1)}, u32[]{:S(2)}, u32[]{:S(2)}) collective-permute-start(f32[672,128]{1,0:T(8,128)} %get-tuple-element.30), channel_id=1, source_target_pairs={{0,32},{16,48},{32,64},{48,80},{64,96},{80,112},{96,0},{112,16},{1... | collective-permute-start | bytes 1032200 | tf_op jit(solution)/shard_map/ppermute | solution.py:277
  6.2 11.3 %collective-permute-start.8 = (f32[672,128]{1,0:T(8,128)}, f32[672,128]{1,0:T(8,128)S(1)}, u32[]{:S(2)}, u32[]{:S(2)}) collective-permute-start(f32[672,128]{1,0:T(8,128)} %get-tuple-element.31), channel_id=1, source_target_pairs={{0,112},{16,96},{32,16},{48,0},{64,48},{80,32},{96,80},{112,64},{1... | collective-permute-start | bytes 1032200 | tf_op jit(solution)/shard_map/ppermute | solution.py:277
  8.3 16.2 %collective-permute-start.9 = (f32[672,128]{1,0:T(8,128)}, f32[672,128]{1,0:T(8,128)S(1)}, u32[]{:S(2)}, u32[]{:S(2)}) collective-permute-start(f32[672,128]{1,0:T(8,128)} %get-tuple-element.32), channel_id=1, source_target_pairs={{0,96},{16,112},{32,0},{48,16},{64,32},{80,48},{96,64},{112,80},{1... | collective-permute-start | bytes 1032200 | tf_op jit(solution)/shard_map/ppermute | solution.py:277
  9.9 19.3 %collective-permute-start.10 = (f32[672,128]{1,0:T(8,128)}, f32[672,128]{1,0:T(8,128)S(1)}, u32[]{:S(2)}, u32[]{:S(2)}) collective-permute-start(f32[672,128]{1,0:T(8,128)} %get-tuple-element.33), channel_id=1, source_target_pairs={{0,16},{16,0},{32,48},{48,32},{64,80},{80,64},{96,112},{112,96},{1... | collective-permute-start | bytes 1032200 | tf_op jit(solution)/shard_map/ppermute | solution.py:277
  9.9 22.9 %collective-permute-start.11 = (f32[672,128]{1,0:T(8,128)}, f32[672,128]{1,0:T(8,128)S(1)}, u32[]{:S(2)}, u32[]{:S(2)}) collective-permute-start(f32[672,128]{1,0:T(8,128)} %get-tuple-element.34), channel_id=1, source_target_pairs={{0,80},{16,64},{32,112},{48,96},{64,16},{80,0},{96,48},{112,32},{1... | collective-permute-start | bytes 1032200 | tf_op jit(solution)/shard_map/ppermute | solution.py:277
  15.4 53.8 %copy-start.2 = (f32[672,128]{1,0:T(8,128)}, f32[672,128]{1,0:T(8,128)S(1)}, u32[]{:S(2)}) copy-start(f32[672,128]{1,0:T(8,128)S(1)} %collective-permute-done.7.refs_8_) | copy-start | bytes 1032196
  15.4 18.9 %collective-permute-start.12 = (f32[672,128]{1,0:T(8,128)S(1)}, f32[672,128]{1,0:T(8,128)S(1)}, u32[]{:S(2)}, u32[]{:S(2)}) collective-permute-start(f32[672,128]{1,0:T(8,128)S(1)} %copy-done.17), channel_id=1, source_target_pairs={{0,64},{16,80},{32,96},{48,112},{64,0},{80,16},{96,32},{112,48},{1... | collective-permute-start | bytes 1032200 | tf_op jit(solution)/shard_map/ppermute | solution.py:277
  17.4 51.8 %copy-start.3 = (f32[672,128]{1,0:T(8,128)}, f32[672,128]{1,0:T(8,128)S(1)}, u32[]{:S(2)}) copy-start(f32[672,128]{1,0:T(8,128)S(1)} %collective-permute-done.8.refs_9_) | copy-start | bytes 1032196
  17.4 20.3 %collective-permute-start.13 = (f32[672,128]{1,0:T(8,128)S(1)}, f32[672,128]{1,0:T(8,128)S(1)}, u32[]{:S(2)}, u32[]{:S(2)}) collective-permute-start(f32[672,128]{1,0:T(8,128)S(1)} %copy-done.16), channel_id=1, source_target_pairs={{0,48},{16,32},{32,80},{48,64},{64,112},{80,96},{96,16},{112,0},{1... | collective-permute-start | bytes 1032200 | tf_op jit(solution)/shard_map/ppermute | solution.py:277
  24.5 44.7 %copy-start.4 = (f32[672,128]{1,0:T(8,128)}, f32[672,128]{1,0:T(8,128)S(1)}, u32[]{:S(2)}) copy-start(f32[672,128]{1,0:T(8,128)S(1)} %collective-permute-done.9.refs_10_) | copy-start | bytes 1032196
  24.5 22.3 %collective-permute-start = (f32[672,128]{1,0:T(8,128)}, f32[672,128]{1,0:T(8,128)S(1)}, u32[]{:S(2)}, u32[]{:S(2)}) collective-permute-start(f32[672,128]{1,0:T(8,128)} %get-tuple-element.22), channel_id=1, source_target_pairs={{0,32},{16,48},{32,64},{48,80},{64,96},{80,112},{96,0},{112,16},{1... | collective-permute-start | bytes 1032200 | tf_op jit(solution)/shard_map/ppermute | solution.py:277
  29.2 40.0 %copy-start.5 = (f32[672,128]{1,0:T(8,128)}, f32[672,128]{1,0:T(8,128)S(1)}, u32[]{:S(2)}) copy-start(f32[672,128]{1,0:T(8,128)S(1)} %collective-permute-done.10.refs_11_) | copy-start | bytes 1032196
  29.2 18.4 %collective-permute-start.1 = (f32[672,128]{1,0:T(8,128)}, f32[672,128]{1,0:T(8,128)S(1)}, u32[]{:S(2)}, u32[]{:S(2)}) collective-permute-start(f32[672,128]{1,0:T(8,128)} %get-tuple-element.23), channel_id=1, source_target_pairs={{0,112},{16,96},{32,16},{48,0},{64,48},{80,32},{96,80},{112,64},{1... | collective-permute-start | bytes 1032200 | tf_op jit(solution)/shard_map/ppermute | solution.py:277
  32.8 36.4 %copy-start.6 = (f32[672,128]{1,0:T(8,128)}, f32[672,128]{1,0:T(8,128)S(1)}, u32[]{:S(2)}) copy-start(f32[672,128]{1,0:T(8,128)S(1)} %collective-permute-done.11.refs_12_) | copy-start | bytes 1032196
  32.8 21.2 %collective-permute-start.2 = (f32[672,128]{1,0:T(8,128)}, f32[672,128]{1,0:T(8,128)S(1)}, u32[]{:S(2)}, u32[]{:S(2)}) collective-permute-start(f32[672,128]{1,0:T(8,128)} %get-tuple-element.24), channel_id=1, source_target_pairs={{0,96},{16,112},{32,0},{48,16},{64,32},{80,48},{96,64},{112,80},{1... | collective-permute-start | bytes 1032200 | tf_op jit(solution)/shard_map/ppermute | solution.py:277
  34.3 34.9 %copy-start.7 = (f32[672,128]{1,0:T(8,128)}, f32[672,128]{1,0:T(8,128)S(1)}, u32[]{:S(2)}) copy-start(f32[672,128]{1,0:T(8,128)S(1)} %collective-permute-done.12.refs_13_) | copy-start | bytes 1032196
  34.3 19.7 %collective-permute-start.3 = (f32[672,128]{1,0:T(8,128)}, f32[672,128]{1,0:T(8,128)S(1)}, u32[]{:S(2)}, u32[]{:S(2)}) collective-permute-start(f32[672,128]{1,0:T(8,128)} %get-tuple-element.25), channel_id=1, source_target_pairs={{0,16},{16,0},{32,48},{48,32},{64,80},{80,64},{96,112},{112,96},{1... | collective-permute-start | bytes 1032200 | tf_op jit(solution)/shard_map/ppermute | solution.py:277
  37.7 31.6 %copy-start.8 = (f32[672,128]{1,0:T(8,128)}, f32[672,128]{1,0:T(8,128)S(1)}, u32[]{:S(2)}) copy-start(f32[672,128]{1,0:T(8,128)S(1)} %collective-permute-done.13.refs_14_) | copy-start | bytes 1032196
  37.7 16.4 %collective-permute-start.4 = (f32[672,128]{1,0:T(8,128)}, f32[672,128]{1,0:T(8,128)S(1)}, u32[]{:S(2)}, u32[]{:S(2)}) collective-permute-start(f32[672,128]{1,0:T(8,128)} %get-tuple-element.26), channel_id=1, source_target_pairs={{0,80},{16,64},{32,112},{48,96},{64,16},{80,0},{96,48},{112,32},{1... | collective-permute-start | bytes 1032200 | tf_op jit(solution)/shard_map/ppermute | solution.py:277
  46.8 22.5 %copy-start.9 = (f32[672,128]{1,0:T(8,128)}, f32[672,128]{1,0:T(8,128)S(1)}, u32[]{:S(2)}) copy-start(f32[672,128]{1,0:T(8,128)S(1)} %collective-permute-done.refs_0_) | copy-start | bytes 1032196
  46.8 15.7 %collective-permute-start.5 = (f32[672,128]{1,0:T(8,128)}, f32[672,128]{1,0:T(8,128)S(1)}, u32[]{:S(2)}, u32[]{:S(2)}) collective-permute-start(f32[672,128]{1,0:T(8,128)} %get-tuple-element.27), channel_id=1, source_target_pairs={{0,64},{16,80},{32,96},{48,112},{64,0},{80,16},{96,32},{112,48},{1... | collective-permute-start | bytes 1032200 | tf_op jit(solution)/shard_map/ppermute | solution.py:277
  47.6 21.7 %copy-start.10 = (f32[672,128]{1,0:T(8,128)}, f32[672,128]{1,0:T(8,128)S(1)}, u32[]{:S(2)}) copy-start(f32[672,128]{1,0:T(8,128)S(1)} %collective-permute-done.1.refs_1_) | copy-start | bytes 1032196
  47.6 21.6 %collective-permute-start.6 = (f32[672,128]{1,0:T(8,128)}, f32[672,128]{1,0:T(8,128)S(1)}, u32[]{:S(2)}, u32[]{:S(2)}) collective-permute-start(f32[672,128]{1,0:T(8,128)} %get-tuple-element.28), channel_id=1, source_target_pairs={{0,48},{16,32},{32,80},{48,64},{64,112},{80,96},{96,16},{112,0},{1... | collective-permute-start | bytes 1032200 | tf_op jit(solution)/shard_map/ppermute | solution.py:277
  54.1 15.2 %copy-start.11 = (f32[672,128]{1,0:T(8,128)}, f32[672,128]{1,0:T(8,128)S(1)}, u32[]{:S(2)}) copy-start(f32[672,128]{1,0:T(8,128)S(1)} %collective-permute-done.2.refs_2_) | copy-start | bytes 1032196
  54.1 15.2 %copy-start.12 = (f32[672,128]{1,0:T(8,128)}, f32[672,128]{1,0:T(8,128)S(1)}, u32[]{:S(2)}) copy-start(f32[672,128]{1,0:T(8,128)S(1)} %collective-permute-done.3.refs_3_) | copy-start | bytes 1032196
  54.1 15.2 %copy-start.13 = (f32[672,128]{1,0:T(8,128)}, f32[672,128]{1,0:T(8,128)S(1)}, u32[]{:S(2)}) copy-start(f32[672,128]{1,0:T(8,128)S(1)} %collective-permute-done.4.refs_4_) | copy-start | bytes 1032196
  62.5 6.8 %copy-start.14 = (f32[672,128]{1,0:T(8,128)}, f32[672,128]{1,0:T(8,128)S(1)}, u32[]{:S(2)}) copy-start(f32[672,128]{1,0:T(8,128)S(1)} %collective-permute-done.5.refs_5_) | copy-start | bytes 1032196
  78.1 2.2 %collective-permute-start.14 = (f32[1024,128]{1,0:T(8,128)}, f32[1024,128]{1,0:T(8,128)S(1)}, u32[]{:S(2)}, u32[]{:S(2)}) collective-permute-start(f32[1024,128]{1,0:T(8,128)} %get-tuple-element.39), channel_id=1, source_target_pairs={{0,16},{16,0},{32,48},{48,32},{64,80},{80,64},{96,112},{112,96},{1... | collective-permute-start | bytes 1572872 | tf_op jit(solution)/shard_map/ppermute | solution.py:55
  119.8 4.7 %copy-start = (f32[64,16,128]{2,1,0:T(8,128)}, f32[64,16,128]{2,1,0:T(8,128)S(1)}, u32[]{:S(2)}) copy-start(f32[64,16,128]{2,1,0:T(8,128)S(1)} %all_to_all.11) | copy-start | bytes 1572868
  119.8 4.7 %collective-permute-start.15 = (f32[1024,128]{1,0:T(8,128)S(1)}, f32[1024,128]{1,0:T(8,128)S(1)}, u32[]{:S(2)}, u32[]{:S(2)}) collective-permute-start(f32[1024,128]{1,0:T(8,128)S(1)} %bitcast.6), channel_id=1, source_target_pairs={{0,16},{16,0},{32,48},{48,32},{64,80},{80,64},{96,112},{112,96},{1... | collective-permute-start | bytes 1572872 | tf_op jit(solution)/shard_map/ppermute | solution.py:62
  (2 other events, 1.5 us)

commit v6 on v5

--- a/solution.py
+++ b/solution.py
@@ -1,3 +1,5 @@
+import functools
+
 import jax
 import jax.numpy as jnp
 from jax import lax
@@ -8,7 +10,7 @@
 X, R = 672, 96
 ROWS = 84
 BLOCK = 16
-OFFSETS = ((1, 0), (3, 1), (3, 0), (0, 1), (2, 1), (2, 0), (1, 1), (0, 0))
+OFFSETS = ((1, 0), (3, 0), (2, 0), (1, 1), (3, 1), (2, 1), (0, 1), (0, 0))
 HALF = 1024
 F32, BF16 = jnp.float32, jnp.bfloat16
 NN = (((1,), (0,)), ((), ()))
@@ -67,45 +69,42 @@
     return lax.div(me, 2), lax.rem(me, 2)
 
 
-def gathers(blocks, cells, sems):
+def row_starts():
     y, c = place()
-    copies = []
-    for i, (dy, dc) in enumerate(OFFSETS):
-        source = 2 * lax.rem(y + 4 - dy, 4) + lax.bitwise_xor(c, dc)
-        at = pl.ds(pl.multiple_of(source * 672, 672), 672)
-        copies += [pltpu.make_async_copy(blocks[8 * k + i], cells.at[k, at], sems.at[k, i]) for k in range(2)]
-    return copies[::2], copies[1::2]
-
-
-def gram_kernel(*refs):
-    blocks, (mine, other, cells, hi, lo, packed, sems) = refs[:16], refs[16:]
-    copies = gathers(blocks, cells, sems)
-    for k in range(2):
-        for copy in copies[k]:
-            copy.start()
-
-    def put(k, start, value):
+    sources = [2 * lax.rem(y + 4 - dy, 4) + lax.bitwise_xor(c, dc) for dy, dc in OFFSETS]
+    return [pl.ds(pl.multiple_of(source * 672, 672), 672) for source in sources]
+
+
+def gram_kernel(k, *refs):
+    blocks, refs = refs[:8], refs[8:]
+    if k:
+        before, mine, other, cells, hi, lo, packed = refs
+    else:
+        packed, cells, hi, lo = refs
+    for block, at in zip(blocks, row_starts()):
+        cells[at, :] = block[...]
+
+    def put(start, value):
         rows = slice(start, start + value.shape[0])
-        packed[rows, :] = packed[rows, :] + value if k else value
-
-    for k in range(2):
-        for copy in copies[k]:
-            copy.wait()
-        for q in range(8):
-            at = slice(128 * q, 128 * q + 128)
-            hi[k, :, at], lo[k, :, at] = split(cells[k, pl.ds(q, X, stride=8), :])
-        for j in range(3):
-            low, high = 256 * j, min(256 * j + 256, X)
-            g = dot3((hi[k, low:, :], lo[k, low:, :]), (hi[k, low:high, :], lo[k, low:high, :]), NT)
-            for t in (2 * j, 2 * j + 1):
-                col = g[128 * (t % 2) :, 128 * (t % 2) : 128 * (t % 2) + 128]
-                if t < 4:
-                    put(k, STARTS[t], col)
-                elif t == 4:
-                    put(k, STARTS[4], col[:128])
-                    put(k, 2 * HALF, col[128:160])
-                else:
-                    put(k, 2 * HALF + 32, jnp.concatenate([col, jnp.zeros((32, 96), F32)], axis=1))
+        packed[rows, :] = before[rows, :] + value if k else value
+
+    for q in range(8):
+        at = slice(128 * q, 128 * q + 128)
+        hi[:, at], lo[:, at] = split(cells[pl.ds(q, X, stride=8), :])
+    for j in range(3):
+        low, high = 256 * j, min(256 * j + 256, X)
+        g = dot3((hi[low:, :], lo[low:, :]), (hi[low:high, :], lo[low:high, :]), NT)
+        for t in (2 * j, 2 * j + 1):
+            col = g[128 * (t % 2) :, 128 * (t % 2) : 128 * (t % 2) + 128]
+            if t < 4:
+                put(STARTS[t], col)
+            elif t == 4:
+                put(STARTS[4], col[:128])
+                put(2 * HALF, col[128:160])
+            else:
+                put(2 * HALF + 32, jnp.concatenate([col, jnp.zeros((32, 96), F32)], axis=1))
+    if not k:
+        return
     packed[STARTS[1] : STARTS[1] + 32, 64:] = packed[2 * HALF : 2 * HALF + 32, :64]
     packed[STARTS[1] + 32 : STARTS[1] + 64, 64:] = packed[2 * HALF : 2 * HALF + 32, 64:]
     packed[0:32, 96:] = packed[2 * HALF + 32 : 2 * HALF + 64, :32]
@@ -114,24 +113,23 @@
         out[...] = packed[pl.ds(pl.multiple_of(half * HALF, HALF), HALF), :]
 
 
-def gram(blocks):
-    hbm = pl.BlockSpec(memory_space=pl.ANY)
+def gram(blocks, before):
+    k = len(before)
     vmem = pl.BlockSpec(memory_space=pltpu.VMEM)
+    out, half = ((2 * HALF + 64, 128), F32), jax.ShapeDtypeStruct((HALF, 128), F32)
     return pl.pallas_call(
-        gram_kernel,
-        out_shape=(jax.ShapeDtypeStruct((HALF, 128), F32),) * 2,
-        in_specs=[hbm] * 16,
-        out_specs=(vmem, vmem),
+        functools.partial(gram_kernel, k),
+        out_shape=(half, half) if k else (jax.ShapeDtypeStruct(*out),),
+        in_specs=[vmem] * (8 + k),
+        out_specs=(vmem,) * (1 + k),
         scratch_shapes=[
-            pltpu.VMEM((2, X * 8, 128), F32),
-            pltpu.VMEM((2, X, 1024), BF16),
-            pltpu.VMEM((2, X, 1024), BF16),
-            pltpu.VMEM((2 * HALF + 64, 128), F32),
-            pltpu.SemaphoreType.DMA((2, 8)),
-        ],
-        compiler_params=pltpu.CompilerParams(vmem_limit_bytes=VMEM_LIMIT),
-        cost_estimate=pl.CostEstimate(flops=3 * 2 * X * X * 2048, bytes_accessed=7 * 2**20, transcendentals=0),
-    )(*blocks)
+            pltpu.VMEM((X * 8, 128), F32),
+            pltpu.VMEM((X, 1024), BF16),
+            pltpu.VMEM((X, 1024), BF16),
+        ] + [pltpu.VMEM(*out)] * k,
+        compiler_params=pltpu.CompilerParams(vmem_limit_bytes=VMEM_LIMIT // 2),
+        cost_estimate=pl.CostEstimate(flops=3 * 2 * X * X * 1024, bytes_accessed=4 * 2**20, transcendentals=0),
+    )(*blocks, *before)
 
 
 def unpack(packed, g):
@@ -197,7 +195,10 @@
 
 def finish_kernel(*refs):
     blocks, (mine, other, basis, factor_t, core, packed, g, work, linv, cells, sems) = refs[:16], refs[16:]
-    copies = sum(gathers(blocks, cells, sems), [])
+    copies = [
+        pltpu.make_async_copy(blocks[8 * k + i], cells.at[k, at], sems.at[k, i])
+        for k in range(2) for i, at in enumerate(row_starts())
+    ]
     for copy in copies:
         copy.start()
     c = place()[1]
@@ -271,11 +272,13 @@
 
 def per_device(tensor, start_basis):
     basis_t = start_basis.T
-    blocks = []
+    blocks, grams = [], ()
     for k in range(2):
         packs = pack(tensor, k)
-        blocks += [lax.ppermute(b, "gx", perm_gx(*o)) for b, o in zip(packs[:7], OFFSETS)] + [packs[7]]
-    factor_t, core = finish(blocks, *total_over_devices(*gram(blocks)), basis_t)
+        part = [lax.ppermute(b, "gx", perm_gx(*o)) for b, o in zip(packs[:7], OFFSETS)] + [packs[7]]
+        grams = gram(part, grams)
+        blocks += part
+    factor_t, core = finish(blocks, *total_over_devices(*grams), basis_t)
     return factor_t.T, core.transpose(0, 3, 1, 2)
 
 

time: 142 us -> 135 us (0.951)
  waiting for transfers between devices: 32.9 us -> 26.9 us
  Pallas kernels: 30.7 us -> 28.3 us
  starting transfers between devices: 35.9 us -> 37.6 us
    ppermute x14, waiting for transfers between devices: 29.7 us -> 23.5 us  [per_device(): lax.ppermute(b, 'gx', perm_gx(*o))]
    pallas_call x1 -> x2, Pallas kernels: 8.15 us -> 5.79 us  [gram(): pl.pallas_call(functools.partial(gram_kernel, k), out_shape=(half, half)...]
    ppermute x14, starting transfers between devices: 32.3 us -> 34.4 us  [per_device(): lax.ppermute(b, 'gx', perm_gx(*o))]
  transfers between devices with their start and end apart: 16 -> 16, of which waited for: 9 -> 9; matrix products, arithmetic and copies ran while one was open for 0% -> 0% of each run, Pallas kernels for 2% -> 4%
where the time goes in v6:
time: 135 us
  blocking collectives  38.6 us (29%)
  starting transfers between devices  37.6 us (28%)
  Pallas kernels  28.3 us (21%)
  waiting for transfers between devices  26.9 us (20%)
  local copies, waits for them, and re-layouts  1.9 us (1%)
    ppermute x14, starting transfers between devices, per_device(): lax.ppermute(b, 'gx', perm_gx(*o))  34.4 us
    ppermute x14, waiting for transfers between devices, per_device(): lax.ppermute(b, 'gx', perm_gx(*o))  23.5 us
    all_to_all x1, blocking collectives, total_over_devices(): lax.all_to_all(half.reshape(64, 16, 128), both, 0, 0, axis_index_groups=S...  22.9 us
    pallas_call x1, Pallas kernels, finish(): pl.pallas_call(finish_kernel, out_shape=(jax.ShapeDtypeStruct((R, X), F32...  16 us
    all_to_all x1, blocking collectives, total_over_devices(): lax.all_to_all(jnp.broadcast_to(piece[None], (64, 16, 128)), both, 0, 0,...  15.7 us
    pallas_call x2, Pallas kernels, pack(): pl.pallas_call(pack_kernel, grid=(2,), in_specs=[pl.BlockSpec((2, rows, 8...  6.58 us
    pallas_call x2, Pallas kernels, gram(): pl.pallas_call(functools.partial(gram_kernel, k), out_shape=(half, half)...  5.79 us
    ppermute x1, starting transfers between devices, total_over_devices(): return (whole, lax.ppermute(whole, 'gx', perm_gx(0, 1)))  3.04 us
  transfers between devices with their start and end apart: 16, of which 9 were waited for; matrix products, arithmetic and copies ran while one was open for 0% of the time, Pallas kernels for 4%

profile of v6, /device:TPU:1, one launch (start us, length us, event | category | flops | bytes accessed | tf_op | source)
XLA Modules:
  0.0 134.5 jit_solution(8944905178389102378)
XLA Ops:
  0.6 3.3 %shard_map.42 = (f32[672,128]{1,0:T(8,128)}, f32[672,128]{1,0:T(8,128)}, f32[672,128]{1,0:T(8,128)}, f32[672,128]{1,0:T(8,128)}, f32[672,128]{1,0:T(8,128)}, /*i...) custom-call(f32[4,84,8,512]{3,2,1,0:T(8,128)} %species.3), custom_call_target="tpu_custom_call" | custom-call | flops 1048576 | bytes 5767168 | tf_op jit(solution)/shard_map/pallas_call | solution.py:262
  4.0 2.2 %collective-permute-start.7 = (f32[672,128]{1,0:T(8,128)}, f32[672,128]{1,0:T(8,128)S(1)}, u32[]{:S(2)}, u32[]{:S(2)}) collective-permute-start(f32[672,128]{1,0:T(8,128)} %get-tuple-element.30), channel_id=1, source_target_pairs={{0,32},{16,48},{32,64},{48,80},{64,96},{80,112},{96,0},{112,16},{1... | collective-permute-start | bytes 1032200 | tf_op jit(solution)/shard_map/ppermute | solution.py:278
  6.2 1.5 %collective-permute-start.8 = (f32[672,128]{1,0:T(8,128)}, f32[672,128]{1,0:T(8,128)S(1)}, u32[]{:S(2)}, u32[]{:S(2)}) collective-permute-start(f32[672,128]{1,0:T(8,128)} %get-tuple-element.31), channel_id=1, source_target_pairs={{0,96},{16,112},{32,0},{48,16},{64,32},{80,48},{96,64},{112,80},{1... | collective-permute-start | bytes 1032200 | tf_op jit(solution)/shard_map/ppermute | solution.py:278
  7.7 3.3 %shard_map.41 = (f32[672,128]{1,0:T(8,128)}, f32[672,128]{1,0:T(8,128)}, f32[672,128]{1,0:T(8,128)}, f32[672,128]{1,0:T(8,128)}, f32[672,128]{1,0:T(8,128)}, /*i...) custom-call(f32[4,84,8,512]{3,2,1,0:T(8,128)} %species.3), custom_call_target="tpu_custom_call" | custom-call | flops 1048576 | bytes 5767168 | tf_op jit(solution)/shard_map/pallas_call | solution.py:262
  11.0 0.1 collective-permute-start
  11.1 2.7 %collective-permute-start.1 = (f32[672,128]{1,0:T(8,128)}, f32[672,128]{1,0:T(8,128)S(1)}, u32[]{:S(2)}, u32[]{:S(2)}) collective-permute-start(f32[672,128]{1,0:T(8,128)} %get-tuple-element.23), channel_id=1, source_target_pairs={{0,96},{16,112},{32,0},{48,16},{64,32},{80,48},{96,64},{112,80},{1... | collective-permute-start | bytes 1032200 | tf_op jit(solution)/shard_map/ppermute | solution.py:278
  13.7 0.3 collective-permute-start.2
  14.1 1.4 %collective-permute-done.7.refs_0_.refs_8_ = f32[672,128]{1,0:T(8,128)S(1)} collective-permute-done((f32[672,128]{1,0:T(8,128)}, f32[672,128]{1,0:T(8,128)S(1)}, u32[]{:S(2)}, u32[]{:S(2)}) %collective-permute-start.7) | collective-permute-done | bytes 344096 | tf_op jit(solution)/shard_map/ppermute | solution.py:278
  15.5 2.4 %collective-permute-start.3 = (f32[672,128]{1,0:T(8,128)}, f32[672,128]{1,0:T(8,128)S(1)}, u32[]{:S(2)}, u32[]{:S(2)}) collective-permute-start(f32[672,128]{1,0:T(8,128)} %get-tuple-element.25), channel_id=1, source_target_pairs={{0,48},{16,32},{32,80},{48,64},{64,112},{80,96},{96,16},{112,0},{1... | collective-permute-start | bytes 1032200 | tf_op jit(solution)/shard_map/ppermute | solution.py:278
  17.9 2.8 %collective-permute-start.4 = (f32[672,128]{1,0:T(8,128)}, f32[672,128]{1,0:T(8,128)S(1)}, u32[]{:S(2)}, u32[]{:S(2)}) collective-permute-start(f32[672,128]{1,0:T(8,128)} %get-tuple-element.26), channel_id=1, source_target_pairs={{0,112},{16,96},{32,16},{48,0},{64,48},{80,32},{96,80},{112,64},{1... | collective-permute-start | bytes 1032200 | tf_op jit(solution)/shard_map/ppermute | solution.py:278
  20.7 2.1 %collective-permute-done.refs_0_ = f32[672,128]{1,0:T(8,128)S(1)} collective-permute-done((f32[672,128]{1,0:T(8,128)}, f32[672,128]{1,0:T(8,128)S(1)}, u32[]{:S(2)}, u32[]{:S(2)}) %collective-permute-start) | collective-permute-done | bytes 344096 | tf_op jit(solution)/shard_map/ppermute | solution.py:278
  22.8 11.4 %collective-permute-start.5 = (f32[672,128]{1,0:T(8,128)}, f32[672,128]{1,0:T(8,128)S(1)}, u32[]{:S(2)}, u32[]{:S(2)}) collective-permute-start(f32[672,128]{1,0:T(8,128)} %get-tuple-element.27), channel_id=1, source_target_pairs={{0,80},{16,64},{32,112},{48,96},{64,16},{80,0},{96,48},{112,32},{1... | collective-permute-start | bytes 1032200 | tf_op jit(solution)/shard_map/ppermute | solution.py:278
  34.3 0.3 collective-permute-start.9
  34.6 3.7 %collective-permute-done.3.refs_3_ = f32[672,128]{1,0:T(8,128)S(1)} collective-permute-done((f32[672,128]{1,0:T(8,128)}, f32[672,128]{1,0:T(8,128)S(1)}, u32[]{:S(2)}, u32[]{:S(2)}) %collective-permute-start.3) | collective-permute-done | bytes 344096 | tf_op jit(solution)/shard_map/ppermute | solution.py:278
  38.3 0.9 collective-permute-start.10
  39.2 1.0 collective-permute-done.4.refs_4_
  40.1 1.2 collective-permute-start.11
  41.3 6.8 %collective-permute-done.5.refs_5_ = f32[672,128]{1,0:T(8,128)S(1)} collective-permute-done((f32[672,128]{1,0:T(8,128)}, f32[672,128]{1,0:T(8,128)S(1)}, u32[]{:S(2)}, u32[]{:S(2)}) %collective-permute-start.5) | collective-permute-done | bytes 344096 | tf_op jit(solution)/shard_map/ppermute | solution.py:278
  48.2 8.6 %collective-permute-start.13 = (f32[672,128]{1,0:T(8,128)S(1)}, f32[672,128]{1,0:T(8,128)S(1)}, u32[]{:S(2)}, u32[]{:S(2)}) collective-permute-start(f32[672,128]{1,0:T(8,128)S(1)} %copy-done.18), channel_id=1, source_target_pairs={{0,16},{16,0},{32,48},{48,32},{64,80},{80,64},{96,112},{112,96},{1... | collective-permute-start | bytes 1032200 | tf_op jit(solution)/shard_map/ppermute | solution.py:278
  56.8 1.0 copy-done.3
  57.8 2.8 %shard_map.43.refs_8_ = f32[2112,128]{1,0:T(8,128)S(1)} custom-call(f32[672,128]{1,0:T(8,128)S(1)} %collective-permute-done.refs_0_, f32[672,128]{1,0:T(8,128)S(1)} %collective-permute-done.1.refs_1_, f32[672,128]{1,0:T(8,128)S(1)} %collective-permute-done.2.refs_2_, f32[672,128]{1,0:T(8,128)S(1)} %collective-permute-done.3.refs_3_, ...), custom_call_target="tpu_custom_call" | custom-call | flops 2774532096 | bytes 4194304 | tf_op jit(solution)/shard_map/pallas_call | solution.py:120
  60.6 2.4 %collective-permute-done.10.refs_3_.refs_11_ = f32[672,128]{1,0:T(8,128)S(1)} collective-permute-done((f32[672,128]{1,0:T(8,128)S(1)}, f32[672,128]{1,0:T(8,128)S(1)}, u32[]{:S(2)}, u32[]{:S(2)}) %collective-permute-start.10) | collective-permute-done | bytes 344096 | tf_op jit(solution)/shard_map/ppermute | solution.py:278
  63.0 6.0 %collective-permute-done.12.refs_5_.refs_13_ = f32[672,128]{1,0:T(8,128)S(1)} collective-permute-done((f32[672,128]{1,0:T(8,128)S(1)}, f32[672,128]{1,0:T(8,128)S(1)}, u32[]{:S(2)}, u32[]{:S(2)}) %collective-permute-start.12) | collective-permute-done | bytes 344096 | tf_op jit(solution)/shard_map/ppermute | solution.py:278
  69.1 3.0 %shard_map.44 = (f32[1024,128]{1,0:T(8,128)S(1)}, f32[1024,128]{1,0:T(8,128)S(1)}) custom-call(f32[672,128]{1,0:T(8,128)S(1)} %collective-permute-done.7.refs_0_.refs_8_, f32[672,128]{1,0:T(8,128)S(1)} %collective-permute-done.8.refs_1_.refs_9_, f32[672,128]{1,0:T(8,128)S(1)} %collective-permute-done.9.refs_2_.refs_10_, ...), custom_call_target="tpu_custom_call" | custom-call | flops 2774532096 | bytes 4194304 | tf_op jit(solution)/shard_map/pallas_call | solution.py:120
  72.2 0.1 collective-permute-start.14
  72.3 1.9 %collective-permute-done.14 = f32[1024,128]{1,0:T(8,128)S(1)} collective-permute-done((f32[1024,128]{1,0:T(8,128)S(1)}, f32[1024,128]{1,0:T(8,128)S(1)}, u32[]{:S(2)}, u32[]{:S(2)}) %collective-permute-start.14) | collective-permute-done | bytes 524320 | tf_op jit(solution)/shard_map/ppermute | solution.py:57
  74.3 22.9 %all_to_all.10 = f32[64,16,128]{2,1,0:T(8,128)S(1)} all-to-all(f32[64,16,128]{2,1,0:T(8,128)S(1)} %bitcast.5), channel_id=1, replica_groups={{0,1,2,3,4,5,6,7,8,9,10,11,12,13,14,15,32,33,34,35,36,37,38,39,40,41,42..., dimensions={0} | all-to-all | bytes 1048576 | tf_op jit(solution)/shard_map/all_to_all | solution.py:59
  97.3 15.7 %all_to_all.11 = f32[64,16,128]{2,1,0:T(8,128)S(1)} all-to-all(f32[64,16,128]{2,1,0:T(8,128)S(1)} %broadcast_in_dim.2), channel_id=1, replica_groups={{0,1,2,3,4,5,6,7,8,9,10,11,12,13,14,15,32,33,34,35,36,37,38,39,40,41,42..., dimensions={0} | all-to-all | bytes 1048576 | tf_op jit(solution)/shard_map/all_to_all | solution.py:61
  113.0 3.0 %collective-permute-start.15 = (f32[1024,128]{1,0:T(8,128)S(1)}, f32[1024,128]{1,0:T(8,128)S(1)}, u32[]{:S(2)}, u32[]{:S(2)}) collective-permute-start(f32[1024,128]{1,0:T(8,128)S(1)} %bitcast.6), channel_id=1, source_target_pairs={{0,16},{16,0},{32,48},{48,32},{64,80},{80,64},{96,112},{112,96},{1... | collective-permute-start | bytes 1572872 | tf_op jit(solution)/shard_map/ppermute | solution.py:64
  116.1 1.5 %collective-permute-done.15.refs_17_ = f32[1024,128]{1,0:T(8,128)S(1)} collective-permute-done((f32[1024,128]{1,0:T(8,128)S(1)}, f32[1024,128]{1,0:T(8,128)S(1)}, u32[]{:S(2)}, u32[]{:S(2)}) %collective-permute-start.15) | collective-permute-done | bytes 524320 | tf_op jit(solution)/shard_map/ppermute | solution.py:64
  117.6 0.8 copy-done.17
  118.4 16.0 %shard_map.45 = (f32[96,672]{1,0:T(8,128)}, f32[4,8,64,96]{3,2,1,0:T(8,128)}) custom-call(f32[672,128]{1,0:T(8,128)} %copy-done.4, f32[672,128]{1,0:T(8,128)} %copy-done.5, f32[672,128]{1,0:T(8,128)} %copy-done.6, f32[672,128]{1,0:T(8,128)} %copy-done.7, f32[672,128]{1,0:T(8,128)} %copy-done.8, f32[672,128]{1,0:T(8,128)} %copy-done.9, ...), custom_call_target="tpu_custom_call" | custom-call | flops 792723456 | bytes 7340032 | tf_op jit(solution)/shard_map/pallas_call | solution.py:227
  (56 shorter events, 0.3 us)
Async XLA Ops:
  4.0 30.4 %copy-start.22 = (f32[672,128]{1,0:T(8,128)S(1)}, f32[672,128]{1,0:T(8,128)}, u32[]{:S(2)}) copy-start(f32[672,128]{1,0:T(8,128)} %get-tuple-element.32) | copy-start | bytes 1032196
  4.0 34.3 %copy-start.21 = (f32[672,128]{1,0:T(8,128)S(1)}, f32[672,128]{1,0:T(8,128)}, u32[]{:S(2)}) copy-start(f32[672,128]{1,0:T(8,128)} %get-tuple-element.33) | copy-start | bytes 1032196
  4.0 36.2 %copy-start.20 = (f32[672,128]{1,0:T(8,128)S(1)}, f32[672,128]{1,0:T(8,128)}, u32[]{:S(2)}) copy-start(f32[672,128]{1,0:T(8,128)} %get-tuple-element.34) | copy-start | bytes 1032196
  4.0 44.1 %copy-start.19 = (f32[672,128]{1,0:T(8,128)S(1)}, f32[672,128]{1,0:T(8,128)}, u32[]{:S(2)}) copy-start(f32[672,128]{1,0:T(8,128)} %get-tuple-element.35) | copy-start | bytes 1032196
  4.0 44.2 %copy-start.18 = (f32[672,128]{1,0:T(8,128)S(1)}, f32[672,128]{1,0:T(8,128)}, u32[]{:S(2)}) copy-start(f32[672,128]{1,0:T(8,128)} %get-tuple-element.36) | copy-start | bytes 1032196
  4.0 11.5 %collective-permute-start.7 = (f32[672,128]{1,0:T(8,128)}, f32[672,128]{1,0:T(8,128)S(1)}, u32[]{:S(2)}, u32[]{:S(2)}) collective-permute-start(f32[672,128]{1,0:T(8,128)} %get-tuple-element.30), channel_id=1, source_target_pairs={{0,32},{16,48},{32,64},{48,80},{64,96},{80,112},{96,0},{112,16},{1... | collective-permute-start | bytes 1032200 | tf_op jit(solution)/shard_map/ppermute | solution.py:278
  6.2 11.7 %collective-permute-start.8 = (f32[672,128]{1,0:T(8,128)}, f32[672,128]{1,0:T(8,128)S(1)}, u32[]{:S(2)}, u32[]{:S(2)}) collective-permute-start(f32[672,128]{1,0:T(8,128)} %get-tuple-element.31), channel_id=1, source_target_pairs={{0,96},{16,112},{32,0},{48,16},{64,32},{80,48},{96,64},{112,80},{1... | collective-permute-start | bytes 1032200 | tf_op jit(solution)/shard_map/ppermute | solution.py:278
  11.0 58.1 %copy-start = (f32[672,128]{1,0:T(8,128)S(1)}, f32[672,128]{1,0:T(8,128)}, u32[]{:S(2)}) copy-start(f32[672,128]{1,0:T(8,128)} %get-tuple-element.37.refs_7_.refs_15_) | copy-start | bytes 1032196
  11.0 11.9 %collective-permute-start = (f32[672,128]{1,0:T(8,128)}, f32[672,128]{1,0:T(8,128)S(1)}, u32[]{:S(2)}, u32[]{:S(2)}) collective-permute-start(f32[672,128]{1,0:T(8,128)} %get-tuple-element.22), channel_id=1, source_target_pairs={{0,32},{16,48},{32,64},{48,80},{64,96},{80,112},{96,0},{112,16},{1... | collective-permute-start | bytes 1032200 | tf_op jit(solution)/shard_map/ppermute | solution.py:278
  11.1 23.2 %collective-permute-start.1 = (f32[672,128]{1,0:T(8,128)}, f32[672,128]{1,0:T(8,128)S(1)}, u32[]{:S(2)}, u32[]{:S(2)}) collective-permute-start(f32[672,128]{1,0:T(8,128)} %get-tuple-element.23), channel_id=1, source_target_pairs={{0,96},{16,112},{32,0},{48,16},{64,32},{80,48},{96,64},{112,80},{1... | collective-permute-start | bytes 1032200 | tf_op jit(solution)/shard_map/ppermute | solution.py:278
  13.7 20.6 %collective-permute-start.2 = (f32[672,128]{1,0:T(8,128)}, f32[672,128]{1,0:T(8,128)S(1)}, u32[]{:S(2)}, u32[]{:S(2)}) collective-permute-start(f32[672,128]{1,0:T(8,128)} %get-tuple-element.24), channel_id=1, source_target_pairs={{0,64},{16,80},{32,96},{48,112},{64,0},{80,16},{96,32},{112,48},{1... | collective-permute-start | bytes 1032200 | tf_op jit(solution)/shard_map/ppermute | solution.py:278
  15.5 56.6 %copy-start.1 = (f32[672,128]{1,0:T(8,128)}, f32[672,128]{1,0:T(8,128)S(1)}, u32[]{:S(2)}) copy-start(f32[672,128]{1,0:T(8,128)S(1)} %collective-permute-done.7.refs_0_.refs_8_) | copy-start | bytes 1032196
  15.5 22.8 %collective-permute-start.3 = (f32[672,128]{1,0:T(8,128)}, f32[672,128]{1,0:T(8,128)S(1)}, u32[]{:S(2)}, u32[]{:S(2)}) collective-permute-start(f32[672,128]{1,0:T(8,128)} %get-tuple-element.25), channel_id=1, source_target_pairs={{0,48},{16,32},{32,80},{48,64},{64,112},{80,96},{96,16},{112,0},{1... | collective-permute-start | bytes 1032200 | tf_op jit(solution)/shard_map/ppermute | solution.py:278
  17.9 54.2 %copy-start.2 = (f32[672,128]{1,0:T(8,128)}, f32[672,128]{1,0:T(8,128)S(1)}, u32[]{:S(2)}) copy-start(f32[672,128]{1,0:T(8,128)S(1)} %collective-permute-done.8.refs_1_.refs_9_) | copy-start | bytes 1032196
  17.9 22.2 %collective-permute-start.4 = (f32[672,128]{1,0:T(8,128)}, f32[672,128]{1,0:T(8,128)S(1)}, u32[]{:S(2)}, u32[]{:S(2)}) collective-permute-start(f32[672,128]{1,0:T(8,128)} %get-tuple-element.26), channel_id=1, source_target_pairs={{0,112},{16,96},{32,16},{48,0},{64,48},{80,32},{96,80},{112,64},{1... | collective-permute-start | bytes 1032200 | tf_op jit(solution)/shard_map/ppermute | solution.py:278
  22.8 49.3 %copy-start.4 = (f32[672,128]{1,0:T(8,128)}, f32[672,128]{1,0:T(8,128)S(1)}, u32[]{:S(2)}) copy-start(f32[672,128]{1,0:T(8,128)S(1)} %collective-permute-done.refs_0_) | copy-start | bytes 1032196
  22.8 25.3 %collective-permute-start.5 = (f32[672,128]{1,0:T(8,128)}, f32[672,128]{1,0:T(8,128)S(1)}, u32[]{:S(2)}, u32[]{:S(2)}) collective-permute-start(f32[672,128]{1,0:T(8,128)} %get-tuple-element.27), channel_id=1, source_target_pairs={{0,80},{16,64},{32,112},{48,96},{64,16},{80,0},{96,48},{112,32},{1... | collective-permute-start | bytes 1032200 | tf_op jit(solution)/shard_map/ppermute | solution.py:278
  34.3 37.8 %copy-start.5 = (f32[672,128]{1,0:T(8,128)}, f32[672,128]{1,0:T(8,128)S(1)}, u32[]{:S(2)}) copy-start(f32[672,128]{1,0:T(8,128)S(1)} %collective-permute-done.1.refs_1_) | copy-start | bytes 1032196
  34.3 13.9 %collective-permute-start.6 = (f32[672,128]{1,0:T(8,128)}, f32[672,128]{1,0:T(8,128)S(1)}, u32[]{:S(2)}, u32[]{:S(2)}) collective-permute-start(f32[672,128]{1,0:T(8,128)} %get-tuple-element.28), channel_id=1, source_target_pairs={{0,16},{16,0},{32,48},{48,32},{64,80},{80,64},{96,112},{112,96},{1... | collective-permute-start | bytes 1032200 | tf_op jit(solution)/shard_map/ppermute | solution.py:278
  34.3 37.8 %copy-start.6 = (f32[672,128]{1,0:T(8,128)}, f32[672,128]{1,0:T(8,128)S(1)}, u32[]{:S(2)}) copy-start(f32[672,128]{1,0:T(8,128)S(1)} %collective-permute-done.2.refs_2_) | copy-start | bytes 1032196
  34.3 26.2 %collective-permute-start.9 = (f32[672,128]{1,0:T(8,128)S(1)}, f32[672,128]{1,0:T(8,128)S(1)}, u32[]{:S(2)}, u32[]{:S(2)}) collective-permute-start(f32[672,128]{1,0:T(8,128)S(1)} %copy-done.22), channel_id=1, source_target_pairs={{0,64},{16,80},{32,96},{48,112},{64,0},{80,16},{96,32},{112,48},{1... | collective-permute-start | bytes 1032200 | tf_op jit(solution)/shard_map/ppermute | solution.py:278
  38.3 33.8 %copy-start.7 = (f32[672,128]{1,0:T(8,128)}, f32[672,128]{1,0:T(8,128)S(1)}, u32[]{:S(2)}) copy-start(f32[672,128]{1,0:T(8,128)S(1)} %collective-permute-done.3.refs_3_) | copy-start | bytes 1032196
  38.3 24.7 %collective-permute-start.10 = (f32[672,128]{1,0:T(8,128)S(1)}, f32[672,128]{1,0:T(8,128)S(1)}, u32[]{:S(2)}, u32[]{:S(2)}) collective-permute-start(f32[672,128]{1,0:T(8,128)S(1)} %copy-done.21), channel_id=1, source_target_pairs={{0,48},{16,32},{32,80},{48,64},{64,112},{80,96},{96,16},{112,0},{1... | collective-permute-start | bytes 1032200 | tf_op jit(solution)/shard_map/ppermute | solution.py:278
  40.1 32.0 %copy-start.8 = (f32[672,128]{1,0:T(8,128)}, f32[672,128]{1,0:T(8,128)S(1)}, u32[]{:S(2)}) copy-start(f32[672,128]{1,0:T(8,128)S(1)} %collective-permute-done.4.refs_4_) | copy-start | bytes 1032196
  40.1 22.9 %collective-permute-start.11 = (f32[672,128]{1,0:T(8,128)S(1)}, f32[672,128]{1,0:T(8,128)S(1)}, u32[]{:S(2)}, u32[]{:S(2)}) collective-permute-start(f32[672,128]{1,0:T(8,128)S(1)} %copy-done.20), channel_id=1, source_target_pairs={{0,112},{16,96},{32,16},{48,0},{64,48},{80,32},{96,80},{112,64},{1... | collective-permute-start | bytes 1032200 | tf_op jit(solution)/shard_map/ppermute | solution.py:278
  48.1 24.0 %copy-start.9 = (f32[672,128]{1,0:T(8,128)}, f32[672,128]{1,0:T(8,128)S(1)}, u32[]{:S(2)}) copy-start(f32[672,128]{1,0:T(8,128)S(1)} %collective-permute-done.5.refs_5_) | copy-start | bytes 1032196
  48.1 20.9 %collective-permute-start.12 = (f32[672,128]{1,0:T(8,128)S(1)}, f32[672,128]{1,0:T(8,128)S(1)}, u32[]{:S(2)}, u32[]{:S(2)}) collective-permute-start(f32[672,128]{1,0:T(8,128)S(1)} %copy-done.19), channel_id=1, source_target_pairs={{0,80},{16,64},{32,112},{48,96},{64,16},{80,0},{96,48},{112,32},{1... | collective-permute-start | bytes 1032200 | tf_op jit(solution)/shard_map/ppermute | solution.py:278
  48.1 24.0 %copy-start.10 = (f32[672,128]{1,0:T(8,128)}, f32[672,128]{1,0:T(8,128)S(1)}, u32[]{:S(2)}) copy-start(f32[672,128]{1,0:T(8,128)S(1)} %collective-permute-done.6.refs_6_) | copy-start | bytes 1032196
  48.2 20.9 %collective-permute-start.13 = (f32[672,128]{1,0:T(8,128)S(1)}, f32[672,128]{1,0:T(8,128)S(1)}, u32[]{:S(2)}, u32[]{:S(2)}) collective-permute-start(f32[672,128]{1,0:T(8,128)S(1)} %copy-done.18), channel_id=1, source_target_pairs={{0,16},{16,0},{32,48},{48,32},{64,80},{80,64},{96,112},{112,96},{1... | collective-permute-start | bytes 1032200 | tf_op jit(solution)/shard_map/ppermute | solution.py:278
  60.6 13.6 %copy-start.11 = (f32[672,128]{1,0:T(8,128)}, f32[672,128]{1,0:T(8,128)S(1)}, u32[]{:S(2)}) copy-start(f32[672,128]{1,0:T(8,128)S(1)} %collective-permute-done.9.refs_2_.refs_10_) | copy-start | bytes 1032196
  72.2 2.0 %collective-permute-start.14 = (f32[1024,128]{1,0:T(8,128)S(1)}, f32[1024,128]{1,0:T(8,128)S(1)}, u32[]{:S(2)}, u32[]{:S(2)}) collective-permute-start(f32[1024,128]{1,0:T(8,128)S(1)} %get-tuple-element.39), channel_id=1, source_target_pairs={{0,16},{16,0},{32,48},{48,32},{64,80},{80,64},{96,112},{112,96},{1... | collective-permute-start | bytes 1572872 | tf_op jit(solution)/shard_map/ppermute | solution.py:57
  113.0 4.6 %collective-permute-start.15 = (f32[1024,128]{1,0:T(8,128)S(1)}, f32[1024,128]{1,0:T(8,128)S(1)}, u32[]{:S(2)}, u32[]{:S(2)}) collective-permute-start(f32[1024,128]{1,0:T(8,128)S(1)} %bitcast.6), channel_id=1, source_target_pairs={{0,16},{16,0},{32,48},{48,32},{64,80},{80,64},{96,112},{112,96},{1... | collective-permute-start | bytes 1572872 | tf_op jit(solution)/shard_map/ppermute | solution.py:64
  (7 other events, 39.2 us)

commit v7 on v6

--- a/solution.py
+++ b/solution.py
@@ -215,10 +215,13 @@
     for copy in copies:
         copy.wait()
     for k in range(2):
-        for y in range(8):
-            value = dot3(f, split(cells[k, pl.ds(y, X, stride=8), :]), NN).T
-            core[2 * k, y] = value[:64]
-            core[2 * k + 1, y] = value[64:]
+        for p in range(4):
+            cell = jnp.concatenate([cells[k, pl.ds(2 * p + q, X, stride=8), :] for q in range(2)], axis=1)
+            value = dot3(f, split(cell), NN)
+            for q in range(2):
+                part = value[:, 128 * q : 128 * q + 128].T
+                core[2 * k, 2 * p + q] = part[:64]
+                core[2 * k + 1, 2 * p + q] = part[64:]
 
 
 def finish(blocks, mine, other, basis_t):
@@ -242,29 +245,28 @@
     )(*blocks, mine, other, basis_t)
 
 
-def pack_kernel(species, *outs):
+def pack_kernel(wanted, species, *outs):
     rows = outs[0].shape[0]
     first = lax.broadcasted_iota(jnp.int32, (rows, 128), 1) < 64
     y, c = place()
     even = c == 0
-    for dy in range(4):
+    for (dy, dc), out in zip(wanted, outs):
         at = pl.ds(pl.multiple_of(lax.rem(y + dy, 4) * 128, 128), 128)
         a, b = (species[q, :, :, at].reshape(rows, 128) for q in range(2))
         low = jnp.where(first, a, pltpu.roll(b, 64, 1))
         high = jnp.where(first, pltpu.roll(a, 64, 1), b)
-        outs[OFFSETS.index((dy, 0))][...] = jnp.where(even, low, high)
-        outs[OFFSETS.index((dy, 1))][...] = jnp.where(even, high, low)
-
-
-def pack(tensor, k):
+        out[...] = jnp.where(even, high, low) if dc else jnp.where(even, low, high)
+
+
+def pack(tensor, k, wanted):
     rows = ROWS // 2
     out = pl.BlockSpec((rows * 8, 128), lambda i: (i, 0))
     return pl.pallas_call(
-        pack_kernel,
+        functools.partial(pack_kernel, wanted),
         grid=(2,),
         in_specs=[pl.BlockSpec((2, rows, 8, 512), lambda i: (k, i, 0, 0))],
-        out_specs=(out,) * 8,
-        out_shape=(jax.ShapeDtypeStruct((ROWS * 8, 128), F32),) * 8,
+        out_specs=(out,) * len(wanted),
+        out_shape=(jax.ShapeDtypeStruct((ROWS * 8, 128), F32),) * len(wanted),
         compiler_params=pltpu.CompilerParams(vmem_limit_bytes=VMEM_LIMIT),
         cost_estimate=pl.CostEstimate(flops=2**20, bytes_accessed=11 * 2**19, transcendentals=0),
     )(tensor)
@@ -274,7 +276,9 @@
     basis_t = start_basis.T
     blocks, grams = [], ()
     for k in range(2):
-        packs = pack(tensor, k)
+        cut = 0 if k else 2
+        packs = list(pack(tensor, k, OFFSETS[:cut])) if cut else []
+        packs += pack(tensor, k, OFFSETS[cut:])
         part = [lax.ppermute(b, "gx", perm_gx(*o)) for b, o in zip(packs[:7], OFFSETS)] + [packs[7]]
         grams = gram(part, grams)
         blocks += part

time: 135 us -> 133 us (0.985)
  starting transfers between devices: 37.6 us -> 33.9 us
  Pallas kernels: 28.3 us -> 31.8 us
    ppermute x14, starting transfers between devices: 34.4 us -> 30.6 us  [per_device(): lax.ppermute(b, 'gx', perm_gx(*o))]
    pallas_call x2 -> x3, Pallas kernels: 6.58 us -> 10.3 us  [pack(): pl.pallas_call(functools.partial(pack_kernel, wanted), grid=(2,), in_spec...]
  transfers between devices with their start and end apart: 16 -> 16, of which waited for: 9 -> 8; matrix products, arithmetic and copies ran while one was open for 0% -> 0% of each run, Pallas kernels for 4% -> 8%
where the time goes in v7:
time: 133 us
  blocking collectives  37.5 us (28%)
  starting transfers between devices  33.9 us (25%)
  Pallas kernels  31.8 us (24%)
  waiting for transfers between devices  27.4 us (21%)
    ppermute x14, starting transfers between devices, per_device(): lax.ppermute(b, 'gx', perm_gx(*o))  30.6 us
    ppermute x14, waiting for transfers between devices, per_device(): lax.ppermute(b, 'gx', perm_gx(*o))  23.9 us
    all_to_all x1, blocking collectives, total_over_devices(): lax.all_to_all(half.reshape(64, 16, 128), both, 0, 0, axis_index_groups=S...  21.9 us
    pallas_call x1, Pallas kernels, finish(): pl.pallas_call(finish_kernel, out_shape=(jax.ShapeDtypeStruct((R, X), F32...  15.7 us
    all_to_all x1, blocking collectives, total_over_devices(): lax.all_to_all(jnp.broadcast_to(piece[None], (64, 16, 128)), both, 0, 0,...  15.7 us
    pallas_call x3, Pallas kernels, pack(): pl.pallas_call(functools.partial(pack_kernel, wanted), grid=(2,), in_spec...  10.3 us
    pallas_call x2, Pallas kernels, gram(): pl.pallas_call(functools.partial(gram_kernel, k), out_shape=(half, half)...  5.8 us
    ppermute x1, starting transfers between devices, total_over_devices(): return (whole, lax.ppermute(whole, 'gx', perm_gx(0, 1)))  3.07 us
  transfers between devices with their start and end apart: 16, of which 8 were waited for; matrix products, arithmetic and copies ran while one was open for 0% of the time, Pallas kernels for 8%

profile of v7, /device:TPU:1, one launch (start us, length us, event | category | flops | bytes accessed | tf_op | source)
XLA Modules:
  0.0 132.7 jit_solution(16072831897084416930)
XLA Ops:
  0.6 2.7 %shard_map.41 = (f32[672,128]{1,0:T(8,128)}, f32[672,128]{1,0:T(8,128)}) custom-call(f32[4,84,8,512]{3,2,1,0:T(8,128)} %species.5), custom_call_target="tpu_custom_call" | custom-call | flops 1048576 | bytes 5767168 | tf_op jit(solution)/shard_map/pallas_call | solution.py:264
  3.3 2.1 %collective-permute-start = (f32[672,128]{1,0:T(8,128)}, f32[672,128]{1,0:T(8,128)S(1)}, u32[]{:S(2)}, u32[]{:S(2)}) collective-permute-start(f32[672,128]{1,0:T(8,128)} %get-tuple-element.22), channel_id=1, source_target_pairs={{0,32},{16,48},{32,64},{48,80},{64,96},{80,112},{96,0},{112,16},{1... | collective-permute-start | bytes 1032200 | tf_op jit(solution)/shard_map/ppermute | solution.py:282
  5.5 1.4 %collective-permute-start.1 = (f32[672,128]{1,0:T(8,128)}, f32[672,128]{1,0:T(8,128)S(1)}, u32[]{:S(2)}, u32[]{:S(2)}) collective-permute-start(f32[672,128]{1,0:T(8,128)} %get-tuple-element.23), channel_id=1, source_target_pairs={{0,96},{16,112},{32,0},{48,16},{64,32},{80,48},{96,64},{112,80},{1... | collective-permute-start | bytes 1032200 | tf_op jit(solution)/shard_map/ppermute | solution.py:282
  6.9 3.6 %shard_map.42 = (f32[672,128]{1,0:T(8,128)}, f32[672,128]{1,0:T(8,128)}, f32[672,128]{1,0:T(8,128)}, f32[672,128]{1,0:T(8,128)}, f32[672,128]{1,0:T(8,128)}, /*index=5*/f32[672,128]{1,0:T(8,128)}) custom-call(f32[4,84,8,512]{3,2,1,0:T(8,128)} %species.5), custom_call_target="tpu_custom_call" | custom-call | flops 1048576 | bytes 5767168 | tf_op jit(solution)/shard_map/pallas_call | solution.py:264
  10.5 1.7 %collective-permute-start.2 = (f32[672,128]{1,0:T(8,128)}, f32[672,128]{1,0:T(8,128)S(1)}, u32[]{:S(2)}, u32[]{:S(2)}) collective-permute-start(f32[672,128]{1,0:T(8,128)} %get-tuple-element.24), channel_id=1, source_target_pairs={{0,64},{16,80},{32,96},{48,112},{64,0},{80,16},{96,32},{112,48},{1... | collective-permute-start | bytes 1032200 | tf_op jit(solution)/shard_map/ppermute | solution.py:282
  12.2 1.8 %collective-permute-start.3 = (f32[672,128]{1,0:T(8,128)}, f32[672,128]{1,0:T(8,128)S(1)}, u32[]{:S(2)}, u32[]{:S(2)}) collective-permute-start(f32[672,128]{1,0:T(8,128)} %get-tuple-element.25), channel_id=1, source_target_pairs={{0,48},{16,32},{32,80},{48,64},{64,112},{80,96},{96,16},{112,0},{1... | collective-permute-start | bytes 1032200 | tf_op jit(solution)/shard_map/ppermute | solution.py:282
  14.0 1.2 collective-permute-start.4
  15.2 4.0 %shard_map.43 = (f32[672,128]{1,0:T(8,128)}, f32[672,128]{1,0:T(8,128)}, f32[672,128]{1,0:T(8,128)}, f32[672,128]{1,0:T(8,128)}, f32[672,128]{1,0:T(8,128)}, /*i...) custom-call(f32[4,84,8,512]{3,2,1,0:T(8,128)} %species.5), custom_call_target="tpu_custom_call" | custom-call | flops 1048576 | bytes 5767168 | tf_op jit(solution)/shard_map/pallas_call | solution.py:264
  19.2 4.9 %collective-permute-start.5 = (f32[672,128]{1,0:T(8,128)S(1)}, f32[672,128]{1,0:T(8,128)S(1)}, u32[]{:S(2)}, u32[]{:S(2)}) collective-permute-start(f32[672,128]{1,0:T(8,128)S(1)} %copy-done.19), channel_id=1, source_target_pairs={{0,80},{16,64},{32,112},{48,96},{64,16},{80,0},{96,48},{112,32},{1... | collective-permute-start | bytes 1032200 | tf_op jit(solution)/shard_map/ppermute | solution.py:282
  24.1 0.1 collective-permute-start.6
  24.2 0.1 collective-permute-start.7
  24.3 6.5 %collective-permute-done.3.refs_3_ = f32[672,128]{1,0:T(8,128)S(1)} collective-permute-done((f32[672,128]{1,0:T(8,128)}, f32[672,128]{1,0:T(8,128)S(1)}, u32[]{:S(2)}, u32[]{:S(2)}) %collective-permute-start.3) | collective-permute-done | bytes 344096 | tf_op jit(solution)/shard_map/ppermute | solution.py:282
  30.8 2.3 %collective-permute-start.8 = (f32[672,128]{1,0:T(8,128)}, f32[672,128]{1,0:T(8,128)S(1)}, u32[]{:S(2)}, u32[]{:S(2)}) collective-permute-start(f32[672,128]{1,0:T(8,128)} %get-tuple-element.31), channel_id=1, source_target_pairs={{0,96},{16,112},{32,0},{48,16},{64,32},{80,48},{96,64},{112,80},{1... | collective-permute-start | bytes 1032200 | tf_op jit(solution)/shard_map/ppermute | solution.py:282
  33.1 5.3 %collective-permute-start.9 = (f32[672,128]{1,0:T(8,128)}, f32[672,128]{1,0:T(8,128)S(1)}, u32[]{:S(2)}, u32[]{:S(2)}) collective-permute-start(f32[672,128]{1,0:T(8,128)} %get-tuple-element.32), channel_id=1, source_target_pairs={{0,64},{16,80},{32,96},{48,112},{64,0},{80,16},{96,32},{112,48},{1... | collective-permute-start | bytes 1032200 | tf_op jit(solution)/shard_map/ppermute | solution.py:282
  38.4 1.6 %collective-permute-done.5.refs_5_ = f32[672,128]{1,0:T(8,128)S(1)} collective-permute-done((f32[672,128]{1,0:T(8,128)S(1)}, f32[672,128]{1,0:T(8,128)S(1)}, u32[]{:S(2)}, u32[]{:S(2)}) %collective-permute-start.5) | collective-permute-done | bytes 344096 | tf_op jit(solution)/shard_map/ppermute | solution.py:282
  40.0 2.9 %collective-permute-start.11 = (f32[672,128]{1,0:T(8,128)}, f32[672,128]{1,0:T(8,128)S(1)}, u32[]{:S(2)}, u32[]{:S(2)}) collective-permute-start(f32[672,128]{1,0:T(8,128)} %get-tuple-element.34), channel_id=1, source_target_pairs={{0,112},{16,96},{32,16},{48,0},{64,48},{80,32},{96,80},{112,64},{1... | collective-permute-start | bytes 1032200 | tf_op jit(solution)/shard_map/ppermute | solution.py:282
  42.9 3.9 %collective-permute-done.7.refs_0_.refs_8_ = f32[672,128]{1,0:T(8,128)S(1)} collective-permute-done((f32[672,128]{1,0:T(8,128)}, f32[672,128]{1,0:T(8,128)S(1)}, u32[]{:S(2)}, u32[]{:S(2)}) %collective-permute-start.7) | collective-permute-done | bytes 344096 | tf_op jit(solution)/shard_map/ppermute | solution.py:282
  46.8 6.7 %collective-permute-start.12 = (f32[672,128]{1,0:T(8,128)}, f32[672,128]{1,0:T(8,128)S(1)}, u32[]{:S(2)}, u32[]{:S(2)}) collective-permute-start(f32[672,128]{1,0:T(8,128)} %get-tuple-element.35), channel_id=1, source_target_pairs={{0,80},{16,64},{32,112},{48,96},{64,16},{80,0},{96,48},{112,32},{1... | collective-permute-start | bytes 1032200 | tf_op jit(solution)/shard_map/ppermute | solution.py:282
  53.5 2.8 %shard_map.44.refs_8_ = f32[2112,128]{1,0:T(8,128)S(1)} custom-call(f32[672,128]{1,0:T(8,128)S(1)} %collective-permute-done.refs_0_, f32[672,128]{1,0:T(8,128)S(1)} %collective-permute-done.1.refs_1_, f32[672,128]{1,0:T(8,128)S(1)} %collective-permute-done.2.refs_2_, f32[672,128]{1,0:T(8,128)S(1)} %collective-permute-done.3.refs_3_, ...), custom_call_target="tpu_custom_call" | custom-call | flops 2774532096 | bytes 4194304 | tf_op jit(solution)/shard_map/pallas_call | solution.py:120
  56.3 3.9 %collective-permute-done.10.refs_3_.refs_11_ = f32[672,128]{1,0:T(8,128)S(1)} collective-permute-done((f32[672,128]{1,0:T(8,128)}, f32[672,128]{1,0:T(8,128)S(1)}, u32[]{:S(2)}, u32[]{:S(2)}) %collective-permute-start.10) | collective-permute-done | bytes 344096 | tf_op jit(solution)/shard_map/ppermute | solution.py:282
  60.2 1.3 %collective-permute-done.11.refs_4_.refs_12_ = f32[672,128]{1,0:T(8,128)S(1)} collective-permute-done((f32[672,128]{1,0:T(8,128)}, f32[672,128]{1,0:T(8,128)S(1)}, u32[]{:S(2)}, u32[]{:S(2)}) %collective-permute-start.11) | collective-permute-done | bytes 344096 | tf_op jit(solution)/shard_map/ppermute | solution.py:282
  61.6 6.8 %collective-permute-done.12.refs_5_.refs_13_ = f32[672,128]{1,0:T(8,128)S(1)} collective-permute-done((f32[672,128]{1,0:T(8,128)}, f32[672,128]{1,0:T(8,128)S(1)}, u32[]{:S(2)}, u32[]{:S(2)}) %collective-permute-start.12) | collective-permute-done | bytes 344096 | tf_op jit(solution)/shard_map/ppermute | solution.py:282
  68.4 3.0 %shard_map.45 = (f32[1024,128]{1,0:T(8,128)S(1)}, f32[1024,128]{1,0:T(8,128)S(1)}) custom-call(f32[672,128]{1,0:T(8,128)S(1)} %collective-permute-done.7.refs_0_.refs_8_, f32[672,128]{1,0:T(8,128)S(1)} %collective-permute-done.8.refs_1_.refs_9_, f32[672,128]{1,0:T(8,128)S(1)} %collective-permute-done.9.refs_2_.refs_10_, ...), custom_call_target="tpu_custom_call" | custom-call | flops 2774532096 | bytes 4194304 | tf_op jit(solution)/shard_map/pallas_call | solution.py:120
  71.5 0.3 collective-permute-start.14
  71.8 1.9 %collective-permute-done.14 = f32[1024,128]{1,0:T(8,128)S(1)} collective-permute-done((f32[1024,128]{1,0:T(8,128)S(1)}, f32[1024,128]{1,0:T(8,128)S(1)}, u32[]{:S(2)}, u32[]{:S(2)}) %collective-permute-start.14) | collective-permute-done | bytes 524320 | tf_op jit(solution)/shard_map/ppermute | solution.py:57
  73.8 21.9 %all_to_all.10 = f32[64,16,128]{2,1,0:T(8,128)S(1)} all-to-all(f32[64,16,128]{2,1,0:T(8,128)S(1)} %bitcast.5), channel_id=1, replica_groups={{0,1,2,3,4,5,6,7,8,9,10,11,12,13,14,15,32,33,34,35,36,37,38,39,40,41,42..., dimensions={0} | all-to-all | bytes 1048576 | tf_op jit(solution)/shard_map/all_to_all | solution.py:59
  95.6 0.1 reduce_sum.9
  95.7 15.7 %all_to_all.11 = f32[64,16,128]{2,1,0:T(8,128)S(1)} all-to-all(f32[64,16,128]{2,1,0:T(8,128)S(1)} %broadcast_in_dim.2), channel_id=1, replica_groups={{0,1,2,3,4,5,6,7,8,9,10,11,12,13,14,15,32,33,34,35,36,37,38,39,40,41,42..., dimensions={0} | all-to-all | bytes 1048576 | tf_op jit(solution)/shard_map/all_to_all | solution.py:61
  111.4 3.1 %collective-permute-start.15 = (f32[1024,128]{1,0:T(8,128)S(1)}, f32[1024,128]{1,0:T(8,128)S(1)}, u32[]{:S(2)}, u32[]{:S(2)}) collective-permute-start(f32[1024,128]{1,0:T(8,128)S(1)} %bitcast.6), channel_id=1, source_target_pairs={{0,16},{16,0},{32,48},{48,32},{64,80},{80,64},{96,112},{112,96},{1... | collective-permute-start | bytes 1572872 | tf_op jit(solution)/shard_map/ppermute | solution.py:64
  114.5 1.5 %collective-permute-done.15.refs_17_ = f32[1024,128]{1,0:T(8,128)S(1)} collective-permute-done((f32[1024,128]{1,0:T(8,128)S(1)}, f32[1024,128]{1,0:T(8,128)S(1)}, u32[]{:S(2)}, u32[]{:S(2)}) %collective-permute-start.15) | collective-permute-done | bytes 524320 | tf_op jit(solution)/shard_map/ppermute | solution.py:64
  116.0 0.8 copy-done.17
  116.8 15.7 %shard_map.46 = (f32[96,672]{1,0:T(8,128)}, f32[4,8,64,96]{3,2,1,0:T(8,128)}) custom-call(f32[672,128]{1,0:T(8,128)} %copy-done, f32[672,128]{1,0:T(8,128)} %copy-done.1, f32[672,128]{1,0:T(8,128)} %copy-done.3, f32[672,128]{1,0:T(8,128)} %copy-done.4, f32[672,128]{1,0:T(8,128)} %copy-done.5, f32[672,128]{1,0:T(8,128)} %copy-done.7, f32[672,128]{1,0:T(8,128)} %copy-done.8, ...), custom_call_target="tpu_custom_call" | custom-call | flops 792723456 | bytes 7340032 | tf_op jit(solution)/shard_map/pallas_call | solution.py:230
  (51 shorter events, 0.2 us)
Async XLA Ops:
  3.3 15.8 %collective-permute-start = (f32[672,128]{1,0:T(8,128)}, f32[672,128]{1,0:T(8,128)S(1)}, u32[]{:S(2)}, u32[]{:S(2)}) collective-permute-start(f32[672,128]{1,0:T(8,128)} %get-tuple-element.22), channel_id=1, source_target_pairs={{0,32},{16,48},{32,64},{48,80},{64,96},{80,112},{96,0},{112,16},{1... | collective-permute-start | bytes 1032200 | tf_op jit(solution)/shard_map/ppermute | solution.py:282
  5.5 18.7 %collective-permute-start.1 = (f32[672,128]{1,0:T(8,128)}, f32[672,128]{1,0:T(8,128)S(1)}, u32[]{:S(2)}, u32[]{:S(2)}) collective-permute-start(f32[672,128]{1,0:T(8,128)} %get-tuple-element.23), channel_id=1, source_target_pairs={{0,96},{16,112},{32,0},{48,16},{64,32},{80,48},{96,64},{112,80},{1... | collective-permute-start | bytes 1032200 | tf_op jit(solution)/shard_map/ppermute | solution.py:282
  10.5 8.7 %copy-start.19 = (f32[672,128]{1,0:T(8,128)S(1)}, f32[672,128]{1,0:T(8,128)}, u32[]{:S(2)}) copy-start(f32[672,128]{1,0:T(8,128)} %get-tuple-element.27) | copy-start | bytes 1032196
  10.5 13.7 %copy-start.18 = (f32[672,128]{1,0:T(8,128)S(1)}, f32[672,128]{1,0:T(8,128)}, u32[]{:S(2)}) copy-start(f32[672,128]{1,0:T(8,128)} %get-tuple-element.28) | copy-start | bytes 1032196
  10.5 43.1 %copy-start.2 = (f32[672,128]{1,0:T(8,128)S(1)}, f32[672,128]{1,0:T(8,128)}, u32[]{:S(2)}) copy-start(f32[672,128]{1,0:T(8,128)} %get-tuple-element.29.refs_7_) | copy-start | bytes 1032196
  10.5 13.7 %collective-permute-start.2 = (f32[672,128]{1,0:T(8,128)}, f32[672,128]{1,0:T(8,128)S(1)}, u32[]{:S(2)}, u32[]{:S(2)}) collective-permute-start(f32[672,128]{1,0:T(8,128)} %get-tuple-element.24), channel_id=1, source_target_pairs={{0,64},{16,80},{32,96},{48,112},{64,0},{80,16},{96,32},{112,48},{1... | collective-permute-start | bytes 1032200 | tf_op jit(solution)/shard_map/ppermute | solution.py:282
  12.2 18.6 %collective-permute-start.3 = (f32[672,128]{1,0:T(8,128)}, f32[672,128]{1,0:T(8,128)S(1)}, u32[]{:S(2)}, u32[]{:S(2)}) collective-permute-start(f32[672,128]{1,0:T(8,128)} %get-tuple-element.25), channel_id=1, source_target_pairs={{0,48},{16,32},{32,80},{48,64},{64,112},{80,96},{96,16},{112,0},{1... | collective-permute-start | bytes 1032200 | tf_op jit(solution)/shard_map/ppermute | solution.py:282
  14.0 19.1 %collective-permute-start.4 = (f32[672,128]{1,0:T(8,128)}, f32[672,128]{1,0:T(8,128)S(1)}, u32[]{:S(2)}, u32[]{:S(2)}) collective-permute-start(f32[672,128]{1,0:T(8,128)} %get-tuple-element.26), channel_id=1, source_target_pairs={{0,112},{16,96},{32,16},{48,0},{64,48},{80,32},{96,80},{112,64},{1... | collective-permute-start | bytes 1032200 | tf_op jit(solution)/shard_map/ppermute | solution.py:282
  19.2 49.2 %copy-start.6 = (f32[672,128]{1,0:T(8,128)S(1)}, f32[672,128]{1,0:T(8,128)}, u32[]{:S(2)}) copy-start(f32[672,128]{1,0:T(8,128)} %get-tuple-element.37.refs_7_.refs_15_) | copy-start | bytes 1032196
  19.2 52.2 %copy-start = (f32[672,128]{1,0:T(8,128)}, f32[672,128]{1,0:T(8,128)S(1)}, u32[]{:S(2)}) copy-start(f32[672,128]{1,0:T(8,128)S(1)} %collective-permute-done.refs_0_) | copy-start | bytes 1032196
  19.2 20.8 %collective-permute-start.5 = (f32[672,128]{1,0:T(8,128)S(1)}, f32[672,128]{1,0:T(8,128)S(1)}, u32[]{:S(2)}, u32[]{:S(2)}) collective-permute-start(f32[672,128]{1,0:T(8,128)S(1)} %copy-done.19), channel_id=1, source_target_pairs={{0,80},{16,64},{32,112},{48,96},{64,16},{80,0},{96,48},{112,32},{1... | collective-permute-start | bytes 1032200 | tf_op jit(solution)/shard_map/ppermute | solution.py:282
  24.1 47.3 %copy-start.1 = (f32[672,128]{1,0:T(8,128)}, f32[672,128]{1,0:T(8,128)S(1)}, u32[]{:S(2)}) copy-start(f32[672,128]{1,0:T(8,128)S(1)} %collective-permute-done.1.refs_1_) | copy-start | bytes 1032196
  24.1 15.8 %collective-permute-start.6 = (f32[672,128]{1,0:T(8,128)S(1)}, f32[672,128]{1,0:T(8,128)S(1)}, u32[]{:S(2)}, u32[]{:S(2)}) collective-permute-start(f32[672,128]{1,0:T(8,128)S(1)} %copy-done.18), channel_id=1, source_target_pairs={{0,16},{16,0},{32,48},{48,32},{64,80},{80,64},{96,112},{112,96},{1... | collective-permute-start | bytes 1032200 | tf_op jit(solution)/shard_map/ppermute | solution.py:282
  24.2 47.2 %copy-start.3 = (f32[672,128]{1,0:T(8,128)}, f32[672,128]{1,0:T(8,128)S(1)}, u32[]{:S(2)}) copy-start(f32[672,128]{1,0:T(8,128)S(1)} %collective-permute-done.2.refs_2_) | copy-start | bytes 1032196
  24.2 22.5 %collective-permute-start.7 = (f32[672,128]{1,0:T(8,128)}, f32[672,128]{1,0:T(8,128)S(1)}, u32[]{:S(2)}, u32[]{:S(2)}) collective-permute-start(f32[672,128]{1,0:T(8,128)} %get-tuple-element.30), channel_id=1, source_target_pairs={{0,32},{16,48},{32,64},{48,80},{64,96},{80,112},{96,0},{112,16},{1... | collective-permute-start | bytes 1032200 | tf_op jit(solution)/shard_map/ppermute | solution.py:282
  30.8 40.6 %copy-start.4 = (f32[672,128]{1,0:T(8,128)}, f32[672,128]{1,0:T(8,128)S(1)}, u32[]{:S(2)}) copy-start(f32[672,128]{1,0:T(8,128)S(1)} %collective-permute-done.3.refs_3_) | copy-start | bytes 1032196
  30.8 22.7 %collective-permute-start.8 = (f32[672,128]{1,0:T(8,128)}, f32[672,128]{1,0:T(8,128)S(1)}, u32[]{:S(2)}, u32[]{:S(2)}) collective-permute-start(f32[672,128]{1,0:T(8,128)} %get-tuple-element.31), channel_id=1, source_target_pairs={{0,96},{16,112},{32,0},{48,16},{64,32},{80,48},{96,64},{112,80},{1... | collective-permute-start | bytes 1032200 | tf_op jit(solution)/shard_map/ppermute | solution.py:282
  33.1 38.3 %copy-start.5 = (f32[672,128]{1,0:T(8,128)}, f32[672,128]{1,0:T(8,128)S(1)}, u32[]{:S(2)}) copy-start(f32[672,128]{1,0:T(8,128)S(1)} %collective-permute-done.4.refs_4_) | copy-start | bytes 1032196
  33.1 23.2 %collective-permute-start.9 = (f32[672,128]{1,0:T(8,128)}, f32[672,128]{1,0:T(8,128)S(1)}, u32[]{:S(2)}, u32[]{:S(2)}) collective-permute-start(f32[672,128]{1,0:T(8,128)} %get-tuple-element.32), channel_id=1, source_target_pairs={{0,64},{16,80},{32,96},{48,112},{64,0},{80,16},{96,32},{112,48},{1... | collective-permute-start | bytes 1032200 | tf_op jit(solution)/shard_map/ppermute | solution.py:282
  40.0 31.5 %copy-start.7 = (f32[672,128]{1,0:T(8,128)}, f32[672,128]{1,0:T(8,128)S(1)}, u32[]{:S(2)}) copy-start(f32[672,128]{1,0:T(8,128)S(1)} %collective-permute-done.5.refs_5_) | copy-start | bytes 1032196
  40.0 20.3 %collective-permute-start.10 = (f32[672,128]{1,0:T(8,128)}, f32[672,128]{1,0:T(8,128)S(1)}, u32[]{:S(2)}, u32[]{:S(2)}) collective-permute-start(f32[672,128]{1,0:T(8,128)} %get-tuple-element.33), channel_id=1, source_target_pairs={{0,48},{16,32},{32,80},{48,64},{64,112},{80,96},{96,16},{112,0},{1... | collective-permute-start | bytes 1032200 | tf_op jit(solution)/shard_map/ppermute | solution.py:282
  40.0 31.5 %copy-start.8 = (f32[672,128]{1,0:T(8,128)}, f32[672,128]{1,0:T(8,128)S(1)}, u32[]{:S(2)}) copy-start(f32[672,128]{1,0:T(8,128)S(1)} %collective-permute-done.6.refs_6_) | copy-start | bytes 1032196
  40.0 21.6 %collective-permute-start.11 = (f32[672,128]{1,0:T(8,128)}, f32[672,128]{1,0:T(8,128)S(1)}, u32[]{:S(2)}, u32[]{:S(2)}) collective-permute-start(f32[672,128]{1,0:T(8,128)} %get-tuple-element.34), channel_id=1, source_target_pairs={{0,112},{16,96},{32,16},{48,0},{64,48},{80,32},{96,80},{112,64},{1... | collective-permute-start | bytes 1032200 | tf_op jit(solution)/shard_map/ppermute | solution.py:282
  46.8 24.7 %copy-start.9 = (f32[672,128]{1,0:T(8,128)}, f32[672,128]{1,0:T(8,128)S(1)}, u32[]{:S(2)}) copy-start(f32[672,128]{1,0:T(8,128)S(1)} %collective-permute-done.7.refs_0_.refs_8_) | copy-start | bytes 1032196
  46.8 21.6 %collective-permute-start.12 = (f32[672,128]{1,0:T(8,128)}, f32[672,128]{1,0:T(8,128)S(1)}, u32[]{:S(2)}, u32[]{:S(2)}) collective-permute-start(f32[672,128]{1,0:T(8,128)} %get-tuple-element.35), channel_id=1, source_target_pairs={{0,80},{16,64},{32,112},{48,96},{64,16},{80,0},{96,48},{112,32},{1... | collective-permute-start | bytes 1032200 | tf_op jit(solution)/shard_map/ppermute | solution.py:282
  53.5 17.9 %copy-start.10 = (f32[672,128]{1,0:T(8,128)}, f32[672,128]{1,0:T(8,128)S(1)}, u32[]{:S(2)}) copy-start(f32[672,128]{1,0:T(8,128)S(1)} %collective-permute-done.8.refs_1_.refs_9_) | copy-start | bytes 1032196
  53.5 14.8 %collective-permute-start.13 = (f32[672,128]{1,0:T(8,128)}, f32[672,128]{1,0:T(8,128)S(1)}, u32[]{:S(2)}, u32[]{:S(2)}) collective-permute-start(f32[672,128]{1,0:T(8,128)} %get-tuple-element.36), channel_id=1, source_target_pairs={{0,16},{16,0},{32,48},{48,32},{64,80},{80,64},{96,112},{112,96},{1... | collective-permute-start | bytes 1032200 | tf_op jit(solution)/shard_map/ppermute | solution.py:282
  56.3 17.4 %copy-start.11 = (f32[672,128]{1,0:T(8,128)}, f32[672,128]{1,0:T(8,128)S(1)}, u32[]{:S(2)}) copy-start(f32[672,128]{1,0:T(8,128)S(1)} %collective-permute-done.9.refs_2_.refs_10_) | copy-start | bytes 1032196
  60.2 13.5 %copy-start.12 = (f32[672,128]{1,0:T(8,128)}, f32[672,128]{1,0:T(8,128)S(1)}, u32[]{:S(2)}) copy-start(f32[672,128]{1,0:T(8,128)S(1)} %collective-permute-done.10.refs_3_.refs_11_) | copy-start | bytes 1032196
  61.6 12.2 %copy-start.13 = (f32[672,128]{1,0:T(8,128)}, f32[672,128]{1,0:T(8,128)S(1)}, u32[]{:S(2)}) copy-start(f32[672,128]{1,0:T(8,128)S(1)} %collective-permute-done.11.refs_4_.refs_12_) | copy-start | bytes 1032196
  71.5 2.2 %collective-permute-start.14 = (f32[1024,128]{1,0:T(8,128)S(1)}, f32[1024,128]{1,0:T(8,128)S(1)}, u32[]{:S(2)}, u32[]{:S(2)}) collective-permute-start(f32[1024,128]{1,0:T(8,128)S(1)} %get-tuple-element.39), channel_id=1, source_target_pairs={{0,16},{16,0},{32,48},{48,32},{64,80},{80,64},{96,112},{112,96},{1... | collective-permute-start | bytes 1572872 | tf_op jit(solution)/shard_map/ppermute | solution.py:57
  111.4 4.6 %collective-permute-start.15 = (f32[1024,128]{1,0:T(8,128)S(1)}, f32[1024,128]{1,0:T(8,128)S(1)}, u32[]{:S(2)}, u32[]{:S(2)}) collective-permute-start(f32[1024,128]{1,0:T(8,128)S(1)} %bitcast.6), channel_id=1, source_target_pairs={{0,16},{16,0},{32,48},{48,32},{64,80},{80,64},{96,112},{112,96},{1... | collective-permute-start | bytes 1572872 | tf_op jit(solution)/shard_map/ppermute | solution.py:64
  (4 other events, 16.2 us)

commit v8 on v7

--- a/solution.py
+++ b/solution.py
@@ -258,6 +258,37 @@
         out[...] = jnp.where(even, high, low) if dc else jnp.where(even, low, high)
 
 
+def first_kernel(wanted, tensor, *refs):
+    outs, (species, sems) = refs[:-2], refs[-2:]
+    y, c = place()
+    copies = []
+    for i, (dy, _) in enumerate(wanted):
+        at = pl.ds(pl.multiple_of(lax.rem(y + dy, 4) * 128, 128), 128)
+        copies.append(pltpu.make_async_copy(tensor.at[pl.ds(0, 2), :, :, at], species.at[i], sems.at[i]))
+        copies[i].start()
+    rows = ROWS * 8
+    first = lax.broadcasted_iota(jnp.int32, (rows, 128), 1) < 64
+    for i, out in enumerate(outs):
+        copies[i].wait()
+        a, b = (species[i, q].reshape(rows, 128) for q in range(2))
+        low = jnp.where(first, a, pltpu.roll(b, 64, 1))
+        high = jnp.where(first, pltpu.roll(a, 64, 1), b)
+        out[...] = jnp.where(c == 0, low, high)
+
+
+def pack_first(tensor, wanted):
+    n = len(wanted)
+    return pl.pallas_call(
+        functools.partial(first_kernel, wanted),
+        in_specs=[pl.BlockSpec(memory_space=pltpu.HBM)],
+        out_specs=(pl.BlockSpec(memory_space=pltpu.VMEM),) * n,
+        out_shape=(jax.ShapeDtypeStruct((ROWS * 8, 128), F32),) * n,
+        scratch_shapes=[pltpu.VMEM((n, 2, ROWS, 8, 128), F32), pltpu.SemaphoreType.DMA((n,))],
+        compiler_params=pltpu.CompilerParams(vmem_limit_bytes=60 * 1024 * 1024),
+        cost_estimate=pl.CostEstimate(flops=2**20, bytes_accessed=2**21, transcendentals=0),
+    )(tensor)
+
+
 def pack(tensor, k, wanted):
     rows = ROWS // 2
     out = pl.BlockSpec((rows * 8, 128), lambda i: (i, 0))
@@ -277,7 +308,7 @@
     blocks, grams = [], ()
     for k in range(2):
         cut = 0 if k else 2
-        packs = list(pack(tensor, k, OFFSETS[:cut])) if cut else []
+        packs = list(pack_first(tensor, OFFSETS[:cut])) if cut else []
         packs += pack(tensor, k, OFFSETS[cut:])
         part = [lax.ppermute(b, "gx", perm_gx(*o)) for b, o in zip(packs[:7], OFFSETS)] + [packs[7]]
         grams = gram(part, grams)

time: 133 us -> 133 us (level)
    pallas_call x3 -> x2, Pallas kernels: 10.3 us -> 7.57 us  [pack(): pl.pallas_call(functools.partial(pack_kernel, wanted), grid=(2,), in_spec...]
    pallas_call x0 -> x1, Pallas kernels: none -> 2.35 us  [pack_first(): pl.pallas_call(functools.partial(first_kernel, wanted), in_specs=[pl.Bloc...]
where the time goes in v8:
time: 133 us; the launch traced here: 132 us
  blocking collectives  37.7 us (28%)
  starting transfers between devices  33.8 us (25%)
  Pallas kernels  31.4 us (24%)
  waiting for transfers between devices  27.3 us (21%)
    ppermute x14, starting transfers between devices, per_device(): lax.ppermute(b, 'gx', perm_gx(*o))  30.7 us
    ppermute x14, waiting for transfers between devices, per_device(): lax.ppermute(b, 'gx', perm_gx(*o))  23.9 us
    all_to_all x1, blocking collectives, total_over_devices(): lax.all_to_all(half.reshape(64, 16, 128), both, 0, 0, axis_index_groups=S...  22 us
    pallas_call x1, Pallas kernels, finish(): pl.pallas_call(finish_kernel, out_shape=(jax.ShapeDtypeStruct((R, X), F32...  15.7 us
    all_to_all x1, blocking collectives, total_over_devices(): lax.all_to_all(jnp.broadcast_to(piece[None], (64, 16, 128)), both, 0, 0,...  15.7 us
    pallas_call x2, Pallas kernels, pack(): pl.pallas_call(functools.partial(pack_kernel, wanted), grid=(2,), in_spec...  7.57 us
    pallas_call x2, Pallas kernels, gram(): pl.pallas_call(functools.partial(gram_kernel, k), out_shape=(half, half)...  5.79 us
    ppermute x1, starting transfers between devices, total_over_devices(): return (whole, lax.ppermute(whole, 'gx', perm_gx(0, 1)))  3.04 us
  transfers between devices with their start and end apart: 16, of which 8 were waited for; matrix products, arithmetic and copies ran while one was open for 0% of the time, Pallas kernels for 8%

profile of v8, /device:TPU:1, one launch (start us, length us, event | category | flops | bytes accessed | tf_op | source)
XLA Modules:
  0.0 132.3 jit_solution(13715275844268656509)
XLA Ops:
  0.6 2.4 %shard_map.41 = (f32[672,128]{1,0:T(8,128)}, f32[672,128]{1,0:T(8,128)}) custom-call(f32[4,84,8,512]{3,2,1,0:T(8,128)} %species.3), custom_call_target="tpu_custom_call" | custom-call | flops 1048576 | bytes 2097152 | tf_op jit(solution)/shard_map/pallas_call | solution.py:281
  3.0 2.2 %collective-permute-start = (f32[672,128]{1,0:T(8,128)}, f32[672,128]{1,0:T(8,128)S(1)}, u32[]{:S(2)}, u32[]{:S(2)}) collective-permute-start(f32[672,128]{1,0:T(8,128)} %get-tuple-element.22), channel_id=1, source_target_pairs={{0,32},{16,48},{32,64},{48,80},{64,96},{80,112},{96,0},{112,16},{1... | collective-permute-start | bytes 1032200 | tf_op jit(solution)/shard_map/ppermute | solution.py:313
  5.2 1.5 %collective-permute-start.1 = (f32[672,128]{1,0:T(8,128)}, f32[672,128]{1,0:T(8,128)S(1)}, u32[]{:S(2)}, u32[]{:S(2)}) collective-permute-start(f32[672,128]{1,0:T(8,128)} %get-tuple-element.23), channel_id=1, source_target_pairs={{0,96},{16,112},{32,0},{48,16},{64,32},{80,48},{96,64},{112,80},{1... | collective-permute-start | bytes 1032200 | tf_op jit(solution)/shard_map/ppermute | solution.py:313
  6.7 3.6 %shard_map.42 = (f32[672,128]{1,0:T(8,128)}, f32[672,128]{1,0:T(8,128)}, f32[672,128]{1,0:T(8,128)}, f32[672,128]{1,0:T(8,128)}, f32[672,128]{1,0:T(8,128)}, /*index=5*/f32[672,128]{1,0:T(8,128)}) custom-call(f32[4,84,8,512]{3,2,1,0:T(8,128)} %species.3), custom_call_target="tpu_custom_call" | custom-call | flops 1048576 | bytes 5767168 | tf_op jit(solution)/shard_map/pallas_call | solution.py:295
  10.3 1.6 %collective-permute-start.2 = (f32[672,128]{1,0:T(8,128)}, f32[672,128]{1,0:T(8,128)S(1)}, u32[]{:S(2)}, u32[]{:S(2)}) collective-permute-start(f32[672,128]{1,0:T(8,128)} %get-tuple-element.24), channel_id=1, source_target_pairs={{0,64},{16,80},{32,96},{48,112},{64,0},{80,16},{96,32},{112,48},{1... | collective-permute-start | bytes 1032200 | tf_op jit(solution)/shard_map/ppermute | solution.py:313
  11.9 1.8 %collective-permute-start.3 = (f32[672,128]{1,0:T(8,128)}, f32[672,128]{1,0:T(8,128)S(1)}, u32[]{:S(2)}, u32[]{:S(2)}) collective-permute-start(f32[672,128]{1,0:T(8,128)} %get-tuple-element.25), channel_id=1, source_target_pairs={{0,48},{16,32},{32,80},{48,64},{64,112},{80,96},{96,16},{112,0},{1... | collective-permute-start | bytes 1032200 | tf_op jit(solution)/shard_map/ppermute | solution.py:313
  13.7 1.2 collective-permute-start.4
  14.9 4.0 %shard_map.43 = (f32[672,128]{1,0:T(8,128)}, f32[672,128]{1,0:T(8,128)}, f32[672,128]{1,0:T(8,128)}, f32[672,128]{1,0:T(8,128)}, f32[672,128]{1,0:T(8,128)}, /*i...) custom-call(f32[4,84,8,512]{3,2,1,0:T(8,128)} %species.3), custom_call_target="tpu_custom_call" | custom-call | flops 1048576 | bytes 5767168 | tf_op jit(solution)/shard_map/pallas_call | solution.py:295
  18.9 4.9 %collective-permute-start.5 = (f32[672,128]{1,0:T(8,128)S(1)}, f32[672,128]{1,0:T(8,128)S(1)}, u32[]{:S(2)}, u32[]{:S(2)}) collective-permute-start(f32[672,128]{1,0:T(8,128)S(1)} %copy-done.19), channel_id=1, source_target_pairs={{0,80},{16,64},{32,112},{48,96},{64,16},{80,0},{96,48},{112,32},{1... | collective-permute-start | bytes 1032200 | tf_op jit(solution)/shard_map/ppermute | solution.py:313
  23.9 0.1 collective-permute-start.6
  24.0 0.1 collective-permute-start.7
  24.1 6.5 %collective-permute-done.3.refs_3_ = f32[672,128]{1,0:T(8,128)S(1)} collective-permute-done((f32[672,128]{1,0:T(8,128)}, f32[672,128]{1,0:T(8,128)S(1)}, u32[]{:S(2)}, u32[]{:S(2)}) %collective-permute-start.3) | collective-permute-done | bytes 344096 | tf_op jit(solution)/shard_map/ppermute | solution.py:313
  30.6 2.3 %collective-permute-start.8 = (f32[672,128]{1,0:T(8,128)}, f32[672,128]{1,0:T(8,128)S(1)}, u32[]{:S(2)}, u32[]{:S(2)}) collective-permute-start(f32[672,128]{1,0:T(8,128)} %get-tuple-element.31), channel_id=1, source_target_pairs={{0,96},{16,112},{32,0},{48,16},{64,32},{80,48},{96,64},{112,80},{1... | collective-permute-start | bytes 1032200 | tf_op jit(solution)/shard_map/ppermute | solution.py:313
  32.9 5.3 %collective-permute-start.9 = (f32[672,128]{1,0:T(8,128)}, f32[672,128]{1,0:T(8,128)S(1)}, u32[]{:S(2)}, u32[]{:S(2)}) collective-permute-start(f32[672,128]{1,0:T(8,128)} %get-tuple-element.32), channel_id=1, source_target_pairs={{0,64},{16,80},{32,96},{48,112},{64,0},{80,16},{96,32},{112,48},{1... | collective-permute-start | bytes 1032200 | tf_op jit(solution)/shard_map/ppermute | solution.py:313
  38.2 1.5 %collective-permute-done.5.refs_5_ = f32[672,128]{1,0:T(8,128)S(1)} collective-permute-done((f32[672,128]{1,0:T(8,128)S(1)}, f32[672,128]{1,0:T(8,128)S(1)}, u32[]{:S(2)}, u32[]{:S(2)}) %collective-permute-start.5) | collective-permute-done | bytes 344096 | tf_op jit(solution)/shard_map/ppermute | solution.py:313
  39.7 2.9 %collective-permute-start.11 = (f32[672,128]{1,0:T(8,128)}, f32[672,128]{1,0:T(8,128)S(1)}, u32[]{:S(2)}, u32[]{:S(2)}) collective-permute-start(f32[672,128]{1,0:T(8,128)} %get-tuple-element.34), channel_id=1, source_target_pairs={{0,112},{16,96},{32,16},{48,0},{64,48},{80,32},{96,80},{112,64},{1... | collective-permute-start | bytes 1032200 | tf_op jit(solution)/shard_map/ppermute | solution.py:313
  42.7 3.9 %collective-permute-done.7.refs_0_.refs_8_ = f32[672,128]{1,0:T(8,128)S(1)} collective-permute-done((f32[672,128]{1,0:T(8,128)}, f32[672,128]{1,0:T(8,128)S(1)}, u32[]{:S(2)}, u32[]{:S(2)}) %collective-permute-start.7) | collective-permute-done | bytes 344096 | tf_op jit(solution)/shard_map/ppermute | solution.py:313
  46.5 6.7 %collective-permute-start.12 = (f32[672,128]{1,0:T(8,128)}, f32[672,128]{1,0:T(8,128)S(1)}, u32[]{:S(2)}, u32[]{:S(2)}) collective-permute-start(f32[672,128]{1,0:T(8,128)} %get-tuple-element.35), channel_id=1, source_target_pairs={{0,80},{16,64},{32,112},{48,96},{64,16},{80,0},{96,48},{112,32},{1... | collective-permute-start | bytes 1032200 | tf_op jit(solution)/shard_map/ppermute | solution.py:313
  53.3 2.8 %shard_map.44.refs_8_ = f32[2112,128]{1,0:T(8,128)S(1)} custom-call(f32[672,128]{1,0:T(8,128)S(1)} %collective-permute-done.refs_0_, f32[672,128]{1,0:T(8,128)S(1)} %collective-permute-done.1.refs_1_, f32[672,128]{1,0:T(8,128)S(1)} %collective-permute-done.2.refs_2_, f32[672,128]{1,0:T(8,128)S(1)} %collective-permute-done.3.refs_3_, ...), custom_call_target="tpu_custom_call" | custom-call | flops 2774532096 | bytes 4194304 | tf_op jit(solution)/shard_map/pallas_call | solution.py:120
  56.1 3.9 %collective-permute-done.10.refs_3_.refs_11_ = f32[672,128]{1,0:T(8,128)S(1)} collective-permute-done((f32[672,128]{1,0:T(8,128)}, f32[672,128]{1,0:T(8,128)S(1)}, u32[]{:S(2)}, u32[]{:S(2)}) %collective-permute-start.10) | collective-permute-done | bytes 344096 | tf_op jit(solution)/shard_map/ppermute | solution.py:313
  60.0 1.3 %collective-permute-done.11.refs_4_.refs_12_ = f32[672,128]{1,0:T(8,128)S(1)} collective-permute-done((f32[672,128]{1,0:T(8,128)}, f32[672,128]{1,0:T(8,128)S(1)}, u32[]{:S(2)}, u32[]{:S(2)}) %collective-permute-start.11) | collective-permute-done | bytes 344096 | tf_op jit(solution)/shard_map/ppermute | solution.py:313
  61.3 6.8 %collective-permute-done.12.refs_5_.refs_13_ = f32[672,128]{1,0:T(8,128)S(1)} collective-permute-done((f32[672,128]{1,0:T(8,128)}, f32[672,128]{1,0:T(8,128)S(1)}, u32[]{:S(2)}, u32[]{:S(2)}) %collective-permute-start.12) | collective-permute-done | bytes 344096 | tf_op jit(solution)/shard_map/ppermute | solution.py:313
  68.1 3.0 %shard_map.45 = (f32[1024,128]{1,0:T(8,128)S(1)}, f32[1024,128]{1,0:T(8,128)S(1)}) custom-call(f32[672,128]{1,0:T(8,128)S(1)} %collective-permute-done.7.refs_0_.refs_8_, f32[672,128]{1,0:T(8,128)S(1)} %collective-permute-done.8.refs_1_.refs_9_, f32[672,128]{1,0:T(8,128)S(1)} %collective-permute-done.9.refs_2_.refs_10_, ...), custom_call_target="tpu_custom_call" | custom-call | flops 2774532096 | bytes 4194304 | tf_op jit(solution)/shard_map/pallas_call | solution.py:120
  71.2 0.1 collective-permute-start.14
  71.3 1.9 %collective-permute-done.14 = f32[1024,128]{1,0:T(8,128)S(1)} collective-permute-done((f32[1024,128]{1,0:T(8,128)S(1)}, f32[1024,128]{1,0:T(8,128)S(1)}, u32[]{:S(2)}, u32[]{:S(2)}) %collective-permute-start.14) | collective-permute-done | bytes 524320 | tf_op jit(solution)/shard_map/ppermute | solution.py:57
  73.3 22.0 %all_to_all.10 = f32[64,16,128]{2,1,0:T(8,128)S(1)} all-to-all(f32[64,16,128]{2,1,0:T(8,128)S(1)} %bitcast.5), channel_id=1, replica_groups={{0,1,2,3,4,5,6,7,8,9,10,11,12,13,14,15,32,33,34,35,36,37,38,39,40,41,42..., dimensions={0} | all-to-all | bytes 1048576 | tf_op jit(solution)/shard_map/all_to_all | solution.py:59
  95.3 0.1 reduce_sum.9
  95.4 15.7 %all_to_all.11 = f32[64,16,128]{2,1,0:T(8,128)S(1)} all-to-all(f32[64,16,128]{2,1,0:T(8,128)S(1)} %broadcast_in_dim.2), channel_id=1, replica_groups={{0,1,2,3,4,5,6,7,8,9,10,11,12,13,14,15,32,33,34,35,36,37,38,39,40,41,42..., dimensions={0} | all-to-all | bytes 1048576 | tf_op jit(solution)/shard_map/all_to_all | solution.py:61
  111.1 3.0 %collective-permute-start.15 = (f32[1024,128]{1,0:T(8,128)S(1)}, f32[1024,128]{1,0:T(8,128)S(1)}, u32[]{:S(2)}, u32[]{:S(2)}) collective-permute-start(f32[1024,128]{1,0:T(8,128)S(1)} %bitcast.6), channel_id=1, source_target_pairs={{0,16},{16,0},{32,48},{48,32},{64,80},{80,64},{96,112},{112,96},{1... | collective-permute-start | bytes 1572872 | tf_op jit(solution)/shard_map/ppermute | solution.py:64
  114.1 1.5 %collective-permute-done.15.refs_17_ = f32[1024,128]{1,0:T(8,128)S(1)} collective-permute-done((f32[1024,128]{1,0:T(8,128)S(1)}, f32[1024,128]{1,0:T(8,128)S(1)}, u32[]{:S(2)}, u32[]{:S(2)}) %collective-permute-start.15) | collective-permute-done | bytes 524320 | tf_op jit(solution)/shard_map/ppermute | solution.py:64
  115.7 0.8 copy-done.17
  116.5 15.7 %shard_map.46 = (f32[96,672]{1,0:T(8,128)}, f32[4,8,64,96]{3,2,1,0:T(8,128)}) custom-call(f32[672,128]{1,0:T(8,128)} %copy-done, f32[672,128]{1,0:T(8,128)} %copy-done.1, f32[672,128]{1,0:T(8,128)} %copy-done.3, f32[672,128]{1,0:T(8,128)} %copy-done.4, f32[672,128]{1,0:T(8,128)} %copy-done.5, f32[672,128]{1,0:T(8,128)} %copy-done.7, f32[672,128]{1,0:T(8,128)} %copy-done.8, ...), custom_call_target="tpu_custom_call" | custom-call | flops 792723456 | bytes 7340032 | tf_op jit(solution)/shard_map/pallas_call | solution.py:230
  (51 shorter events, 0.2 us)
Async XLA Ops:
  3.0 15.9 %collective-permute-start = (f32[672,128]{1,0:T(8,128)}, f32[672,128]{1,0:T(8,128)S(1)}, u32[]{:S(2)}, u32[]{:S(2)}) collective-permute-start(f32[672,128]{1,0:T(8,128)} %get-tuple-element.22), channel_id=1, source_target_pairs={{0,32},{16,48},{32,64},{48,80},{64,96},{80,112},{96,0},{112,16},{1... | collective-permute-start | bytes 1032200 | tf_op jit(solution)/shard_map/ppermute | solution.py:313
  5.2 18.7 %collective-permute-start.1 = (f32[672,128]{1,0:T(8,128)}, f32[672,128]{1,0:T(8,128)S(1)}, u32[]{:S(2)}, u32[]{:S(2)}) collective-permute-start(f32[672,128]{1,0:T(8,128)} %get-tuple-element.23), channel_id=1, source_target_pairs={{0,96},{16,112},{32,0},{48,16},{64,32},{80,48},{96,64},{112,80},{1... | collective-permute-start | bytes 1032200 | tf_op jit(solution)/shard_map/ppermute | solution.py:313
  10.3 8.6 %copy-start.19 = (f32[672,128]{1,0:T(8,128)S(1)}, f32[672,128]{1,0:T(8,128)}, u32[]{:S(2)}) copy-start(f32[672,128]{1,0:T(8,128)} %get-tuple-element.27) | copy-start | bytes 1032196
  10.3 13.6 %copy-start.18 = (f32[672,128]{1,0:T(8,128)S(1)}, f32[672,128]{1,0:T(8,128)}, u32[]{:S(2)}) copy-start(f32[672,128]{1,0:T(8,128)} %get-tuple-element.28) | copy-start | bytes 1032196
  10.3 43.0 %copy-start.2 = (f32[672,128]{1,0:T(8,128)S(1)}, f32[672,128]{1,0:T(8,128)}, u32[]{:S(2)}) copy-start(f32[672,128]{1,0:T(8,128)} %get-tuple-element.29.refs_7_) | copy-start | bytes 1032196
  10.3 13.7 %collective-permute-start.2 = (f32[672,128]{1,0:T(8,128)}, f32[672,128]{1,0:T(8,128)S(1)}, u32[]{:S(2)}, u32[]{:S(2)}) collective-permute-start(f32[672,128]{1,0:T(8,128)} %get-tuple-element.24), channel_id=1, source_target_pairs={{0,64},{16,80},{32,96},{48,112},{64,0},{80,16},{96,32},{112,48},{1... | collective-permute-start | bytes 1032200 | tf_op jit(solution)/shard_map/ppermute | solution.py:313
  11.9 18.6 %collective-permute-start.3 = (f32[672,128]{1,0:T(8,128)}, f32[672,128]{1,0:T(8,128)S(1)}, u32[]{:S(2)}, u32[]{:S(2)}) collective-permute-start(f32[672,128]{1,0:T(8,128)} %get-tuple-element.25), channel_id=1, source_target_pairs={{0,48},{16,32},{32,80},{48,64},{64,112},{80,96},{96,16},{112,0},{1... | collective-permute-start | bytes 1032200 | tf_op jit(solution)/shard_map/ppermute | solution.py:313
  13.7 19.1 %collective-permute-start.4 = (f32[672,128]{1,0:T(8,128)}, f32[672,128]{1,0:T(8,128)S(1)}, u32[]{:S(2)}, u32[]{:S(2)}) collective-permute-start(f32[672,128]{1,0:T(8,128)} %get-tuple-element.26), channel_id=1, source_target_pairs={{0,112},{16,96},{32,16},{48,0},{64,48},{80,32},{96,80},{112,64},{1... | collective-permute-start | bytes 1032200 | tf_op jit(solution)/shard_map/ppermute | solution.py:313
  18.9 49.2 %copy-start.6 = (f32[672,128]{1,0:T(8,128)S(1)}, f32[672,128]{1,0:T(8,128)}, u32[]{:S(2)}) copy-start(f32[672,128]{1,0:T(8,128)} %get-tuple-element.37.refs_7_.refs_15_) | copy-start | bytes 1032196
  18.9 52.2 %copy-start = (f32[672,128]{1,0:T(8,128)}, f32[672,128]{1,0:T(8,128)S(1)}, u32[]{:S(2)}) copy-start(f32[672,128]{1,0:T(8,128)S(1)} %collective-permute-done.refs_0_) | copy-start | bytes 1032196
  18.9 20.8 %collective-permute-start.5 = (f32[672,128]{1,0:T(8,128)S(1)}, f32[672,128]{1,0:T(8,128)S(1)}, u32[]{:S(2)}, u32[]{:S(2)}) collective-permute-start(f32[672,128]{1,0:T(8,128)S(1)} %copy-done.19), channel_id=1, source_target_pairs={{0,80},{16,64},{32,112},{48,96},{64,16},{80,0},{96,48},{112,32},{1... | collective-permute-start | bytes 1032200 | tf_op jit(solution)/shard_map/ppermute | solution.py:313
  23.9 47.3 %copy-start.1 = (f32[672,128]{1,0:T(8,128)}, f32[672,128]{1,0:T(8,128)S(1)}, u32[]{:S(2)}) copy-start(f32[672,128]{1,0:T(8,128)S(1)} %collective-permute-done.1.refs_1_) | copy-start | bytes 1032196
  23.9 15.8 %collective-permute-start.6 = (f32[672,128]{1,0:T(8,128)S(1)}, f32[672,128]{1,0:T(8,128)S(1)}, u32[]{:S(2)}, u32[]{:S(2)}) collective-permute-start(f32[672,128]{1,0:T(8,128)S(1)} %copy-done.18), channel_id=1, source_target_pairs={{0,16},{16,0},{32,48},{48,32},{64,80},{80,64},{96,112},{112,96},{1... | collective-permute-start | bytes 1032200 | tf_op jit(solution)/shard_map/ppermute | solution.py:313
  24.0 47.2 %copy-start.3 = (f32[672,128]{1,0:T(8,128)}, f32[672,128]{1,0:T(8,128)S(1)}, u32[]{:S(2)}) copy-start(f32[672,128]{1,0:T(8,128)S(1)} %collective-permute-done.2.refs_2_) | copy-start | bytes 1032196
  24.0 22.5 %collective-permute-start.7 = (f32[672,128]{1,0:T(8,128)}, f32[672,128]{1,0:T(8,128)S(1)}, u32[]{:S(2)}, u32[]{:S(2)}) collective-permute-start(f32[672,128]{1,0:T(8,128)} %get-tuple-element.30), channel_id=1, source_target_pairs={{0,32},{16,48},{32,64},{48,80},{64,96},{80,112},{96,0},{112,16},{1... | collective-permute-start | bytes 1032200 | tf_op jit(solution)/shard_map/ppermute | solution.py:313
  30.6 40.6 %copy-start.4 = (f32[672,128]{1,0:T(8,128)}, f32[672,128]{1,0:T(8,128)S(1)}, u32[]{:S(2)}) copy-start(f32[672,128]{1,0:T(8,128)S(1)} %collective-permute-done.3.refs_3_) | copy-start | bytes 1032196
  30.6 22.7 %collective-permute-start.8 = (f32[672,128]{1,0:T(8,128)}, f32[672,128]{1,0:T(8,128)S(1)}, u32[]{:S(2)}, u32[]{:S(2)}) collective-permute-start(f32[672,128]{1,0:T(8,128)} %get-tuple-element.31), channel_id=1, source_target_pairs={{0,96},{16,112},{32,0},{48,16},{64,32},{80,48},{96,64},{112,80},{1... | collective-permute-start | bytes 1032200 | tf_op jit(solution)/shard_map/ppermute | solution.py:313
  32.9 38.3 %copy-start.5 = (f32[672,128]{1,0:T(8,128)}, f32[672,128]{1,0:T(8,128)S(1)}, u32[]{:S(2)}) copy-start(f32[672,128]{1,0:T(8,128)S(1)} %collective-permute-done.4.refs_4_) | copy-start | bytes 1032196
  32.9 23.2 %collective-permute-start.9 = (f32[672,128]{1,0:T(8,128)}, f32[672,128]{1,0:T(8,128)S(1)}, u32[]{:S(2)}, u32[]{:S(2)}) collective-permute-start(f32[672,128]{1,0:T(8,128)} %get-tuple-element.32), channel_id=1, source_target_pairs={{0,64},{16,80},{32,96},{48,112},{64,0},{80,16},{96,32},{112,48},{1... | collective-permute-start | bytes 1032200 | tf_op jit(solution)/shard_map/ppermute | solution.py:313
  39.7 31.5 %copy-start.7 = (f32[672,128]{1,0:T(8,128)}, f32[672,128]{1,0:T(8,128)S(1)}, u32[]{:S(2)}) copy-start(f32[672,128]{1,0:T(8,128)S(1)} %collective-permute-done.5.refs_5_) | copy-start | bytes 1032196
  39.7 20.3 %collective-permute-start.10 = (f32[672,128]{1,0:T(8,128)}, f32[672,128]{1,0:T(8,128)S(1)}, u32[]{:S(2)}, u32[]{:S(2)}) collective-permute-start(f32[672,128]{1,0:T(8,128)} %get-tuple-element.33), channel_id=1, source_target_pairs={{0,48},{16,32},{32,80},{48,64},{64,112},{80,96},{96,16},{112,0},{1... | collective-permute-start | bytes 1032200 | tf_op jit(solution)/shard_map/ppermute | solution.py:313
  39.7 31.5 %copy-start.8 = (f32[672,128]{1,0:T(8,128)}, f32[672,128]{1,0:T(8,128)S(1)}, u32[]{:S(2)}) copy-start(f32[672,128]{1,0:T(8,128)S(1)} %collective-permute-done.6.refs_6_) | copy-start | bytes 1032196
  39.7 21.6 %collective-permute-start.11 = (f32[672,128]{1,0:T(8,128)}, f32[672,128]{1,0:T(8,128)S(1)}, u32[]{:S(2)}, u32[]{:S(2)}) collective-permute-start(f32[672,128]{1,0:T(8,128)} %get-tuple-element.34), channel_id=1, source_target_pairs={{0,112},{16,96},{32,16},{48,0},{64,48},{80,32},{96,80},{112,64},{1... | collective-permute-start | bytes 1032200 | tf_op jit(solution)/shard_map/ppermute | solution.py:313
  46.5 24.7 %copy-start.9 = (f32[672,128]{1,0:T(8,128)}, f32[672,128]{1,0:T(8,128)S(1)}, u32[]{:S(2)}) copy-start(f32[672,128]{1,0:T(8,128)S(1)} %collective-permute-done.7.refs_0_.refs_8_) | copy-start | bytes 1032196
  46.5 21.6 %collective-permute-start.12 = (f32[672,128]{1,0:T(8,128)}, f32[672,128]{1,0:T(8,128)S(1)}, u32[]{:S(2)}, u32[]{:S(2)}) collective-permute-start(f32[672,128]{1,0:T(8,128)} %get-tuple-element.35), channel_id=1, source_target_pairs={{0,80},{16,64},{32,112},{48,96},{64,16},{80,0},{96,48},{112,32},{1... | collective-permute-start | bytes 1032200 | tf_op jit(solution)/shard_map/ppermute | solution.py:313
  53.3 17.9 %copy-start.10 = (f32[672,128]{1,0:T(8,128)}, f32[672,128]{1,0:T(8,128)S(1)}, u32[]{:S(2)}) copy-start(f32[672,128]{1,0:T(8,128)S(1)} %collective-permute-done.8.refs_1_.refs_9_) | copy-start | bytes 1032196
  53.3 14.8 %collective-permute-start.13 = (f32[672,128]{1,0:T(8,128)}, f32[672,128]{1,0:T(8,128)S(1)}, u32[]{:S(2)}, u32[]{:S(2)}) collective-permute-start(f32[672,128]{1,0:T(8,128)} %get-tuple-element.36), channel_id=1, source_target_pairs={{0,16},{16,0},{32,48},{48,32},{64,80},{80,64},{96,112},{112,96},{1... | collective-permute-start | bytes 1032200 | tf_op jit(solution)/shard_map/ppermute | solution.py:313
  56.1 17.2 %copy-start.11 = (f32[672,128]{1,0:T(8,128)}, f32[672,128]{1,0:T(8,128)S(1)}, u32[]{:S(2)}) copy-start(f32[672,128]{1,0:T(8,128)S(1)} %collective-permute-done.9.refs_2_.refs_10_) | copy-start | bytes 1032196
  60.0 13.3 %copy-start.12 = (f32[672,128]{1,0:T(8,128)}, f32[672,128]{1,0:T(8,128)S(1)}, u32[]{:S(2)}) copy-start(f32[672,128]{1,0:T(8,128)S(1)} %collective-permute-done.10.refs_3_.refs_11_) | copy-start | bytes 1032196
  61.3 12.0 %copy-start.13 = (f32[672,128]{1,0:T(8,128)}, f32[672,128]{1,0:T(8,128)S(1)}, u32[]{:S(2)}) copy-start(f32[672,128]{1,0:T(8,128)S(1)} %collective-permute-done.11.refs_4_.refs_12_) | copy-start | bytes 1032196
  71.2 2.0 %collective-permute-start.14 = (f32[1024,128]{1,0:T(8,128)S(1)}, f32[1024,128]{1,0:T(8,128)S(1)}, u32[]{:S(2)}, u32[]{:S(2)}) collective-permute-start(f32[1024,128]{1,0:T(8,128)S(1)} %get-tuple-element.39), channel_id=1, source_target_pairs={{0,16},{16,0},{32,48},{48,32},{64,80},{80,64},{96,112},{112,96},{1... | collective-permute-start | bytes 1572872 | tf_op jit(solution)/shard_map/ppermute | solution.py:57
  111.1 4.6 %collective-permute-start.15 = (f32[1024,128]{1,0:T(8,128)S(1)}, f32[1024,128]{1,0:T(8,128)S(1)}, u32[]{:S(2)}, u32[]{:S(2)}) collective-permute-start(f32[1024,128]{1,0:T(8,128)S(1)} %bitcast.6), channel_id=1, source_target_pairs={{0,16},{16,0},{32,48},{48,32},{64,80},{80,64},{96,112},{112,96},{1... | collective-permute-start | bytes 1572872 | tf_op jit(solution)/shard_map/ppermute | solution.py:64
  (4 other events, 15.8 us)
